TPU v7x, 32 devices: a whole 2x2x4 slice. The times are simulated.
32 devices in a mesh: tm: 2 (over core), space: 16 (over z, y, x).
Axes of the slice: x: 2, y: 2, z: 4, core: 2. Of those that a mesh axis runs over, the one named last changes fastest.
Arguments:
- field_a: float32 [2, 8, 96, 18432], P('tm', None, 'space'), may hold values from -6 to 6
- field_b: float32 [2, 8, 96, 18432], P('tm', None, 'space'), may hold values from -6 to 6
- pairs: int32 [4, 16, 2], replicated, may hold values from 0 to 7
- signs: int32 [4, 16], replicated, may hold values from -1 to 1, as said below
Outputs:
- correlator: float32 [2, 4, 96, 18432], P('tm', None, 'space')
- first_diff: float32 [2, 4, 96, 18432], P('tm', None, 'space')
- second_diff: float32 [2, 4, 96, 18432], P('tm', None, 'space')
Inputs may be any that keep to these rules, and one draw needn't show every extreme that they name: `signs`: each coefficient is -1 or 1.
All inputs are finite; a program needn't handle non-finite values.
Results may differ from a plain program's by a relative error of at most 0.0001.
Values sent between devices are 32-bit elements; how exact they have to be, the bound alone decides.
No kernel may reach another device: no remote copies, remote signals or barrier semaphores. Data moves between devices by JAX's collectives and lax.ppermute only.
A program may use at most 256 MiB of HBM per device.

v0:
```python
import math

import jax
import jax.numpy as jnp
from jax import lax
from jax.sharding import PartitionSpec as P

NZ = 96


highest = lax.Precision.HIGHEST


def padded_2(value, sides, width):
    for axis, dim in sides:
        devices, length = (lax.axis_size(axis), value.shape[dim])
        up = [(i, (i + 1) % devices) for i in range(devices)]
        down = [(j, i) for i, j in up]
        last = lax.slice_in_dim(value, length - width, length, axis=dim)
        leading = lax.slice_in_dim(value, 0, width, axis=dim)
        before = lax.ppermute(last, axis, up)
        after = lax.ppermute(leading, axis, down)
        value = jnp.concatenate([before, value, after], axis=dim)
    return value


def dft_tables(length):
    index = jnp.arange(length, dtype=jnp.int32)
    product = index[:, None] * index[None, :] % length
    angle = product.astype(jnp.float32) * (2.0 * math.pi / length)
    norm_scale = 1.0 / math.sqrt(length)
    return (jnp.cos(angle) * norm_scale, jnp.sin(angle) * norm_scale)


def as_five(values):
    return values.reshape(values.shape[:3] + (-1, 2 * NZ))


def as_four(values):
    return values.reshape(values.shape[:3] + (-1,))


def swap_parts(values):
    half = values.shape[-1] // 2
    return jnp.concatenate([values[..., half:], -values[..., :half]], axis=-1)


def along_depth(values, inverse):
    cosines, sines = dft_tables(values.shape[-1] // 2)
    matrix = jnp.block([[cosines, -sines], [sines, cosines]])
    if inverse:
        return jnp.einsum("tcxyr,kr->tcxyk", values, matrix, precision=highest)
    return jnp.einsum("tcxyr,rk->tcxyk", values, matrix, precision=highest)


def along_rows(values, sign):
    cosines, sines = dft_tables(values.shape[3])
    table = jnp.concatenate([cosines, sign * sines], axis=1)
    stacked = jnp.concatenate([values, swap_parts(values)], axis=3)
    return jnp.einsum("ky,tcxyr->tcxkr", table, stacked, precision=highest)


def along_columns(values, sign):
    cosines, sines = dft_tables(values.shape[2])
    table = jnp.concatenate([cosines, sign * sines], axis=1)
    stacked = jnp.concatenate([values, swap_parts(values)], axis=2)
    return jnp.einsum("kx,tcxyr->tckyr", table, stacked, precision=highest)


def contract(weights, hat_a, hat_b):
    depth = hat_a.shape[-1] // 2
    outputs = []
    for channel in range(weights.shape[0]):
        mixed_b = jnp.einsum("ij,tjxyk->tixyk", weights[channel], hat_b, precision=highest)
        direct = jnp.sum(hat_a * mixed_b, axis=1)
        crossed = jnp.sum(hat_a * swap_parts(mixed_b), axis=1)
        real_part = direct[..., :depth] + direct[..., depth:]
        imag_part = -(crossed[..., :depth] + crossed[..., depth:])
        outputs.append(jnp.concatenate([real_part, imag_part], axis=-1))
    return jnp.stack(outputs, axis=1)


def per_device(field_a, field_b, pairs, signs):
    components = field_a.shape[1]
    indices = jnp.arange(components, dtype=jnp.int32)
    first = (pairs[:, :, 0][:, :, None] == indices[None, None, :]).astype(jnp.float32)
    second = (pairs[:, :, 1][:, :, None] == indices[None, None, :]).astype(jnp.float32)
    weights = jnp.einsum(
        "cp,cpi,cpj->cij", signs.astype(jnp.float32), first, second, precision=highest
    )
    partial_a = as_four(along_rows(along_depth(as_five(field_a), False), 1.0))
    partial_b = as_four(along_rows(along_depth(as_five(field_b), False), 1.0))
    lines_a = lax.all_to_all(partial_a, "space", split_axis=3, concat_axis=2, tiled=True)
    lines_b = lax.all_to_all(partial_b, "space", split_axis=3, concat_axis=2, tiled=True)
    hat_a = along_columns(as_five(lines_a), 1.0)
    hat_b = along_columns(as_five(lines_b), 1.0)
    returned = as_four(along_columns(contract(weights, hat_a, hat_b), -1.0))
    mixed_sites = lax.all_to_all(returned, "space", split_axis=2, concat_axis=3, tiled=True)
    correlator = as_four(along_depth(along_rows(as_five(mixed_sites), -1.0), True))
    padded = padded_2(correlator, (("tm", 0),), 1)
    later = padded[2:]
    earlier = padded[:-2]
    first_diff = later - correlator
    second_diff = later - 2.0 * correlator + earlier
    return (correlator, first_diff, second_diff)


def solution(mesh):
    return jax.shard_map(
        per_device,
        mesh=mesh,
        in_specs=(P("tm", None, "space", None), P("tm", None, "space", None), P(), P()),
        out_specs=(
            P("tm", None, "space", None),
            P("tm", None, "space", None),
            P("tm", None, "space", None),
        ),
        check_vma=False,
    )
```

profile of v0, /device:TPU:9, one launch (start us, length us, event | category | flops | bytes accessed | tf_op | source)
XLA Modules:
  0.0 1538.1 jit_solution(4608059889914422060)
XLA Ops:
  7.1 7.3 fusion.53
  14.9 11.6 fusion.57
  37.0 82.8 %copy.115 = f32[1,8,6,18432]{1,0,2,3:T(1,128)} copy(f32[1,8,6,18432]{3,1,2,0:T(8,128)S(1)} %reshape.108) | data formatting | bytes 7077888 | tf_op jit(solution)/shard_map/reshape | solution.py:40
  120.3 161.7 %reduce.8 = f32[18432,6,8]{2,1,0:T(8,128)} reduce(f32[18432,6,1,8]{3,2,1,0:T(1,128)} %bitcast.237, f32[]{:T(128)} %broadcast.46), dimensions={2}, to_apply=%bitcast.221.reduce_sub_computation | reduce | bytes 7077892
  282.0 73.5 %reshape.132 = f32[16,1,55296]{2,1,0:T(1,128)} reshape(f32[18432,6,8]{2,1,0:T(8,128)} %reduce.8) | data formatting | bytes 7077888
  368.1 7.7 fusion.50
  376.7 11.6 fusion.58
  400.5 98.0 %copy.105 = f32[1,8,6,18432]{1,0,2,3:T(1,128)} copy(f32[1,8,6,18432]{3,1,2,0:T(8,128)} %reshape.103) | data formatting | bytes 7077888 | tf_op jit(solution)/shard_map/reshape | solution.py:40
  498.5 161.7 %reduce.10 = f32[18432,6,8]{2,1,0:T(8,128)} reduce(f32[18432,6,1,8]{3,2,1,0:T(1,128)} %bitcast.238, f32[]{:T(128)} %broadcast.46), dimensions={2}, to_apply=%bitcast.219.reduce_sub_computation | reduce | bytes 7077892
  660.2 81.8 %reshape.130 = f32[16,1,55296]{2,1,0:T(1,128)} reshape(f32[18432,6,8]{2,1,0:T(8,128)} %reduce.10) | data formatting | bytes 7077888
  751.1 21.8 %reduce.9 = f32[16,55296]{1,0:T(8,128)} reduce(f32[16,1,55296]{2,1,0:T(1,128)} %copy-done.3, f32[]{:T(128)} %broadcast.46), dimensions={1}, to_apply=%all_to_all.36.reduce_sub_computation | reduce | bytes 7077892 | tf_op jit(solution)/shard_map/all_to_all | solution.py:94
  772.9 148.1 %reshape.133 = f32[18432,6,1,8]{3,2,1,0:T(1,128)} reshape(f32[16,55296]{1,0:T(8,128)} %reduce.9) | data formatting | bytes 7077888
  920.9 101.5 %copy.116 = f32[1,8,6,18432]{3,1,2,0:T(8,128)} copy(f32[1,8,6,18432]{1,0,2,3:T(1,128)} %bitcast.235) | data formatting | bytes 7077888 | tf_op jit(solution)/shard_map/all_to_all | solution.py:94
  1044.9 11.8 fusion.56
  1056.7 6.9 copy.122
  1063.6 8.7 fusion.90
  1089.5 30.1 %reduce.11 = f32[16,55296]{1,0:T(8,128)} reduce(f32[16,1,55296]{2,1,0:T(1,128)S(1)} %all-to-all-done, f32[]{:T(128)} %broadcast.46), dimensions={1}, to_apply=%all_to_all.33.reduce_sub_computation | reduce | bytes 7077892 | tf_op jit(solution)/shard_map/all_to_all | solution.py:93
  1119.6 148.2 %reshape.131 = f32[18432,6,1,8]{3,2,1,0:T(1,128)} reshape(f32[16,55296]{1,0:T(8,128)} %reduce.11) | data formatting | bytes 7077888
  1267.8 98.9 %copy.106 = f32[1,8,6,18432]{3,1,2,0:T(8,128)S(1)} copy(f32[1,8,6,18432]{1,0,2,3:T(1,128)} %bitcast.236) | data formatting | bytes 7077888 | tf_op jit(solution)/shard_map/all_to_all | solution.py:93
  1384.4 6.7 copy.129
  1391.1 7.1 copy.127
  1398.1 6.7 copy.123
  1427.3 20.3 %fusion.40 = (f32[96,6,192]{0,2,1:T(8,128)}, f32[96,6,192]{0,2,1:T(8,128)}, f32[96,6,192]{0,2,1:T(8,128)}, f32[96,6,192]{0,2,1:T(8,128)}, f32[96,6,192]{0,2,1:T(...) fusion(f32[96,6,192,8]{0,2,1,3:T(8,128)} %copy.123, ...), kind=kOutput, calls=%fused_computation.54 | convolution fusion | flops 2058799104 | bytes 39002112 | tf_op jit(solution)/shard_map/kx,tcxyr->tckyr/dot_general | solution.py:67
  1462.4 46.9 %all_to_all.45 = f32[1,4,96,1152]{3,1,0,2:T(4,128)S(1)} all-to-all(f32[1,4,96,1152]{3,1,0,2:T(4,128)S(1)} %copy.131), channel_id=1, replica_groups=mesh['tm'=2,'space'=16] {'space'}, dimensions={2} | all-to-all | bytes 3538944 | tf_op jit(solution)/shard_map/all_to_all | solution.py:98
  (106 shorter events, 175.6 us)
Async XLA Ops:
  0.8 13.5 copy-start.13
  1.1 13.8 copy-start.4
  1.1 13.8 copy-start.8
  355.5 386.5 %all-to-all-start.1 = ((f32[16,1,55296]{2,1,0:T(1,128)}), f32[16,1,55296]{2,1,0:T(1,128)S(1)}, u32[]{:S(2)}, u32[]{:S(2)}) async-start(f32[16,1,55296]{2,1,0:T(1,128)} %reshape.132), calls=%async_computation.1 | async-start | bytes 7077888 | tf_op jit(solution)/shard_map/all_to_all | solution.py:94
  375.8 0.8 copy-start.5
  375.8 0.8 copy-start.9
  742.0 8.1 copy-start.17
  742.0 8.9 copy-start.16
  742.0 1.7 copy-start.3
  743.7 345.7 %all-to-all-start = ((f32[16,1,55296]{2,1,0:T(1,128)}), f32[16,1,55296]{2,1,0:T(1,128)S(1)}, u32[]{:S(2)}, u32[]{:S(2)}) async-start(f32[16,1,55296]{2,1,0:T(1,128)} %reshape.130), calls=%async_computation | async-start | bytes 7077888 | tf_op jit(solution)/shard_map/all_to_all | solution.py:93
  1041.1 3.8 copy-start.1
  1041.1 3.8 copy-start.6
  1041.1 3.8 copy-start.10
  1063.6 8.7 copy-start
  1411.6 5.1 copy-start.2
  1416.7 8.0 slice-start
  1419.6 5.1 slice-start.1
  1424.7 2.5 copy-start.7
  1424.7 2.5 copy-start.11
  1447.5 5.5 copy-start.12
  1453.4 0.8 copy-start.15
  1514.3 4.1 copy-start.14
  1525.6 5.6 collective-permute-start.1
  1527.7 6.1 collective-permute-start
where the time goes:
time: 1570 us; the launch traced here: 1540 us
  local copies, waits for them, and re-layouts  947 us (60%)
  other arithmetic  412 us (26%)
  matrix products  110 us (7%)
  blocking collectives  46.9 us (3%)
    unnamed x47, local copies, waits for them, and re-layouts  459 us
    unnamed x3, other arithmetic  323 us
    reshape x6, local copies, waits for them, and re-layouts, as_four(): return values.reshape(values.shape[:3] + (-1,))  196 us
    all_to_all x2, local copies, waits for them, and re-layouts, per_device(): lax.all_to_all(partial_b, 'space', split_axis=3, concat_axis=2, tiled=True)  104 us
    all_to_all x2, local copies, waits for them, and re-layouts, per_device(): lax.all_to_all(partial_a, 'space', split_axis=3, concat_axis=2, tiled=True)  100 us
    all_to_all x1, blocking collectives, per_device(): lax.all_to_all(returned, 'space', split_axis=2, concat_axis=3, tiled=True)  46.9 us
    dot_general x3, matrix products, along_columns(): return jnp.einsum('kx,tcxyr->tckyr', table, stacked, precision=highest)  37.4 us
  transfers between devices with their start and end apart: 4, of which 2 were waited for; matrix products, arithmetic and copies ran while one was open for 47% of the time, Pallas kernels for 0%

commit v1 on v0

v1 whole, which is shorter than its diff:
```python
import functools
import math

import jax
import jax.numpy as jnp
import ml_dtypes
import numpy as np
from jax import lax
from jax.experimental import pallas as pl
from jax.experimental.pallas import tpu as pltpu
from jax.sharding import PartitionSpec as P

highest = lax.Precision.HIGHEST
LANES = 128
SUB = 8


def unitary(length):
    index = np.arange(length)
    angle = (index[:, None] * index[None, :] % length) * (2.0 * np.pi / length)
    return np.cos(angle) / math.sqrt(length), np.sin(angle) / math.sqrt(length)


def halves(table):
    high = table.astype(np.float32).astype(ml_dtypes.bfloat16)
    low = (table - high.astype(np.float64)).astype(np.float32).astype(ml_dtypes.bfloat16)
    return np.stack([high, low])


def owned(devices, length):
    each = length // devices
    me = np.arange(devices)
    return ((me[:, None] ^ me[None, :]) * each)[:, :, None] + np.arange(each)


def rows_forward(devices, length):
    cos, sin = unitary(length)
    out = []
    for spots in owned(devices, length):
        k = spots.reshape(devices, -1, 2).transpose(2, 0, 1).reshape(-1)
        y = np.arange(length).reshape(-1, 2).T.reshape(-1)
        c, s = cos[k][:, y], sin[k][:, y]
        out.append(halves(np.block([[c, s], [-s, c]])))
    return np.stack(out)


def rows_inverse(devices, length):
    cos, sin = unitary(length)
    out = []
    for spots in owned(devices, length):
        y = np.arange(length).reshape(-1, 2).T.reshape(-1)
        blocks = []
        for e in range(2):
            k = spots.reshape(devices, -1, 2)[:, :, e].T.reshape(-1)
            c, s = cos[y][:, k], sin[y][:, k]
            blocks.append(np.block([[c, -s], [s, c]]))
        out.append(halves(np.concatenate(blocks)))
    return np.stack(out)


def columns_forward(devices, length):
    cos, sin = unitary(length)
    out = []
    for spots in owned(devices, length):
        c, s = cos[:, spots.reshape(-1)], sin[:, spots.reshape(-1)]
        out.append(halves(np.block([[c, s], [-s, c]])))
    return np.stack(out)


def columns_inverse(devices, length):
    cos, sin = unitary(length)
    out = []
    for spots in owned(devices, length):
        c, s = cos[spots.reshape(-1)], sin[spots.reshape(-1)]
        out.append(halves(np.block([[c, -s], [s, c]])))
    return np.stack(out)


def depth_forward(length, first, count):
    cos, sin = unitary(length)
    k = np.tile(np.arange(first, first + count), LANES // count)
    matrix = np.block([[cos[:, k], -sin[:, k]], [sin[:, k], cos[:, k]]])
    gap = np.zeros((2 * LANES - 2 * length, 2 * LANES))
    both = np.stack([np.concatenate([matrix, gap]), np.concatenate([gap, matrix])])
    return np.stack([halves(b) for b in both], axis=1)


def depth_inverse(length, wide):
    cos, sin = unitary(length)
    out = []
    for half in range(2):
        rows = []
        for first, count, lanes in ((0, wide, (0, 1)), (wide, length - wide, (half / 2, half / 2 + 0.5))):
            k = np.tile(np.arange(first, first + count), LANES // count)
            keep = np.zeros((LANES, 1))
            keep[int(lanes[0] * LANES) : int(lanes[1] * LANES)] = 1.0
            rows.append(np.concatenate([cos[k], sin[k]], axis=1) * keep)
            rows.append(np.concatenate([-sin[k], cos[k]], axis=1) * keep)
        matrix = np.concatenate(rows)
        gap = np.zeros((matrix.shape[0], 2 * LANES - 2 * length))
        both = (np.concatenate([matrix, gap], axis=1), np.concatenate([gap, matrix], axis=1))
        out.append(np.stack([halves(b) for b in both], axis=1))
    return np.stack(out)


def split(value):
    high = value.astype(jnp.bfloat16)
    return high, (value - high.astype(jnp.float32)).astype(jnp.bfloat16)


def dot3(left, right):
    dot = functools.partial(jnp.dot, preferred_element_type=jnp.float32)
    return dot(left[0], right[0]) + (dot(left[0], right[1]) + dot(left[1], right[0]))


def lane_index(shape):
    return lax.broadcasted_iota(jnp.int32, shape, len(shape) - 1)


def forward_kernel(narrow, sites, pairs_y, a0, a1, b0, b1, depth, table, out, staged, spectra):
    step = pl.program_id(0)
    groups = 1 if narrow else 2
    width = LANES // 4 if narrow else LANES // 2
    block = 2 * groups * sites * SUB
    rows = pairs_y * SUB
    y_table = (table[0], table[1])

    def one(field, which):
        def stage(p, carry):
            for q in range(3):
                start = pl.multiple_of((p * 3 + q) * LANES, LANES)
                staged[q, pl.ds(pl.multiple_of(p * SUB, SUB), sites), :] = field[0, 0, :, pl.ds(start, LANES)]
            return carry

        lax.fori_loop(0, pairs_y, stage, 0, unroll=4)
        for e in range(2):
            left = split(jnp.concatenate([staged[e], staged[e + 1]], axis=1))
            result = dot3(left, (depth[0, e], depth[1, e]))
            for part in range(2):
                spectra[which, part * 2 + e] = result[:, part * LANES : (part + 1) * LANES]

    def rows_of(which, x):
        return jnp.concatenate(
            [spectra[which, k, pl.ds(x, pairs_y, stride=SUB), :] for k in range(4)], axis=0
        )

    def send(load, group, slot):
        right = split(jnp.concatenate([load(x) for x in range(sites)], axis=1))
        result = dot3(y_table, right)
        half = result.shape[0] // 4
        for part in range(2):
            even = result[2 * part * half : (2 * part + 1) * half]
            odd = result[(2 * part + 1) * half : (2 * part + 2) * half]
            merged = jnp.where(lane_index(even.shape) // width % 2 == 0, even, odd)
            for x in range(sites):
                start = ((part * groups + group) * sites + x) * SUB + slot
                out[pl.ds(start, half, stride=block), :] = merged[:, x * LANES : (x + 1) * LANES]

    for group, (low, high) in enumerate(((a0, a1), (b0, b1))):
        one(low, 0)
        one(high, 1)
        if narrow:

            def load(x):
                first, second = rows_of(0, x), rows_of(1, x)
                return jnp.where(lane_index(first.shape) < LANES // 2, first, second)

            send(load, 0, group * 4 + step)
        else:
            send(functools.partial(rows_of, 0), group, step)
            send(functools.partial(rows_of, 1), group, step + 4)


def forward(field_a, field_b, depth, table, narrow):
    _, components, sites, flat = field_a.shape
    groups = 1 if narrow else 2
    size = table.shape[1] // 2
    pairs_y = size // 2
    lines = size // 2
    rows = lines * 2 * groups * sites * SUB
    spot = lambda shift: pl.BlockSpec((1, 1, sites, flat), lambda c: (0, c + shift, 0, 0))
    half = components // 2
    whole = lambda value: pl.BlockSpec(value.shape, lambda c: (0,) * value.ndim)
    return pl.pallas_call(
        functools.partial(forward_kernel, narrow, sites, pairs_y),
        grid=(half,),
        in_specs=[spot(0), spot(half), spot(0), spot(half), whole(depth), whole(table)],
        out_specs=pl.BlockSpec((rows, LANES), lambda c: (0, 0)),
        out_shape=jax.ShapeDtypeStruct((rows, LANES), jnp.float32),
        scratch_shapes=[
            pltpu.VMEM((3, pairs_y * SUB, LANES), jnp.float32),
            pltpu.VMEM((2, 4, pairs_y * SUB, LANES), jnp.float32),
        ],
        compiler_params=pltpu.CompilerParams(vmem_limit_bytes=40 << 20),
        cost_estimate=pl.CostEstimate(flops=8 * 10**9, bytes_accessed=12 * 10**6, transcendentals=0),
        name="forward_narrow" if narrow else "forward_wide",
    )(field_a, field_a, field_b, field_b, depth, table)


def middle_kernel(narrow, devices, sites, channels, count, pairs, signs, *refs):
    pieces, (table_f, table_i, out, lines, hats, mixed) = refs[:devices], refs[devices:]
    groups = 1 if narrow else 2
    size = devices * sites
    both = 2 * size
    for s, piece in enumerate(pieces):
        for part in range(2):
            for g in range(groups):
                for x in range(sites):
                    at = part * size + s * sites + x
                    lines[g, pl.ds(at, SUB, stride=both), :] = piece[0, part, g, x * SUB : (x + 1) * SUB, :]
    forward_table = (table_f[0], table_f[1])
    for g in range(groups):
        for quad in range(2):
            tiles = [lines[g, (quad * 4 + j) * both : (quad * 4 + j + 1) * both, :] for j in range(4)]
            result = dot3(forward_table, split(jnp.concatenate(tiles, axis=1)))
            for j in range(4):
                hat = result[:, j * LANES : (j + 1) * LANES]
                if narrow:
                    hats[quad, j] = hat
                    hats[quad, j + 4] = pltpu.roll(hat, LANES // 2, axis=1)
                else:
                    hats[g, quad * 4 + j] = hat

    def channel(c, carry):
        def pair(p, totals):
            i, j = pairs[c, 2 * p], pairs[c, 2 * p + 1]
            sign = signs[c, p].astype(jnp.float32)
            a_re, a_im = hats[0, i, 0:size, :], hats[0, i, size:both, :]
            b_re, b_im = hats[1, j, 0:size, :] * sign, hats[1, j, size:both, :] * sign
            return (
                totals[0] + (a_re * b_re + a_im * b_im),
                totals[1] + (a_im * b_re - a_re * b_im),
            )

        zero = jnp.zeros((size, LANES), jnp.float32)
        real, imag = lax.fori_loop(0, count, pair, (zero, zero))
        mixed[c, 0:size, :] = real
        mixed[c, size:both, :] = imag
        return carry

    lax.fori_loop(0, channels, channel, 0)
    inverse_table = (table_i[0], table_i[1])
    if narrow:
        tiles = []
        for c in range(0, channels, 2):
            other = pltpu.roll(mixed[c + 1], LANES // 2, axis=1)
            tiles.append(jnp.where(lane_index(other.shape) < LANES // 2, mixed[c], other))
    else:
        tiles = [mixed[c] for c in range(channels)]
    result = dot3(inverse_table, split(jnp.concatenate(tiles, axis=1)))
    for t in range(len(tiles)):
        for part in range(2):
            value = result[part * size : (part + 1) * size, t * LANES : (t + 1) * LANES]
            if narrow:
                out[0, pl.ds(2 * t + part, size, stride=4), :] = value
            else:
                out[0, part, pl.ds(t, size, stride=4), :] = value


def middle(pieces, pairs, signs, table_f, table_i, sites, channels, narrow):
    devices = len(pieces)
    size = devices * sites
    steps = pieces[0].shape[0]
    block = pieces[0].shape[1:]
    whole = lambda value: pl.BlockSpec(value.shape, lambda r: (0,) * value.ndim)
    smem = pl.BlockSpec(memory_space=pltpu.SMEM)
    rows = size * 4
    shape = (rows, LANES) if narrow else (2, rows, LANES)
    groups = 1 if narrow else 2
    return pl.pallas_call(
        functools.partial(middle_kernel, narrow, devices, sites, channels, signs.shape[1]),
        grid=(steps,),
        in_specs=[smem, smem]
        + [pl.BlockSpec((1,) + block, lambda r: (r,) + (0,) * len(block))] * devices
        + [whole(table_f), whole(table_i)],
        out_specs=pl.BlockSpec((1,) + shape, lambda r: (r,) + (0,) * len(shape)),
        out_shape=jax.ShapeDtypeStruct((steps,) + shape, jnp.float32),
        scratch_shapes=[
            pltpu.VMEM((groups, SUB * 2 * size, LANES), jnp.float32),
            pltpu.VMEM((2, SUB, 2 * size, LANES), jnp.float32),
            pltpu.VMEM((channels, 2 * size, LANES), jnp.float32),
        ],
        compiler_params=pltpu.CompilerParams(vmem_limit_bytes=40 << 20),
        cost_estimate=pl.CostEstimate(flops=4 * 10**9, bytes_accessed=10 * 10**6, transcendentals=0),
        name="middle_narrow" if narrow else "middle_wide",
    )(pairs, signs, *pieces, table_f, table_i)


def inverse_kernel(devices, sites, channels, pairs_y, *refs):
    wide, narrow = refs[:devices], refs[devices : 2 * devices]
    table, depth, out, lines_w, lines_n, staged = refs[2 * devices :]
    channel = pl.program_id(0)
    thirds = wide[0].shape[0]
    size = 2 * thirds * devices

    @pl.when(channel == 0)
    def _():
        for s in range(devices):
            for r in range(thirds):
                for v in range(sites * 4 // SUB):
                    tile = pl.ds(v * SUB, SUB)
                    at = r * devices + s
                    for part in range(2):
                        start = v * SUB * size + part * (size // 2) + at
                        lines_w[pl.ds(start, SUB, stride=size), :] = wide[s][r, part, tile, :]
                    start = v * SUB * (size // 2) + at
                    lines_n[pl.ds(start, SUB, stride=size // 2), :] = narrow[s][r, tile, :]

    y_table = (table[0], table[1])

    def rows_of(lines, spot, width):
        tiles = [lines[pl.ds(pl.multiple_of(spot(x) * size, SUB), size), :] for x in range(sites)]
        result = dot3(y_table, split(jnp.concatenate(tiles, axis=1)))
        half = result.shape[0] // 2
        first, second = result[:half], result[half:]
        return jnp.where(lane_index(first.shape) // width % 2 == 0, first, second)

    big = rows_of(lines_w, lambda x: x * 4 + channel, LANES // 2)
    small = rows_of(lines_n, lambda x: x * 2 + channel // 2, LANES // 4)
    products = []
    for e in range(2):
        rows = []
        for x in range(sites):
            lanes = slice(x * LANES, (x + 1) * LANES)
            rows.append(
                jnp.concatenate(
                    [
                        value[(2 * part + e) * pairs_y : (2 * part + e + 1) * pairs_y, lanes]
                        for value in (big, small)
                        for part in range(2)
                    ],
                    axis=1,
                )
            )
        left = split(jnp.concatenate(rows, axis=0))
        products.append(dot3(left, (depth[0, 0, e], depth[0, 1, e])))
    tiles = (
        products[0][:, :LANES],
        products[0][:, LANES:] + products[1][:, :LANES],
        products[1][:, LANES:],
    )
    for q in range(3):
        for x in range(sites):
            staged[q, pl.ds(x, pairs_y, stride=SUB), :] = tiles[q][x * pairs_y : (x + 1) * pairs_y]

    def store(p, carry):
        for q in range(3):
            start = pl.multiple_of((p * 3 + q) * LANES, LANES)
            out[0, 0, :, pl.ds(start, LANES)] = staged[q, pl.ds(pl.multiple_of(p * SUB, SUB), sites), :]
        return carry

    lax.fori_loop(0, pairs_y, store, 0, unroll=4)


def inverse(wide, narrow, table, depth, sites, channels, flat):
    devices = len(wide)
    size = table.shape[2]
    pairs_y = size // 2
    whole = lambda value: pl.BlockSpec(value.shape, lambda c: (0,) * value.ndim)
    return pl.pallas_call(
        functools.partial(inverse_kernel, devices, sites, channels, pairs_y),
        grid=(channels,),
        in_specs=[whole(v) for v in wide]
        + [whole(v) for v in narrow]
        + [whole(table), pl.BlockSpec((1,) + depth.shape[1:], lambda c: (c % 2, 0, 0, 0, 0))],
        out_specs=pl.BlockSpec((1, 1, sites, flat), lambda c: (0, c, 0, 0)),
        out_shape=jax.ShapeDtypeStruct((1, channels, sites, flat), jnp.float32),
        scratch_shapes=[
            pltpu.VMEM((sites * 4 * size, LANES), jnp.float32),
            pltpu.VMEM((sites * 2 * size, LANES), jnp.float32),
            pltpu.VMEM((3, pairs_y * SUB, LANES), jnp.float32),
        ],
        compiler_params=pltpu.CompilerParams(vmem_limit_bytes=40 << 20),
        cost_estimate=pl.CostEstimate(flops=8 * 10**9, bytes_accessed=6 * 10**6, transcendentals=0),
        name="inverse_rows_depth",
    )(*wide, *narrow, table, depth)


def exchange(pieces):
    devices = len(pieces)
    order = sorted(range(1, devices), key=lambda s: (s % 4, -(s // 8), s))
    got = [pieces[0]] + [None] * (devices - 1)
    for s in order:
        got[s] = lax.ppermute(pieces[s], "space", [(i, i ^ s) for i in range(devices)])
    return got


def fast_slice(field_a, field_b, pairs, signs, tables):
    _, components, sites, flat = field_a.shape
    devices = lax.axis_size("space")
    channels = pairs.shape[0]
    me = lax.axis_index("space")
    rows_f, rows_i, columns_f, columns_i = (
        lax.dynamic_index_in_dim(jnp.asarray(t), me, 0, False) for t in tables[:4]
    )
    depth_n, depth_w, depth_i = (jnp.asarray(t) for t in tables[4:])
    thirds = rows_f.shape[1] // 4 // devices
    flat_pairs = pairs.reshape(channels, -1)
    returned = []
    sent = []
    for narrow, depth in ((True, depth_n), (False, depth_w)):
        groups = 1 if narrow else 2
        packed = forward(field_a, field_b, depth, rows_f, narrow)
        packed = packed.reshape(devices, thirds, 2, groups, sites * SUB, LANES)
        sent.append(exchange([packed[s] for s in range(devices)]))
    for narrow, pieces in zip((True, False), sent):
        mixed = middle(pieces, flat_pairs, signs, columns_f, columns_i, sites, channels, narrow)
        rows = sites * 4
        if narrow:
            back = [mixed[:, s * rows : (s + 1) * rows] for s in range(devices)]
        else:
            back = [mixed[:, :, s * rows : (s + 1) * rows] for s in range(devices)]
        returned.append(exchange(back))
    return inverse(returned[1], returned[0], rows_i, depth_i, sites, channels, flat)


def neighbours(value):
    devices, length = lax.axis_size("tm"), value.shape[0]
    up = [(i, (i + 1) % devices) for i in range(devices)]
    down = [(j, i) for i, j in up]
    after = lax.ppermute(value[:1], "tm", down)
    before = after if devices == 2 and length == 1 else lax.ppermute(value[-1:], "tm", up)
    later = jnp.concatenate([value[1:], after], axis=0)
    earlier = jnp.concatenate([before, value[:-1]], axis=0)
    return later, earlier


def differences(correlator):
    later, earlier = neighbours(correlator)
    return correlator, later - correlator, later - 2.0 * correlator + earlier


def fast_device(tables, field_a, field_b, pairs, signs):
    parts = [
        fast_slice(field_a[t : t + 1], field_b[t : t + 1], pairs, signs, tables)
        for t in range(field_a.shape[0])
    ]
    return differences(jnp.concatenate(parts, axis=0))


def dft_tables(length):
    cos, sin = unitary(length)
    return jnp.asarray(cos, jnp.float32), jnp.asarray(sin, jnp.float32)


def swap_parts(values):
    half = values.shape[-1] // 2
    return jnp.concatenate([values[..., half:], -values[..., :half]], axis=-1)


def along_depth(values, inverse):
    cosines, sines = dft_tables(values.shape[-1] // 2)
    matrix = jnp.block([[cosines, -sines], [sines, cosines]])
    if inverse:
        return jnp.einsum("tcxyr,kr->tcxyk", values, matrix, precision=highest)
    return jnp.einsum("tcxyr,rk->tcxyk", values, matrix, precision=highest)


def along(values, sign, axis):
    cosines, sines = dft_tables(values.shape[axis])
    table = jnp.concatenate([cosines, sign * sines], axis=1)
    stacked = jnp.concatenate([values, swap_parts(values)], axis=axis)
    spec = "ky,tcxyr->tcxkr" if axis == 3 else "kx,tcxyr->tckyr"
    return jnp.einsum(spec, table, stacked, precision=highest)


def contract(weights, hat_a, hat_b):
    depth = hat_a.shape[-1] // 2
    outputs = []
    for channel in range(weights.shape[0]):
        mixed_b = jnp.einsum("ij,tjxyk->tixyk", weights[channel], hat_b, precision=highest)
        direct = jnp.sum(hat_a * mixed_b, axis=1)
        crossed = jnp.sum(hat_a * swap_parts(mixed_b), axis=1)
        real_part = direct[..., :depth] + direct[..., depth:]
        imag_part = -(crossed[..., :depth] + crossed[..., depth:])
        outputs.append(jnp.concatenate([real_part, imag_part], axis=-1))
    return jnp.stack(outputs, axis=1)


def any_device(depth, field_a, field_b, pairs, signs):
    as_five = lambda v: v.reshape(v.shape[:3] + (-1, 2 * depth))
    as_four = lambda v: v.reshape(v.shape[:3] + (-1,))
    indices = jnp.arange(field_a.shape[1], dtype=jnp.int32)
    first = (pairs[:, :, 0][:, :, None] == indices).astype(jnp.float32)
    second = (pairs[:, :, 1][:, :, None] == indices).astype(jnp.float32)
    weights = jnp.einsum("cp,cpi,cpj->cij", signs.astype(jnp.float32), first, second, precision=highest)
    hats = []
    for field in (field_a, field_b):
        partial = as_four(along(along_depth(as_five(field), False), 1.0, 3))
        lines = lax.all_to_all(partial, "space", split_axis=3, concat_axis=2, tiled=True)
        hats.append(along(as_five(lines), 1.0, 2))
    returned = as_four(along(contract(weights, *hats), -1.0, 2))
    sites = lax.all_to_all(returned, "space", split_axis=2, concat_axis=3, tiled=True)
    return differences(as_four(along_depth(along(as_five(sites), -1.0, 3), True)))


def solution(mesh):
    devices = mesh.shape["space"]
    times = mesh.shape["tm"]

    def program(field_a, field_b, pairs, signs):
        _, components, size, flat = field_a.shape
        depth = flat // size // 2
        wide = LANES // 2
        fits = (
            depth == size
            and 2 * depth == 3 * wide
            and components == SUB
            and pairs.shape[0] == 4
            and size % (2 * devices) == 0
            and devices & (devices - 1) == 0
            and (size // devices) * 4 % SUB == 0
            and size % (2 * SUB) == 0
        )
        if fits:
            tables = (
                rows_forward(devices, size),
                rows_inverse(devices, size),
                columns_forward(devices, size),
                columns_inverse(devices, size),
                depth_forward(depth, wide, depth - wide),
                depth_forward(depth, 0, wide),
                depth_inverse(depth, wide),
            )
            per_device = functools.partial(fast_device, tables)
        else:
            per_device = functools.partial(any_device, depth)
        spec = P("tm", None, "space", None)
        return jax.shard_map(
            per_device,
            mesh=mesh,
            in_specs=(spec, spec, P(), P()),
            out_specs=(spec, spec, spec),
            check_vma=False,
        )(field_a, field_b, pairs, signs)

    return program
```

time: 1570 us -> 326 us (0.21); the launches traced: 1540 us -> 321 us
  local copies, waits for them, and re-layouts: 947 us -> 27.2 us
  other arithmetic: 412 us -> 1.28 us
  waiting for transfers between devices: 6.06 us -> 123 us
  matrix products: 110 us -> 0 us
  starting transfers between devices: 15.1 us -> 94.3 us
  Pallas kernels: 0 us -> 74.6 us
  blocking collectives: 46.9 us -> 0 us
    unnamed x47 -> x30, local copies, waits for them, and re-layouts: 459 us -> 23.6 us
    unnamed x3 -> x1, other arithmetic: 323 us -> 0.01 us
    reshape x13 -> x1, local copies, waits for them, and re-layouts: 230 us -> 0.08 us  [fast_slice(): flat_pairs = pairs.reshape(channels, -1)]
    all_to_all x5 -> x0, local copies, waits for them, and re-layouts: 205 us -> none  [the longest x2 104 us: per_device(): lax.all_to_all(partial_b, 'space', split_axis=3, concat_axis=2, tiled=True)]
    ppermute x2 -> x61, waiting for transfers between devices: 6.06 us -> 123 us  [the longest x60 119 us: exchange(): lax.ppermute(pieces[s], 'space', [(i, i ^ s) for i in range(devices)])]
    dot_general x14 -> x0, matrix products: 110 us -> none  [the longest x3 37.4 us: along_columns(): return jnp.einsum('kx,tcxyr->tckyr', table, stacked, precision=highest)]
    ppermute x2 -> x61, starting transfers between devices: 2.08 us -> 94.3 us  [the longest x60 88.2 us: exchange(): lax.ppermute(pieces[s], 'space', [(i, i ^ s) for i in range(devices)])]
    pallas_call x0 -> x5, Pallas kernels: none -> 74.6 us  [the longest x2 38.4 us: forward(): pl.pallas_call(functools.partial(forward_kernel, narrow, sites, pairs_y),...]
  transfers between devices with their start and end apart: 4 -> 61, of which waited for: 2 -> 20; matrix products, arithmetic and copies ran while one was open for 47% -> 1% of each run, Pallas kernels for 0% -> 11%
where the time goes in v1:
time: 326 us; the launch traced here: 321 us
  waiting for transfers between devices  123 us (38%)
  starting transfers between devices  94.3 us (29%)
  Pallas kernels  74.6 us (23%)
  local copies, waits for them, and re-layouts  27.2 us (8%)
    ppermute x60, waiting for transfers between devices, exchange(): lax.ppermute(pieces[s], 'space', [(i, i ^ s) for i in range(devices)])  119 us
    ppermute x60, starting transfers between devices, exchange(): lax.ppermute(pieces[s], 'space', [(i, i ^ s) for i in range(devices)])  88.2 us
    pallas_call x2, Pallas kernels, forward(): pl.pallas_call(functools.partial(forward_kernel, narrow, sites, pairs_y),...  38.4 us
    pallas_call x2, Pallas kernels, middle(): pl.pallas_call(functools.partial(middle_kernel, narrow, devices, sites, c...  24.2 us
    unnamed x30, local copies, waits for them, and re-layouts  23.6 us
    pallas_call x1, Pallas kernels, inverse(): pl.pallas_call(functools.partial(inverse_kernel, devices, sites, channels...  11.9 us
  transfers between devices with their start and end apart: 61, of which 20 were waited for; matrix products, arithmetic and copies ran while one was open for 1% of the time, Pallas kernels for 11%

profile of v1, /device:TPU:9, one launch (start us, length us, event | category | flops | bytes accessed | tf_op | source)
XLA Modules:
  0.0 320.9 jit_solution(12508405796776604006)
XLA Ops:
  0.6 6.5 %copy.29.a0.a1 = f32[1,8,6,18432]{3,2,1,0:T(8,128)} copy(f32[1,8,6,18432]{3,1,2,0:T(8,128)} %param.11) | data formatting | bytes 7077888 | tf_op args[0]
  7.1 4.3 %copy.31.b0.b1 = f32[1,8,6,18432]{3,2,1,0:T(8,128)} copy(f32[1,8,6,18432]{3,1,2,0:T(8,128)S(1)} %copy-done.7) | data formatting | bytes 7077888 | tf_op args[1]
  17.0 17.4 %forward_narrow.1 = f32[4608,128]{1,0:T(8,128)S(1)} custom-call(f32[1,8,6,18432]{3,2,1,0:T(8,128)S(1)} %copy-done.1, f32[1,8,6,18432]{3,2,1,0:T(8,128)S(1)} %copy-done.1, f32[1,8,6,18432]{3,2,1,0:T(8,128)S(1)} %copy-done.2, f32[1,8,6,18432]{3,2,1,0:T(8,128)S(1)} %copy-done.2, bf16[2,2,256,256]{3,2,1,0:T(8,128)(2,1)S(1)} %copy-done.6, ...), custom_call_target="tpu_custom_call" | custom-call | flops 8000000000 | bytes 12000000 | tf_op jit(solution)/shard_map/forward_narrow/pallas_call | solution.py:184
  51.6 3.8 %collective-permute-done.36.refs_7_ = f32[3,2,1,48,128]{4,3,2,1,0:T(8,128)S(1)} collective-permute-done((f32[3,2,1,48,128]{4,3,2,1,0:T(8,128)S(1)}, f32[3,2,1,48,128]{4,3,2,1,0:T(8,128)S(1)}, u32[]{:S(2)}, u32[]{:S(2)}) %collective-permute-start.36) | collective-permute-done | bytes 147488 | tf_op jit(solution)/shard_map/ppermute | solution.py:384
  60.3 12.9 %collective-permute-done.39.refs_10_ = f32[3,2,1,48,128]{4,3,2,1,0:T(8,128)S(1)} collective-permute-done((f32[3,2,1,48,128]{4,3,2,1,0:T(8,128)S(1)}, f32[3,2,1,48,128]{4,3,2,1,0:T(8,128)S(1)}, u32[]{:S(2)}, u32[]{:S(2)}) %collective-permute-start.39) | collective-permute-done | bytes 147488 | tf_op jit(solution)/shard_map/ppermute | solution.py:384
  73.2 21.0 %forward_wide.1 = f32[9216,128]{1,0:T(8,128)S(1)} custom-call(f32[1,8,6,18432]{3,2,1,0:T(8,128)S(1)} %copy-done.1, f32[1,8,6,18432]{3,2,1,0:T(8,128)S(1)} %copy-done.1, f32[1,8,6,18432]{3,2,1,0:T(8,128)} %copy.31.b0.b1, f32[1,8,6,18432]{3,2,1,0:T(8,128)} %copy.31.b0.b1, bf16[2,2,256,256]{3,2,1,0:T(8,128)(2,1)S(1)} %copy-done.5, ...), custom_call_target="tpu_custom_call" | custom-call | flops 8000000000 | bytes 12000000 | tf_op jit(solution)/shard_map/forward_wide/pallas_call | solution.py:184
  97.7 11.3 %middle_narrow.1 = f32[3,384,128]{2,1,0:T(8,128)S(1)} custom-call(s32[4,32]{1,0:T(4,128)S(1)} %copy.33.pairs, s32[4,16]{1,0:T(4,128)S(1)} %copy-done.3, f32[3,2,1,48,128]{4,3,2,1,0:T(8,128)S(1)} %bitcast.44, f32[3,2,1,48,128]{4,3,2,1,0:T(8,128)S(1)} %collective-permute-done.30.refs_1_, f32[3,2,1,48,128]{4,3,2,1,0:T(8,128)S(1)} %collective-permute-done.31.refs_2_, ...), custom_call_target="tpu_custom_call" | custom-call | flops 4000000000 | bytes 10000000 | tf_op jit(solution)/shard_map/middle_narrow/pallas_call | solution.py:270
  112.3 6.3 %collective-permute-start.48 = (f32[3,24,128]{2,1,0:T(8,128)S(1)}, f32[3,24,128]{2,1,0:T(8,128)S(1)}, u32[]{:S(2)}, u32[]{:S(2)}) collective-permute-start(f32[3,24,128]{2,1,0:T(8,128)S(1)} %get-tuple-element.70), channel_id=1, source_target_pairs={{0,4},{1,5},{2,6},{3,7},{4,0},{5,1},{6,2},{7,3},{8,12},{9,13},{10,... | collective-permute-start | bytes 110600 | tf_op jit(solution)/shard_map/ppermute | solution.py:384
  126.2 3.5 %collective-permute-done.1.refs_2_ = f32[3,2,2,48,128]{4,3,2,1,0:T(8,128)S(1)} collective-permute-done((f32[3,2,2,48,128]{4,3,2,1,0:T(8,128)S(1)}, f32[3,2,2,48,128]{4,3,2,1,0:T(8,128)S(1)}, u32[]{:S(2)}, u32[]{:S(2)}) %collective-permute-start.1) | collective-permute-done | bytes 294944 | tf_op jit(solution)/shard_map/ppermute | solution.py:384
  131.8 29.0 %collective-permute-done.10.refs_11_ = f32[3,2,2,48,128]{4,3,2,1,0:T(8,128)S(1)} collective-permute-done((f32[3,2,2,48,128]{4,3,2,1,0:T(8,128)S(1)}, f32[3,2,2,48,128]{4,3,2,1,0:T(8,128)S(1)}, u32[]{:S(2)}, u32[]{:S(2)}) %collective-permute-start.10) | collective-permute-done | bytes 294944 | tf_op jit(solution)/shard_map/ppermute | solution.py:384
  160.8 7.7 %collective-permute-done.11.refs_12_ = f32[3,2,2,48,128]{4,3,2,1,0:T(8,128)S(1)} collective-permute-done((f32[3,2,2,48,128]{4,3,2,1,0:T(8,128)S(1)}, f32[3,2,2,48,128]{4,3,2,1,0:T(8,128)S(1)}, u32[]{:S(2)}, u32[]{:S(2)}) %collective-permute-start.11) | collective-permute-done | bytes 294944 | tf_op jit(solution)/shard_map/ppermute | solution.py:384
  168.5 7.3 %collective-permute-done.12.refs_13_ = f32[3,2,2,48,128]{4,3,2,1,0:T(8,128)S(1)} collective-permute-done((f32[3,2,2,48,128]{4,3,2,1,0:T(8,128)S(1)}, f32[3,2,2,48,128]{4,3,2,1,0:T(8,128)S(1)}, u32[]{:S(2)}, u32[]{:S(2)}) %collective-permute-start.12) | collective-permute-done | bytes 294944 | tf_op jit(solution)/shard_map/ppermute | solution.py:384
  175.7 5.3 %collective-permute-done.13.refs_14_ = f32[3,2,2,48,128]{4,3,2,1,0:T(8,128)S(1)} collective-permute-done((f32[3,2,2,48,128]{4,3,2,1,0:T(8,128)S(1)}, f32[3,2,2,48,128]{4,3,2,1,0:T(8,128)S(1)}, u32[]{:S(2)}, u32[]{:S(2)}) %collective-permute-start.13) | collective-permute-done | bytes 294944 | tf_op jit(solution)/shard_map/ppermute | solution.py:384
  181.0 11.9 %collective-permute-done.14.refs_15_ = f32[3,2,2,48,128]{4,3,2,1,0:T(8,128)S(1)} collective-permute-done((f32[3,2,2,48,128]{4,3,2,1,0:T(8,128)S(1)}, f32[3,2,2,48,128]{4,3,2,1,0:T(8,128)S(1)}, u32[]{:S(2)}, u32[]{:S(2)}) %collective-permute-start.14) | collective-permute-done | bytes 294944 | tf_op jit(solution)/shard_map/ppermute | solution.py:384
  201.0 4.2 %collective-permute-start.51 = (f32[3,24,128]{2,1,0:T(8,128)S(1)}, f32[3,24,128]{2,1,0:T(8,128)S(1)}, u32[]{:S(2)}, u32[]{:S(2)}) collective-permute-start(f32[3,24,128]{2,1,0:T(8,128)S(1)} %get-tuple-element.67), channel_id=1, source_target_pairs={{0,7},{1,6},{2,5},{3,4},{4,3},{5,2},{6,1},{7,0},{8,15},{9,14},{10,... | collective-permute-start | bytes 110600 | tf_op jit(solution)/shard_map/ppermute | solution.py:384
  210.7 15.4 %collective-permute-done.8.refs_9_ = f32[3,2,2,48,128]{4,3,2,1,0:T(8,128)S(1)} collective-permute-done((f32[3,2,2,48,128]{4,3,2,1,0:T(8,128)S(1)}, f32[3,2,2,48,128]{4,3,2,1,0:T(8,128)S(1)}, u32[]{:S(2)}, u32[]{:S(2)}) %collective-permute-start.8) | collective-permute-done | bytes 294944 | tf_op jit(solution)/shard_map/ppermute | solution.py:384
  226.1 4.0 %collective-permute-start.53 = (f32[3,24,128]{2,1,0:T(8,128)S(1)}, f32[3,24,128]{2,1,0:T(8,128)S(1)}, u32[]{:S(2)}, u32[]{:S(2)}) collective-permute-start(f32[3,24,128]{2,1,0:T(8,128)S(1)} %get-tuple-element.65), channel_id=1, source_target_pairs={{0,9},{1,8},{2,11},{3,10},{4,13},{5,12},{6,15},{7,14},{8,1},{9,0},... | collective-permute-start | bytes 110600 | tf_op jit(solution)/shard_map/ppermute | solution.py:384
  233.2 4.0 %collective-permute-start.54 = (f32[3,24,128]{2,1,0:T(8,128)S(1)}, f32[3,24,128]{2,1,0:T(8,128)S(1)}, u32[]{:S(2)}, u32[]{:S(2)}) collective-permute-start(f32[3,24,128]{2,1,0:T(8,128)S(1)} %get-tuple-element.64), channel_id=1, source_target_pairs={{0,10},{1,11},{2,8},{3,9},{4,14},{5,15},{6,12},{7,13},{8,2},{9,3},... | collective-permute-start | bytes 110600 | tf_op jit(solution)/shard_map/ppermute | solution.py:384
  237.2 12.9 %middle_wide.1 = f32[3,2,384,128]{3,2,1,0:T(8,128)S(1)} custom-call(s32[4,32]{1,0:T(4,128)S(1)} %copy.33.pairs, s32[4,16]{1,0:T(4,128)S(1)} %copy-done.3, f32[3,2,2,48,128]{4,3,2,1,0:T(8,128)S(1)} %bitcast.43, f32[3,2,2,48,128]{4,3,2,1,0:T(8,128)S(1)} %collective-permute-done.refs_1_, f32[3,2,2,48,128]{4,3,2,1,0:T(8,128)S(1)} %collective-permute-done.1.refs_2_, ...), custom_call_target="tpu_custom_call" | custom-call | flops 4000000000 | bytes 10000000 | tf_op jit(solution)/shard_map/middle_wide/pallas_call | solution.py:270
  258.7 5.9 %collective-permute-start.18 = (f32[3,2,24,128]{3,2,1,0:T(8,128)S(1)}, f32[3,2,24,128]{3,2,1,0:T(8,128)S(1)}, u32[]{:S(2)}, u32[]{:S(2)}) collective-permute-start(f32[3,2,24,128]{3,2,1,0:T(8,128)S(1)} %get-tuple-element.54), channel_id=1, source_target_pairs={{0,4},{1,5},{2,6},{3,7},{4,0},{5,1},{6,2},{7,3},{8,12},{9,13},{10,... | collective-permute-start | bytes 221192 | tf_op jit(solution)/shard_map/ppermute | solution.py:384
  284.8 5.8 %collective-permute-done.27.refs_13_ = f32[3,2,24,128]{3,2,1,0:T(8,128)S(1)} collective-permute-done((f32[3,2,24,128]{3,2,1,0:T(8,128)S(1)}, f32[3,2,24,128]{3,2,1,0:T(8,128)S(1)}, u32[]{:S(2)}, u32[]{:S(2)}) %collective-permute-start.27) | collective-permute-done | bytes 73760 | tf_op jit(solution)/shard_map/ppermute | solution.py:384
  292.4 11.9 %inverse_rows_depth.1 = f32[1,4,6,18432]{3,2,1,0:T(8,128)S(1)} custom-call(f32[3,2,24,128]{3,2,1,0:T(8,128)S(1)} %get-tuple-element.58.refs_0_, f32[3,2,24,128]{3,2,1,0:T(8,128)S(1)} %collective-permute-done.15.refs_1_, f32[3,2,24,128]{3,2,1,0:T(8,128)S(1)} %collective-permute-done.16.refs_2_, f32[3,2,24,128]{3,2,1,0:T(8,128)S(1)} %collective-permute-done.17.refs_3_, ...), custom_call_target="tpu_custom_call" | custom-call | flops 8000000000 | bytes 6000000 | tf_op jit(solution)/shard_map/inverse_rows_depth/pallas_call | solution.py:360
  305.5 6.1 %collective-permute-start.60 = (f32[1,4,6,18432]{3,1,2,0:T(4,128)S(1)}, f32[1,4,6,18432]{3,1,2,0:T(4,128)S(1)}, u32[]{:S(2)}, u32[]{:S(2)}) collective-permute-start(f32[1,4,6,18432]{3,1,2,0:T(4,128)S(1)} %copy.43), channel_id=1, source_target_pairs={{16,0},{0,16},{17,1},{1,17},{18,2},{2,18},{19,3},{3,19},{20,4},{4,... | collective-permute-start | bytes 5308424 | tf_op jit(solution)/shard_map/ppermute | solution.py:421
  311.6 3.3 %collective-permute-done.60 = f32[1,4,6,18432]{3,1,2,0:T(4,128)S(1)} collective-permute-done((f32[1,4,6,18432]{3,1,2,0:T(4,128)S(1)}, f32[1,4,6,18432]{3,1,2,0:T(4,128)S(1)}, u32[]{:S(2)}, u32[]{:S(2)}) %collective-permute-start.60) | collective-permute-done | bytes 1769504 | tf_op jit(solution)/shard_map/ppermute | solution.py:421
  (143 shorter events, 98.2 us)
Async XLA Ops:
  41.0 14.4 %collective-permute-start.36 = (f32[3,2,1,48,128]{4,3,2,1,0:T(8,128)S(1)}, f32[3,2,1,48,128]{4,3,2,1,0:T(8,128)S(1)}, u32[]{:S(2)}, u32[]{:S(2)}) collective-permute-start(f32[3,2,1,48,128]{4,3,2,1,0:T(8,128)S(1)} %bitcast.68), channel_id=1, source_target_pairs={{0,7},{1,6},{2,5},{3,4},{4,3},{5,2},{6,1},{7,0},{8,15},{9,14},{10,... | collective-permute-start | bytes 442376 | tf_op jit(solution)/shard_map/ppermute | solution.py:384
  48.3 24.9 %collective-permute-start.39 = (f32[3,2,1,48,128]{4,3,2,1,0:T(8,128)S(1)}, f32[3,2,1,48,128]{4,3,2,1,0:T(8,128)S(1)}, u32[]{:S(2)}, u32[]{:S(2)}) collective-permute-start(f32[3,2,1,48,128]{4,3,2,1,0:T(8,128)S(1)} %bitcast.65), channel_id=1, source_target_pairs={{0,10},{1,11},{2,8},{3,9},{4,14},{5,15},{6,12},{7,13},{8,2},{9,3},... | collective-permute-start | bytes 442376 | tf_op jit(solution)/shard_map/ppermute | solution.py:384
  50.4 47.2 %collective-permute-start.40 = (f32[3,2,1,48,128]{4,3,2,1,0:T(8,128)S(1)}, f32[3,2,1,48,128]{4,3,2,1,0:T(8,128)S(1)}, u32[]{:S(2)}, u32[]{:S(2)}) collective-permute-start(f32[3,2,1,48,128]{4,3,2,1,0:T(8,128)S(1)} %bitcast.64), channel_id=1, source_target_pairs={{0,11},{1,10},{2,9},{3,8},{4,15},{5,14},{6,13},{7,12},{8,3},{9,2},... | collective-permute-start | bytes 442376 | tf_op jit(solution)/shard_map/ppermute | solution.py:384
  55.4 42.2 %collective-permute-start.41 = (f32[3,2,1,48,128]{4,3,2,1,0:T(8,128)S(1)}, f32[3,2,1,48,128]{4,3,2,1,0:T(8,128)S(1)}, u32[]{:S(2)}, u32[]{:S(2)}) collective-permute-start(f32[3,2,1,48,128]{4,3,2,1,0:T(8,128)S(1)} %bitcast.63), channel_id=1, source_target_pairs={{0,12},{1,13},{2,14},{3,15},{4,8},{5,9},{6,10},{7,11},{8,4},{9,5},... | collective-permute-start | bytes 442376 | tf_op jit(solution)/shard_map/ppermute | solution.py:384
  56.0 41.7 %collective-permute-start.42 = (f32[3,2,1,48,128]{4,3,2,1,0:T(8,128)S(1)}, f32[3,2,1,48,128]{4,3,2,1,0:T(8,128)S(1)}, u32[]{:S(2)}, u32[]{:S(2)}) collective-permute-start(f32[3,2,1,48,128]{4,3,2,1,0:T(8,128)S(1)} %bitcast.62), channel_id=1, source_target_pairs={{0,13},{1,12},{2,15},{3,14},{4,9},{5,8},{6,11},{7,10},{8,5},{9,4},... | collective-permute-start | bytes 442376 | tf_op jit(solution)/shard_map/ppermute | solution.py:384
  58.8 38.8 %collective-permute-start.43 = (f32[3,2,1,48,128]{4,3,2,1,0:T(8,128)S(1)}, f32[3,2,1,48,128]{4,3,2,1,0:T(8,128)S(1)}, u32[]{:S(2)}, u32[]{:S(2)}) collective-permute-start(f32[3,2,1,48,128]{4,3,2,1,0:T(8,128)S(1)} %bitcast.61), channel_id=1, source_target_pairs={{0,14},{1,15},{2,12},{3,13},{4,10},{5,11},{6,8},{7,9},{8,6},{9,7},... | collective-permute-start | bytes 442376 | tf_op jit(solution)/shard_map/ppermute | solution.py:384
  73.2 24.4 %collective-permute-start.44 = (f32[3,2,1,48,128]{4,3,2,1,0:T(8,128)S(1)}, f32[3,2,1,48,128]{4,3,2,1,0:T(8,128)S(1)}, u32[]{:S(2)}, u32[]{:S(2)}) collective-permute-start(f32[3,2,1,48,128]{4,3,2,1,0:T(8,128)S(1)} %bitcast.60), channel_id=1, source_target_pairs={{0,15},{1,14},{2,13},{3,12},{4,11},{5,10},{6,9},{7,8},{8,7},{9,6},... | collective-permute-start | bytes 442376 | tf_op jit(solution)/shard_map/ppermute | solution.py:384
  120.2 40.6 %collective-permute-start.10 = (f32[3,2,2,48,128]{4,3,2,1,0:T(8,128)S(1)}, f32[3,2,2,48,128]{4,3,2,1,0:T(8,128)S(1)}, u32[]{:S(2)}, u32[]{:S(2)}) collective-permute-start(f32[3,2,2,48,128]{4,3,2,1,0:T(8,128)S(1)} %bitcast.57), channel_id=1, source_target_pairs={{0,11},{1,10},{2,9},{3,8},{4,15},{5,14},{6,13},{7,12},{8,3},{9,2},... | collective-permute-start | bytes 884744 | tf_op jit(solution)/shard_map/ppermute | solution.py:384
  122.2 46.3 %collective-permute-start.11 = (f32[3,2,2,48,128]{4,3,2,1,0:T(8,128)S(1)}, f32[3,2,2,48,128]{4,3,2,1,0:T(8,128)S(1)}, u32[]{:S(2)}, u32[]{:S(2)}) collective-permute-start(f32[3,2,2,48,128]{4,3,2,1,0:T(8,128)S(1)} %bitcast.56), channel_id=1, source_target_pairs={{0,12},{1,13},{2,14},{3,15},{4,8},{5,9},{6,10},{7,11},{8,4},{9,5},... | collective-permute-start | bytes 884744 | tf_op jit(solution)/shard_map/ppermute | solution.py:384
  123.8 51.9 %collective-permute-start.12 = (f32[3,2,2,48,128]{4,3,2,1,0:T(8,128)S(1)}, f32[3,2,2,48,128]{4,3,2,1,0:T(8,128)S(1)}, u32[]{:S(2)}, u32[]{:S(2)}) collective-permute-start(f32[3,2,2,48,128]{4,3,2,1,0:T(8,128)S(1)} %bitcast.55), channel_id=1, source_target_pairs={{0,13},{1,12},{2,15},{3,14},{4,9},{5,8},{6,11},{7,10},{8,5},{9,4},... | collective-permute-start | bytes 884744 | tf_op jit(solution)/shard_map/ppermute | solution.py:384
  125.4 55.6 %collective-permute-start.13 = (f32[3,2,2,48,128]{4,3,2,1,0:T(8,128)S(1)}, f32[3,2,2,48,128]{4,3,2,1,0:T(8,128)S(1)}, u32[]{:S(2)}, u32[]{:S(2)}) collective-permute-start(f32[3,2,2,48,128]{4,3,2,1,0:T(8,128)S(1)} %bitcast.54), channel_id=1, source_target_pairs={{0,14},{1,15},{2,12},{3,13},{4,10},{5,11},{6,8},{7,9},{8,6},{9,7},... | collective-permute-start | bytes 884744 | tf_op jit(solution)/shard_map/ppermute | solution.py:384
  129.7 63.2 %collective-permute-start.14 = (f32[3,2,2,48,128]{4,3,2,1,0:T(8,128)S(1)}, f32[3,2,2,48,128]{4,3,2,1,0:T(8,128)S(1)}, u32[]{:S(2)}, u32[]{:S(2)}) collective-permute-start(f32[3,2,2,48,128]{4,3,2,1,0:T(8,128)S(1)} %bitcast.53), channel_id=1, source_target_pairs={{0,15},{1,14},{2,13},{3,12},{4,11},{5,10},{6,9},{7,8},{8,7},{9,6},... | collective-permute-start | bytes 884744 | tf_op jit(solution)/shard_map/ppermute | solution.py:384
  160.8 32.2 %collective-permute-start.2 = (f32[3,2,2,48,128]{4,3,2,1,0:T(8,128)S(1)}, f32[3,2,2,48,128]{4,3,2,1,0:T(8,128)S(1)}, u32[]{:S(2)}, u32[]{:S(2)}) collective-permute-start(f32[3,2,2,48,128]{4,3,2,1,0:T(8,128)S(1)} %bitcast.52), channel_id=1, source_target_pairs={{0,3},{1,2},{2,1},{3,0},{4,7},{5,6},{6,5},{7,4},{8,11},{9,10},{10,... | collective-permute-start | bytes 884744 | tf_op jit(solution)/shard_map/ppermute | solution.py:384
  168.5 27.7 %collective-permute-start.3 = (f32[3,2,2,48,128]{4,3,2,1,0:T(8,128)S(1)}, f32[3,2,2,48,128]{4,3,2,1,0:T(8,128)S(1)}, u32[]{:S(2)}, u32[]{:S(2)}) collective-permute-start(f32[3,2,2,48,128]{4,3,2,1,0:T(8,128)S(1)} %bitcast.51), channel_id=1, source_target_pairs={{0,4},{1,5},{2,6},{3,7},{4,0},{5,1},{6,2},{7,3},{8,12},{9,13},{10,... | collective-permute-start | bytes 884744 | tf_op jit(solution)/shard_map/ppermute | solution.py:384
  175.7 20.5 %collective-permute-start.4 = (f32[3,2,2,48,128]{4,3,2,1,0:T(8,128)S(1)}, f32[3,2,2,48,128]{4,3,2,1,0:T(8,128)S(1)}, u32[]{:S(2)}, u32[]{:S(2)}) collective-permute-start(f32[3,2,2,48,128]{4,3,2,1,0:T(8,128)S(1)} %bitcast.50), channel_id=1, source_target_pairs={{0,5},{1,4},{2,7},{3,6},{4,1},{5,0},{6,3},{7,2},{8,13},{9,12},{10,... | collective-permute-start | bytes 884744 | tf_op jit(solution)/shard_map/ppermute | solution.py:384
  181.0 15.9 %collective-permute-start.5 = (f32[3,2,2,48,128]{4,3,2,1,0:T(8,128)S(1)}, f32[3,2,2,48,128]{4,3,2,1,0:T(8,128)S(1)}, u32[]{:S(2)}, u32[]{:S(2)}) collective-permute-start(f32[3,2,2,48,128]{4,3,2,1,0:T(8,128)S(1)} %bitcast.49), channel_id=1, source_target_pairs={{0,6},{1,7},{2,4},{3,5},{4,2},{5,3},{6,0},{7,1},{8,14},{9,15},{10,... | collective-permute-start | bytes 884744 | tf_op jit(solution)/shard_map/ppermute | solution.py:384
  196.2 29.9 %collective-permute-start.8 = (f32[3,2,2,48,128]{4,3,2,1,0:T(8,128)S(1)}, f32[3,2,2,48,128]{4,3,2,1,0:T(8,128)S(1)}, u32[]{:S(2)}, u32[]{:S(2)}) collective-permute-start(f32[3,2,2,48,128]{4,3,2,1,0:T(8,128)S(1)} %bitcast.46), channel_id=1, source_target_pairs={{0,9},{1,8},{2,11},{3,10},{4,13},{5,12},{6,15},{7,14},{8,1},{9,0},... | collective-permute-start | bytes 884744 | tf_op jit(solution)/shard_map/ppermute | solution.py:384
  196.2 37.0 %collective-permute-start.9 = (f32[3,2,2,48,128]{4,3,2,1,0:T(8,128)S(1)}, f32[3,2,2,48,128]{4,3,2,1,0:T(8,128)S(1)}, u32[]{:S(2)}, u32[]{:S(2)}) collective-permute-start(f32[3,2,2,48,128]{4,3,2,1,0:T(8,128)S(1)} %bitcast.45), channel_id=1, source_target_pairs={{0,10},{1,11},{2,8},{3,9},{4,14},{5,15},{6,12},{7,13},{8,2},{9,3},... | collective-permute-start | bytes 884744 | tf_op jit(solution)/shard_map/ppermute | solution.py:384
  196.9 53.2 %collective-permute-start.50 = (f32[3,24,128]{2,1,0:T(8,128)S(1)}, f32[3,24,128]{2,1,0:T(8,128)S(1)}, u32[]{:S(2)}, u32[]{:S(2)}) collective-permute-start(f32[3,24,128]{2,1,0:T(8,128)S(1)} %get-tuple-element.68), channel_id=1, source_target_pairs={{0,6},{1,7},{2,4},{3,5},{4,2},{5,3},{6,0},{7,1},{8,14},{9,15},{10,... | collective-permute-start | bytes 110600 | tf_op jit(solution)/shard_map/ppermute | solution.py:384
  201.0 49.2 %collective-permute-start.51 = (f32[3,24,128]{2,1,0:T(8,128)S(1)}, f32[3,24,128]{2,1,0:T(8,128)S(1)}, u32[]{:S(2)}, u32[]{:S(2)}) collective-permute-start(f32[3,24,128]{2,1,0:T(8,128)S(1)} %get-tuple-element.67), channel_id=1, source_target_pairs={{0,7},{1,6},{2,5},{3,4},{4,3},{5,2},{6,1},{7,0},{8,15},{9,14},{10,... | collective-permute-start | bytes 110600 | tf_op jit(solution)/shard_map/ppermute | solution.py:384
  207.4 45.2 %collective-permute-start.52 = (f32[3,24,128]{2,1,0:T(8,128)S(1)}, f32[3,24,128]{2,1,0:T(8,128)S(1)}, u32[]{:S(2)}, u32[]{:S(2)}) collective-permute-start(f32[3,24,128]{2,1,0:T(8,128)S(1)} %get-tuple-element.66), channel_id=1, source_target_pairs={{0,8},{1,9},{2,10},{3,11},{4,12},{5,13},{6,14},{7,15},{8,0},{9,1},... | collective-permute-start | bytes 110600 | tf_op jit(solution)/shard_map/ppermute | solution.py:384
  226.1 26.6 %collective-permute-start.53 = (f32[3,24,128]{2,1,0:T(8,128)S(1)}, f32[3,24,128]{2,1,0:T(8,128)S(1)}, u32[]{:S(2)}, u32[]{:S(2)}) collective-permute-start(f32[3,24,128]{2,1,0:T(8,128)S(1)} %get-tuple-element.65), channel_id=1, source_target_pairs={{0,9},{1,8},{2,11},{3,10},{4,13},{5,12},{6,15},{7,14},{8,1},{9,0},... | collective-permute-start | bytes 110600 | tf_op jit(solution)/shard_map/ppermute | solution.py:384
  233.2 20.4 %collective-permute-start.54 = (f32[3,24,128]{2,1,0:T(8,128)S(1)}, f32[3,24,128]{2,1,0:T(8,128)S(1)}, u32[]{:S(2)}, u32[]{:S(2)}) collective-permute-start(f32[3,24,128]{2,1,0:T(8,128)S(1)} %get-tuple-element.64), channel_id=1, source_target_pairs={{0,10},{1,11},{2,8},{3,9},{4,14},{5,15},{6,12},{7,13},{8,2},{9,3},... | collective-permute-start | bytes 110600 | tf_op jit(solution)/shard_map/ppermute | solution.py:384
  275.4 15.2 %collective-permute-start.27 = (f32[3,2,24,128]{3,2,1,0:T(8,128)S(1)}, f32[3,2,24,128]{3,2,1,0:T(8,128)S(1)}, u32[]{:S(2)}, u32[]{:S(2)}) collective-permute-start(f32[3,2,24,128]{3,2,1,0:T(8,128)S(1)} %get-tuple-element.45), channel_id=1, source_target_pairs={{0,13},{1,12},{2,15},{3,14},{4,9},{5,8},{6,11},{7,10},{8,5},{9,4},... | collective-permute-start | bytes 221192 | tf_op jit(solution)/shard_map/ppermute | solution.py:384
  (49 other events, 527.4 us)

commit v2 on v1

v2 whole, which is shorter than its diff:
```python
import functools
import math

import jax
import jax.numpy as jnp
import ml_dtypes
import numpy as np
from jax import lax
from jax.experimental import pallas as pl
from jax.experimental.pallas import tpu as pltpu
from jax.sharding import PartitionSpec as P

highest = lax.Precision.HIGHEST
LANES = 128
SUB = 8
GRANT = 56 << 20


def unitary(length):
    index = np.arange(length)
    angle = (index[:, None] * index[None, :] % length) * (2.0 * np.pi / length)
    return np.cos(angle) / math.sqrt(length), np.sin(angle) / math.sqrt(length)


def halves(table):
    high = table.astype(np.float32).astype(ml_dtypes.bfloat16)
    low = (table - high.astype(np.float64)).astype(np.float32).astype(ml_dtypes.bfloat16)
    return high, low


def left_table(table):
    high, low = halves(table)
    return np.concatenate([high, high, low], axis=1)


def right_table(table):
    high, low = halves(table)
    return np.concatenate([high, high, low], axis=0)


def owned(devices, length):
    each = length // devices
    me = np.arange(devices)
    return ((me[:, None] ^ me[None, :]) * each)[:, :, None] + np.arange(each)


def rows_forward(devices, length):
    cos, sin = unitary(length)
    out = []
    for spots in owned(devices, length):
        k = spots.reshape(devices, -1, 2).transpose(2, 0, 1).reshape(-1)
        y = np.arange(length).reshape(-1, 2).T.reshape(-1)
        c, s = cos[k][:, y], sin[k][:, y]
        out.append(left_table(np.block([[c, s], [-s, c]])))
    return np.stack(out)


def rows_inverse(devices, length):
    cos, sin = unitary(length)
    out = []
    for spots in owned(devices, length):
        y = np.arange(length).reshape(-1, 2).T.reshape(-1)
        blocks = []
        for e in range(2):
            k = spots.reshape(devices, -1, 2)[:, :, e].T.reshape(-1)
            c, s = cos[y][:, k], sin[y][:, k]
            blocks.append(np.block([[c, -s], [s, c]]))
        out.append(left_table(np.concatenate(blocks)))
    return np.stack(out)


def columns_forward(devices, length):
    cos, sin = unitary(length)
    out = []
    for spots in owned(devices, length):
        c, s = cos[:, spots.reshape(-1)], sin[:, spots.reshape(-1)]
        out.append(left_table(np.block([[c, s], [-s, c]])))
    return np.stack(out)


def columns_inverse(devices, length):
    cos, sin = unitary(length)
    out = []
    for spots in owned(devices, length):
        c, s = cos[spots.reshape(-1)], sin[spots.reshape(-1)]
        out.append(left_table(np.block([[c, -s], [s, c]])))
    return np.stack(out)


def depth_forward(length, first, count):
    cos, sin = unitary(length)
    k = np.tile(np.arange(first, first + count), LANES // count)
    matrix = np.block([[cos[:, k], -sin[:, k]], [sin[:, k], cos[:, k]]])
    gap = np.zeros((2 * LANES - 2 * length, 2 * LANES))
    both = np.stack([np.concatenate([matrix, gap]), np.concatenate([gap, matrix])])
    return np.stack([right_table(b) for b in both])


def depth_inverse(length, first, count, halves_of):
    cos, sin = unitary(length)
    k = np.tile(np.arange(first, first + count), LANES // count)
    out = []
    for half in range(halves_of):
        keep = (np.arange(LANES) * halves_of // LANES == half)[:, None] * 1.0
        matrix = np.block([[cos[k] * keep, sin[k] * keep], [-sin[k] * keep, cos[k] * keep]])
        gap = np.zeros((matrix.shape[0], 2 * LANES - 2 * length))
        both = (np.concatenate([matrix, gap], axis=1), np.concatenate([gap, matrix], axis=1))
        out.append(np.stack([right_table(b) for b in both]))
    return np.stack(out)


def split(value):
    high = value.astype(jnp.bfloat16)
    return high, (value - high.astype(jnp.float32)).astype(jnp.bfloat16)


def dot(left, right):
    return jnp.dot(left, right, preferred_element_type=jnp.float32)


def left_dot(table, value):
    high, low = split(value)
    return dot(table, jnp.concatenate([high, low, high], axis=0))


def lane_index(shape):
    return lax.broadcasted_iota(jnp.int32, shape, len(shape) - 1)


def forward_kernel(narrow, sites, pairs_y, field_a, field_b, depth, table, token, out, spectra):
    x = pl.program_id(0)
    groups = 1 if narrow else 2
    width = LANES // 4 if narrow else LANES // 2
    block = 2 * groups * sites * SUB
    slots = []
    for group, field in enumerate((field_a, field_b)):
        tiles = [
            jnp.concatenate(
                [field[0, 0, :, (3 * p + q) * LANES : (3 * p + q + 1) * LANES] for p in range(pairs_y)], axis=0
            )
            for q in range(3)
        ]
        tiles = [split(tile) for tile in tiles]
        for e in range(2):
            left = [tiles[e + k][part] for part in (0, 1, 0) for k in range(2)]
            result = dot(jnp.concatenate(left, axis=1), depth[e])
            for part in range(2):
                spectra[group, part * 2 + e] = result[:, part * LANES : (part + 1) * LANES]

        def rows_of(c, group=group):
            return jnp.concatenate(
                [spectra[group, k, pl.ds(c, pairs_y, stride=SUB), :] for k in range(4)], axis=0
            )

        if narrow:
            for c in range(SUB // 2):
                first, second = rows_of(c), rows_of(c + SUB // 2)
                pick = lane_index(first.shape) < LANES // 2
                slots.append((0, group * 4 + c, jnp.where(pick, first, second)))
        else:
            slots += [(group, c, rows_of(c)) for c in range(SUB)]

    for first in range(0, len(slots), SUB):
        batch = slots[first : first + SUB]
        result = left_dot(table[...], jnp.concatenate([value for _, _, value in batch], axis=1))
        half = result.shape[0] // 4
        for part in range(2):
            even = result[2 * part * half : (2 * part + 1) * half]
            odd = result[(2 * part + 1) * half : (2 * part + 2) * half]
            merged = jnp.where(lane_index(even.shape) // width % 2 == 0, even, odd)
            for i, (group, slot, _) in enumerate(batch):
                start = ((part * groups + group) * sites + x) * SUB + slot
                out[pl.ds(start, half, stride=block), :] = merged[:, i * LANES : (i + 1) * LANES]


def forward(field_a, field_b, depth, table, narrow, token):
    _, sites, components, flat = field_a.shape
    groups = 1 if narrow else 2
    size = table.shape[0] // 2
    pairs_y = size // 2
    lines = size // 2
    rows = lines * 2 * groups * sites * SUB
    spot = pl.BlockSpec((1, 1, components, flat), lambda x: (0, x, 0, 0))
    whole = lambda value: pl.BlockSpec(value.shape, lambda x: (0,) * value.ndim)
    return pl.pallas_call(
        functools.partial(forward_kernel, narrow, sites, pairs_y),
        grid=(sites,),
        in_specs=[spot, spot, whole(depth), whole(table), pl.BlockSpec(memory_space=pl.ANY)],
        out_specs=pl.BlockSpec((rows, LANES), lambda x: (0, 0)),
        out_shape=jax.ShapeDtypeStruct((rows, LANES), jnp.float32),
        scratch_shapes=[pltpu.VMEM((2, 4, pairs_y * SUB, LANES), jnp.float32)],
        compiler_params=pltpu.CompilerParams(vmem_limit_bytes=GRANT),
        cost_estimate=pl.CostEstimate(flops=8 * 10**9, bytes_accessed=12 * 10**6, transcendentals=0),
        name="forward_narrow" if narrow else "forward_wide",
    )(field_a, field_b, depth, table, token)


def each(refs):
    return [ref.at[i] for ref in refs for i in range(ref.shape[0])]


def middle_kernel(narrow, arrays, devices, sites, channels, count, pairs, signs, *refs):
    pieces, refs = each(refs[:arrays]), refs[arrays:]
    table_f, table_i, out, lines, hats, mixed, rows = refs
    groups = 1 if narrow else 2
    size = devices * sites
    both = 2 * size
    for s, piece in enumerate(pieces):
        for part in range(2):
            for g in range(groups):
                for x in range(sites):
                    at = part * size + s * sites + x
                    lines[g, pl.ds(at, SUB, stride=both), :] = piece[0, part, g, x * SUB : (x + 1) * SUB, :]
    for g in range(groups):
        for quad in range(2):
            tiles = [lines[g, (quad * 4 + j) * both : (quad * 4 + j + 1) * both, :] for j in range(4)]
            result = left_dot(table_f[...], jnp.concatenate(tiles, axis=1))
            for j in range(4):
                hat = result[:, j * LANES : (j + 1) * LANES]
                if narrow:
                    turned = pltpu.roll(hat, LANES // 2, axis=1)
                    places = ((quad, j, hat), (quad, j + SUB // 2, turned))
                else:
                    places = ((g, quad * 4 + j, hat),)
                for field, c, value in places:
                    hats[field * SUB + c] = value
                    if field:
                        hats[2 * SUB + c] = -value

    def channel(c, carry):
        def pair(p, totals):
            i = pairs[c, 2 * p]
            j = pairs[c, 2 * p + 1] + jnp.where(signs[c, p] < 0, 2 * SUB, SUB)
            a_re, a_im = hats[i, 0:size, :], hats[i, size:both, :]
            b_re, b_im = hats[j, 0:size, :], hats[j, size:both, :]
            return (
                totals[0] + (a_re * b_re + a_im * b_im),
                totals[1] + (a_im * b_re - a_re * b_im),
            )

        zero = jnp.zeros((size, LANES), jnp.float32)
        real, imag = lax.fori_loop(0, count, pair, (zero, zero), unroll=2)
        mixed[c, 0:size, :] = real
        mixed[c, size:both, :] = imag
        return carry

    lax.fori_loop(0, channels, channel, 0)
    if narrow:
        tiles = []
        for c in range(0, channels, 2):
            other = pltpu.roll(mixed[c + 1], LANES // 2, axis=1)
            tiles.append(jnp.where(lane_index(other.shape) < LANES // 2, mixed[c], other))
    else:
        tiles = [mixed[c] for c in range(channels)]
    result = left_dot(table_i[...], jnp.concatenate(tiles, axis=1))
    each_site = 2 * len(tiles)
    for t in range(len(tiles)):
        for part in range(2):
            value = result[part * size : (part + 1) * size, t * LANES : (t + 1) * LANES]
            first = 2 * t + part if narrow else part * channels + t
            rows[pl.ds(first, size, stride=each_site), :] = value
    for s in range(devices):
        out[s, 0] = rows[s * sites * each_site : (s + 1) * sites * each_site, :]


def middle(pieces, pairs, signs, table_f, table_i, sites, channels, narrow):
    size = table_f.shape[0] // 2
    devices = size // sites
    steps = pieces[0].shape[1]
    smem = pl.BlockSpec(memory_space=pltpu.SMEM)
    whole = lambda value: pl.BlockSpec(value.shape, lambda r: (0,) * value.ndim)
    third = lambda value: pl.BlockSpec(
        value.shape[:1] + (1,) + value.shape[2:], lambda r: (0, r) + (0,) * (value.ndim - 2)
    )
    rows = sites * (channels if narrow else 2 * channels)
    groups = 1 if narrow else 2
    return pl.pallas_call(
        functools.partial(middle_kernel, narrow, len(pieces), devices, sites, channels, signs.shape[1]),
        grid=(steps,),
        in_specs=[smem, smem] + [third(v) for v in pieces] + [whole(table_f), whole(table_i)],
        out_specs=pl.BlockSpec((devices, 1, rows, LANES), lambda r: (0, r, 0, 0)),
        out_shape=jax.ShapeDtypeStruct((devices, steps, rows, LANES), jnp.float32),
        scratch_shapes=[
            pltpu.VMEM((groups, SUB * 2 * size, LANES), jnp.float32),
            pltpu.VMEM((3 * SUB, 2 * size, LANES), jnp.float32),
            pltpu.VMEM((channels, 2 * size, LANES), jnp.float32),
            pltpu.VMEM((devices * rows, LANES), jnp.float32),
        ],
        compiler_params=pltpu.CompilerParams(vmem_limit_bytes=GRANT),
        cost_estimate=pl.CostEstimate(flops=4 * 10**9, bytes_accessed=10 * 10**6, transcendentals=0),
        name="middle_narrow" if narrow else "middle_wide",
    )(pairs, signs, *pieces, table_f, table_i)


def inverse_kernel(narrow, arrays, devices, channels, pairs_y, *refs):
    pieces, refs = each(refs[:arrays]), refs[arrays:]
    if narrow:
        table, depth, out, lines = refs
        staged = out.at[0]
    else:
        partial, table, depth, out, lines, staged = refs
    x = pl.program_id(0)
    thirds = pieces[0].shape[0]
    size = thirds * devices

    @pl.when(x == 0)
    def _():
        for s in range(devices):
            for r in range(thirds):
                for v in range(pieces[s].shape[1] // SUB):
                    start = v * SUB * size + r * devices + s
                    lines[pl.ds(start, SUB, stride=size), :] = pieces[s][r, v * SUB : (v + 1) * SUB, :]

    def tile(*spots):
        return jnp.concatenate([lines[pl.ds(pl.multiple_of(k * size, SUB), size), :] for k in spots], axis=0)

    if narrow:
        tiles = [tile(x * channels + 2 * c, x * channels + 2 * c + 1) for c in range(channels // 2)]
        width, sets = LANES // 4, [range(parity, channels, 2) for parity in range(2)]
    else:
        big = 2 * x * channels
        tiles = [tile(big + c, big + channels + c) for c in range(channels)]
        width, sets = LANES // 2, [range(channels)]
    result = left_dot(table[...], jnp.concatenate(tiles, axis=1))
    half = result.shape[0] // 2
    first, second = result[:half], result[half:]
    high, low = split(jnp.where(lane_index(first.shape) & width == 0, first, second))

    def rows_of(value, e, c):
        spot = c // 2 if narrow else c
        return jnp.concatenate(
            [
                value[(2 * part + e) * pairs_y : (2 * part + e + 1) * pairs_y, spot * LANES : (spot + 1) * LANES]
                for part in range(2)
            ],
            axis=1,
        )

    for k, members in enumerate(sets):
        products = []
        for e in range(2):
            left = [jnp.concatenate([rows_of(value, e, c) for c in members], axis=0) for value in (high, low)]
            products.append(dot(jnp.concatenate([left[0], left[1], left[0]], axis=1), depth[k, e]))
        for i, c in enumerate(members):
            rows = slice(i * pairs_y, (i + 1) * pairs_y)
            zero, one = products[0][rows], products[1][rows]
            for q, value in enumerate((zero[:, :LANES], zero[:, LANES:] + one[:, :LANES], one[:, LANES:])):
                staged[q, pl.ds(c, pairs_y, stride=channels), :] = value
    if not narrow:
        for p in range(pairs_y):
            rows = slice(p * channels, (p + 1) * channels)
            for q in range(3):
                lanes = slice((3 * p + q) * LANES, (3 * p + q + 1) * LANES)
                out[0, 0, :, lanes] = staged[q, rows, :] + partial[0, q, rows, :]


def inverse(pieces, partial, table, depth, sites, channels, flat):
    narrow = partial is None
    size = table.shape[1] // 6
    devices = size // pieces[0].shape[1]
    whole = lambda value: pl.BlockSpec(value.shape, lambda x: (0,) * value.ndim)
    tiles = (3, size * channels, LANES)
    lines = pltpu.VMEM((sites * pieces[0].shape[2] // sites * size, LANES), jnp.float32)
    kept = pl.BlockSpec((1,) + tiles, lambda x: (x, 0, 0, 0))
    return pl.pallas_call(
        functools.partial(inverse_kernel, narrow, len(pieces), devices, channels, size),
        grid=(sites,),
        in_specs=[whole(v) for v in pieces] + ([] if narrow else [kept]) + [whole(table), whole(depth)],
        out_specs=kept if narrow else pl.BlockSpec((1, 1, channels, flat), lambda x: (0, x, 0, 0)),
        out_shape=jax.ShapeDtypeStruct((sites,) + tiles if narrow else (1, sites, channels, flat), jnp.float32),
        scratch_shapes=[lines] if narrow else [lines, pltpu.VMEM(tiles, jnp.float32)],
        compiler_params=pltpu.CompilerParams(vmem_limit_bytes=GRANT),
        cost_estimate=pl.CostEstimate(flops=4 * 10**9, bytes_accessed=6 * 10**6, transcendentals=0),
        name="inverse_narrow" if narrow else "inverse_wide",
    )(*pieces, *([] if narrow else [partial]), table, depth)


AT_ONCE = dict(sent_narrow=True, sent_wide=True, back_narrow=True, back_wide=True)


def exchange(packed, at_once):
    if at_once:
        return [lax.all_to_all(packed, "space", 0, 0, tiled=True)]
    devices = packed.shape[0]
    order = sorted(range(1, devices), key=lambda s: (s % 4, -(s // 8), s))
    got = [packed[:1]] + [None] * (devices - 1)
    for s in order:
        got[s] = lax.ppermute(packed[s : s + 1], "space", [(i, i ^ s) for i in range(devices)])
    return got


def fast_slice(field_a, field_b, pairs, signs, tables):
    _, sites, components, flat = field_a.shape
    devices = lax.axis_size("space")
    channels = pairs.shape[0]
    me = lax.axis_index("space")
    mine = [lax.dynamic_index_in_dim(jnp.asarray(t), me, 0, False) for t in tables[:4]]
    fixed = [jnp.asarray(t[0]) for t in tables[:4]]

    def table(which, name):
        return (fixed if AT_ONCE[name] else mine)[which]

    depth_n, depth_w, depth_in, depth_iw = (jnp.asarray(t) for t in tables[4:])
    thirds = tables[0].shape[1] // 4 // devices
    flat_pairs = pairs.reshape(channels, -1)
    sent = {}
    token = signs
    for narrow, depth in ((True, depth_n), (False, depth_w)):
        name = "sent_narrow" if narrow else "sent_wide"
        groups = 1 if narrow else 2
        packed = forward(field_a, field_b, depth, table(0, name), narrow, token)
        token = packed[:SUB]
        packed = packed.reshape(devices, thirds, 2, groups, sites * SUB, LANES)
        sent[narrow] = exchange(packed, AT_ONCE[name])
    result = None
    for narrow, depth in ((True, depth_in), (False, depth_iw)):
        come, go = ("sent_narrow", "back_narrow") if narrow else ("sent_wide", "back_wide")
        mixed = middle(sent[narrow], flat_pairs, signs, table(2, come), table(3, go), sites, channels, narrow)
        back = exchange(mixed, AT_ONCE[go])
        result = inverse(back, result, table(1, go), depth, sites, channels, flat)
    return result


def neighbours(value):
    devices, length = lax.axis_size("tm"), value.shape[0]
    up = [(i, (i + 1) % devices) for i in range(devices)]
    down = [(j, i) for i, j in up]
    after = lax.ppermute(value[:1], "tm", down)
    before = after if devices == 2 and length == 1 else lax.ppermute(value[-1:], "tm", up)
    later = jnp.concatenate([value[1:], after], axis=0)
    earlier = jnp.concatenate([before, value[:-1]], axis=0)
    return later, earlier


def differences(correlator):
    later, earlier = neighbours(correlator)
    return correlator, later - correlator, later - 2.0 * correlator + earlier


def fast_device(tables, field_a, field_b, pairs, signs):
    field_a, field_b = field_a.swapaxes(1, 2), field_b.swapaxes(1, 2)
    parts = [
        fast_slice(field_a[t : t + 1], field_b[t : t + 1], pairs, signs, tables)
        for t in range(field_a.shape[0])
    ]
    return tuple(out.swapaxes(1, 2) for out in differences(jnp.concatenate(parts, axis=0)))


def dft_tables(length):
    cos, sin = unitary(length)
    return jnp.asarray(cos, jnp.float32), jnp.asarray(sin, jnp.float32)


def swap_parts(values):
    half = values.shape[-1] // 2
    return jnp.concatenate([values[..., half:], -values[..., :half]], axis=-1)


def along_depth(values, inverse):
    cosines, sines = dft_tables(values.shape[-1] // 2)
    matrix = jnp.block([[cosines, -sines], [sines, cosines]])
    if inverse:
        return jnp.einsum("tcxyr,kr->tcxyk", values, matrix, precision=highest)
    return jnp.einsum("tcxyr,rk->tcxyk", values, matrix, precision=highest)


def along(values, sign, axis):
    cosines, sines = dft_tables(values.shape[axis])
    table = jnp.concatenate([cosines, sign * sines], axis=1)
    stacked = jnp.concatenate([values, swap_parts(values)], axis=axis)
    spec = "ky,tcxyr->tcxkr" if axis == 3 else "kx,tcxyr->tckyr"
    return jnp.einsum(spec, table, stacked, precision=highest)


def contract(weights, hat_a, hat_b):
    depth = hat_a.shape[-1] // 2
    outputs = []
    for channel in range(weights.shape[0]):
        mixed_b = jnp.einsum("ij,tjxyk->tixyk", weights[channel], hat_b, precision=highest)
        direct = jnp.sum(hat_a * mixed_b, axis=1)
        crossed = jnp.sum(hat_a * swap_parts(mixed_b), axis=1)
        real_part = direct[..., :depth] + direct[..., depth:]
        imag_part = -(crossed[..., :depth] + crossed[..., depth:])
        outputs.append(jnp.concatenate([real_part, imag_part], axis=-1))
    return jnp.stack(outputs, axis=1)


def any_device(depth, field_a, field_b, pairs, signs):
    as_five = lambda v: v.reshape(v.shape[:3] + (-1, 2 * depth))
    as_four = lambda v: v.reshape(v.shape[:3] + (-1,))
    indices = jnp.arange(field_a.shape[1], dtype=jnp.int32)
    first = (pairs[:, :, 0][:, :, None] == indices).astype(jnp.float32)
    second = (pairs[:, :, 1][:, :, None] == indices).astype(jnp.float32)
    weights = jnp.einsum("cp,cpi,cpj->cij", signs.astype(jnp.float32), first, second, precision=highest)
    hats = []
    for field in (field_a, field_b):
        partial = as_four(along(along_depth(as_five(field), False), 1.0, 3))
        lines = lax.all_to_all(partial, "space", split_axis=3, concat_axis=2, tiled=True)
        hats.append(along(as_five(lines), 1.0, 2))
    returned = as_four(along(contract(weights, *hats), -1.0, 2))
    sites = lax.all_to_all(returned, "space", split_axis=2, concat_axis=3, tiled=True)
    return differences(as_four(along_depth(along(as_five(sites), -1.0, 3), True)))


def solution(mesh):
    devices = mesh.shape["space"]
    times = mesh.shape["tm"]

    def program(field_a, field_b, pairs, signs):
        _, components, size, flat = field_a.shape
        depth = flat // size // 2
        wide = LANES // 2
        fits = (
            depth == size
            and 2 * depth == 3 * wide
            and components == SUB
            and pairs.shape[0] == 4
            and size % (2 * devices) == 0
            and devices & (devices - 1) == 0
            and (size // devices) * 4 % SUB == 0
            and size % (2 * SUB) == 0
        )
        if fits:
            tables = (
                rows_forward(devices, size),
                rows_inverse(devices, size),
                columns_forward(devices, size),
                columns_inverse(devices, size),
                depth_forward(depth, wide, depth - wide),
                depth_forward(depth, 0, wide),
                depth_inverse(depth, wide, depth - wide, 2),
                depth_inverse(depth, 0, wide, 1),
            )
            per_device = functools.partial(fast_device, tables)
        else:
            per_device = functools.partial(any_device, depth)
        spec = P("tm", None, "space", None)
        return jax.shard_map(
            per_device,
            mesh=mesh,
            in_specs=(spec, spec, P(), P()),
            out_specs=(spec, spec, spec),
            check_vma=False,
        )(field_a, field_b, pairs, signs)

    return program
```

time: 326 us -> 254 us (0.78); the launches traced: 321 us -> 254 us
  starting transfers between devices: 94.3 us -> 29.3 us
  waiting for transfers between devices: 123 us -> 149 us
  local copies, waits for them, and re-layouts: 27.2 us -> 4.44 us
  Pallas kernels: 74.6 us -> 66.5 us
    all_to_all x0 -> x4, waiting for transfers between devices: none -> 145 us  [exchange(): return [lax.all_to_all(packed, 'space', 0, 0, tiled=True)]]
    ppermute x60 -> x0, waiting for transfers between devices: 119 us -> none  [exchange(): lax.ppermute(pieces[s], 'space', [(i, i ^ s) for i in range(devices)])]
    ppermute x60 -> x0, starting transfers between devices: 88.2 us -> none  [exchange(): lax.ppermute(pieces[s], 'space', [(i, i ^ s) for i in range(devices)])]
    all_to_all x0 -> x4, starting transfers between devices: none -> 26.7 us  [exchange(): return [lax.all_to_all(packed, 'space', 0, 0, tiled=True)]]
    unnamed x30 -> x9, local copies, waits for them, and re-layouts: 23.6 us -> 2.5 us
    pallas_call x2, Pallas kernels: 38.4 us -> 26.7 us  [forward(): pl.pallas_call(functools.partial(forward_kernel, narrow, sites, pairs_y),...]
    transpose x0 -> x1, other arithmetic: none -> 4.02 us  [fast_device(): out.swapaxes(1, 2)]
    pallas_call x3 -> x4, Pallas kernels: 36.2 us -> 39.8 us  [the longest x2 24.3 us: middle(): pl.pallas_call(functools.partial(middle_kernel, narrow, len(pieces), devi...]
  transfers between devices with their start and end apart: 61 -> 5, of which waited for: 20 -> 5; matrix products, arithmetic and copies ran while one was open for 1% -> 1% of each run, Pallas kernels for 11% -> 18%
where the time goes in v2:
time: 254 us
  waiting for transfers between devices  149 us (59%)
  Pallas kernels  66.5 us (26%)
  starting transfers between devices  29.3 us (12%)
  local copies, waits for them, and re-layouts  4.44 us (2%)
  other arithmetic  4.02 us (2%)
    all_to_all x4, waiting for transfers between devices, exchange(): return [lax.all_to_all(packed, 'space', 0, 0, tiled=True)]  145 us
    all_to_all x4, starting transfers between devices, exchange(): return [lax.all_to_all(packed, 'space', 0, 0, tiled=True)]  26.7 us
    pallas_call x2, Pallas kernels, forward(): pl.pallas_call(functools.partial(forward_kernel, narrow, sites, pairs_y),...  26.7 us
    pallas_call x2, Pallas kernels, middle(): pl.pallas_call(functools.partial(middle_kernel, narrow, len(pieces), devi...  24.3 us
    pallas_call x2, Pallas kernels, inverse(): pl.pallas_call(functools.partial(inverse_kernel, narrow, len(pieces), dev...  15.5 us
  transfers between devices with their start and end apart: 5, of which 5 were waited for; matrix products, arithmetic and copies ran while one was open for 1% of the time, Pallas kernels for 18%

profile of v2, /device:TPU:9, one launch (start us, length us, event | category | flops | bytes accessed | tf_op | source)
XLA Modules:
  0.0 253.7 jit_solution(1779698610372314309)
XLA Ops:
  0.6 11.7 %forward_narrow.1 = f32[4608,128]{1,0:T(8,128)} custom-call(f32[1,6,8,18432]{3,2,1,0:T(8,128)} %bitcast.14, f32[1,6,8,18432]{3,2,1,0:T(8,128)} %bitcast.16, bf16[2,768,256]{2,1,0:T(8,128)(2,1)} %constant.22.clone.depth, bf16[192,576]{1,0:T(8,128)(2,1)} %constant.18.clone.table, s32[4,16]{1,0:T(4,128)} %signs.3), custom_call_target="tpu_custom_call" | custom-call | flops 8000000000 | bytes 12000000 | tf_op jit(solution)/shard_map/forward_narrow/pallas_call | solution.py:185
  12.3 6.7 %all-to-all-start.2 = ((f32[16,3,2,1,48,128]{5,4,3,2,1,0:T(8,128)}), f32[16,3,2,1,48,128]{5,4,3,2,1,0:T(8,128)S(1)}, u32[]{:S(2)}, u32[]{:S(2)}) async-start(f32[16,3,2,1,48,128]{5,4,3,2,1,0:T(8,128)} %bitcast.11), calls=%async_computation.2 | async-start | bytes 4718592 | tf_op jit(solution)/shard_map/all_to_all | solution.py:383
  19.0 1.3 slice.4.token
  20.2 15.0 %forward_wide.1 = f32[9216,128]{1,0:T(8,128)} custom-call(f32[1,6,8,18432]{3,2,1,0:T(8,128)} %bitcast.15, f32[1,6,8,18432]{3,2,1,0:T(8,128)} %bitcast.17, bf16[2,768,256]{2,1,0:T(8,128)(2,1)} %constant.23.clone.depth, bf16[192,576]{1,0:T(8,128)(2,1)} %constant.18.clone.table, f32[8,128]{1,0:T(8,128)} %slice.4.token), custom_call_target="tpu_custom_call" | custom-call | flops 8000000000 | bytes 12000000 | tf_op jit(solution)/shard_map/forward_wide/pallas_call | solution.py:185
  35.2 35.0 %all-to-all-done.2.refs_0_ = f32[16,3,2,1,48,128]{5,4,3,2,1,0:T(8,128)S(1)} async-done(((f32[16,3,2,1,48,128]{5,4,3,2,1,0:T(8,128)}), f32[16,3,2,1,48,128]{5,4,3,2,1,0:T(8,128)S(1)}, u32[]{:S(2)}, u32[]{:S(2)}) %all-to-all-start.2) | async-done | bytes 2359328 | tf_op jit(solution)/shard_map/all_to_all | solution.py:383
  70.2 1.4 copy-done
  71.6 6.6 %all-to-all-start = ((f32[16,3,2,2,48,128]{5,4,3,2,1,0:T(8,128)}), f32[16,3,2,2,48,128]{5,4,3,2,1,0:T(8,128)}, u32[]{:S(2)}, u32[]{:S(2)}) async-start(f32[16,3,2,2,48,128]{5,4,3,2,1,0:T(8,128)} %bitcast.10), calls=%async_computation | async-start | bytes 9437184 | tf_op jit(solution)/shard_map/all_to_all | solution.py:383
  78.2 0.0 copy-done.3
  78.2 0.1 copy.15
  78.3 0.7 copy.16.pairs
  79.0 11.0 %middle_narrow.1 = f32[16,3,24,128]{3,2,1,0:T(8,128)} custom-call(s32[4,32]{1,0:T(4,128)} %copy.16.pairs, s32[4,16]{1,0:T(4,128)} %signs.3, f32[16,3,2,1,48,128]{5,4,3,2,1,0:T(8,128)} %copy-done, bf16[192,576]{1,0:T(8,128)(2,1)} %constant.20.clone.refs_1_, bf16[192,576]{1,0:T(8,128)(2,1)} %constant.21.clone.refs_2_), custom_call_target="tpu_custom_call" | custom-call | flops 4000000000 | bytes 10000000 | tf_op jit(solution)/shard_map/middle_narrow/pallas_call | solution.py:277
  90.0 88.9 %all-to-all-done.refs_0_ = f32[16,3,2,2,48,128]{5,4,3,2,1,0:T(8,128)} async-done(((f32[16,3,2,2,48,128]{5,4,3,2,1,0:T(8,128)}), f32[16,3,2,2,48,128]{5,4,3,2,1,0:T(8,128)}, u32[]{:S(2)}, u32[]{:S(2)}) %all-to-all-start) | async-done | bytes 4718624 | tf_op jit(solution)/shard_map/all_to_all | solution.py:383
  178.9 8.7 %all-to-all-start.3 = ((f32[16,3,24,128]{3,2,1,0:T(8,128)}), f32[16,3,24,128]{3,2,1,0:T(8,128)S(1)}, u32[]{:S(2)}, u32[]{:S(2)}) async-start(f32[16,3,24,128]{3,2,1,0:T(8,128)} %middle_narrow.1), calls=%async_computation.3 | async-start | bytes 1179648 | tf_op jit(solution)/shard_map/all_to_all | solution.py:383
  187.6 13.3 %middle_wide.1 = f32[16,3,48,128]{3,2,1,0:T(8,128)} custom-call(s32[4,32]{1,0:T(4,128)} %copy.16.pairs, s32[4,16]{1,0:T(4,128)} %signs.3, f32[16,3,2,2,48,128]{5,4,3,2,1,0:T(8,128)} %all-to-all-done.refs_0_, bf16[192,576]{1,0:T(8,128)(2,1)} %constant.20.clone.refs_1_, bf16[192,576]{1,0:T(8,128)(2,1)} %constant.21.clone.refs_2_), custom_call_target="tpu_custom_call" | custom-call | flops 4000000000 | bytes 10000000 | tf_op jit(solution)/shard_map/middle_wide/pallas_call | solution.py:277
  200.9 1.6 all-to-all-done.3.refs_0_
  202.5 4.8 %all-to-all-start.1 = ((f32[16,3,48,128]{3,2,1,0:T(8,128)}), f32[16,3,48,128]{3,2,1,0:T(8,128)S(1)}, u32[]{:S(2)}, u32[]{:S(2)}) async-start(f32[16,3,48,128]{3,2,1,0:T(8,128)} %middle_wide.1), calls=%async_computation.1 | async-start | bytes 2359296 | tf_op jit(solution)/shard_map/all_to_all | solution.py:383
  207.2 0.0 copy-done.2
  207.2 7.4 %inverse_narrow.1.refs_1_ = f32[6,3,192,128]{3,2,1,0:T(8,128)} custom-call(f32[16,3,24,128]{3,2,1,0:T(8,128)} %copy-done.2, bf16[384,288]{1,0:T(8,128)(2,1)} %constant.19.clone.refs_1_.refs_2_, bf16[2,2,768,256]{3,2,1,0:T(8,128)(2,1)} %constant.24.clone.refs_2_), custom_call_target="tpu_custom_call" | custom-call | flops 4000000000 | bytes 6000000 | tf_op jit(solution)/shard_map/inverse_narrow/pallas_call | solution.py:365
  214.7 19.8 %all-to-all-done.1.refs_0_ = f32[16,3,48,128]{3,2,1,0:T(8,128)S(1)} async-done(((f32[16,3,48,128]{3,2,1,0:T(8,128)}), f32[16,3,48,128]{3,2,1,0:T(8,128)S(1)}, u32[]{:S(2)}, u32[]{:S(2)}) %all-to-all-start.1) | async-done | bytes 1179680 | tf_op jit(solution)/shard_map/all_to_all | solution.py:383
  234.5 1.0 copy-done.1
  235.5 8.1 %inverse_wide.1 = f32[1,6,4,18432]{3,2,1,0:T(4,128)} custom-call(f32[16,3,48,128]{3,2,1,0:T(8,128)} %copy-done.1, f32[6,3,192,128]{3,2,1,0:T(8,128)} %inverse_narrow.1.refs_1_, bf16[384,288]{1,0:T(8,128)(2,1)} %constant.19.clone.refs_1_.refs_2_, bf16[1,2,768,256]{3,2,1,0:T(8,128)(2,1)} %constant.25.clone.refs_3_), custom_call_target="tpu_custom_call" | custom-call | flops 4000000000 | bytes 6000000 | tf_op jit(solution)/shard_map/inverse_wide/pallas_call | solution.py:365
  243.6 2.5 %collective-permute-start = (f32[1,6,4,18432]{3,2,1,0:T(4,128)}, f32[1,6,4,18432]{3,2,1,0:T(4,128)S(1)}, u32[]{:S(2)}, u32[]{:S(2)}) collective-permute-start(f32[1,6,4,18432]{3,2,1,0:T(4,128)} %inverse_wide.1), channel_id=1, source_target_pairs={{16,0},{0,16},{17,1},{1,17},{18,2},{2,18},{19,3},{3,19},{20,4},{4,... | collective-permute-start | bytes 5308424 | tf_op jit(solution)/shard_map/ppermute | solution.py:428
  246.1 3.5 %collective-permute-done = f32[1,6,4,18432]{3,2,1,0:T(4,128)S(1)} collective-permute-done((f32[1,6,4,18432]{3,2,1,0:T(4,128)}, f32[1,6,4,18432]{3,2,1,0:T(4,128)S(1)}, u32[]{:S(2)}, u32[]{:S(2)}) %collective-permute-start) | collective-permute-done | bytes 1769504 | tf_op jit(solution)/shard_map/ppermute | solution.py:428
  249.6 4.0 %fusion = (f32[1,4,6,18432]{3,1,2,0:T(4,128)}, f32[1,4,6,18432]{3,1,2,0:T(4,128)}) fusion(f32[1,6,4,18432]{3,2,1,0:T(4,128)S(1)} %collective-permute-done, f32[1,6,4,18432]{3,2,1,0:T(4,128)} %inverse_wide.1), kind=kLoop, calls=%fused_computation.1 | loop fusion | flops 1769472 | bytes 7077888 | tf_op jit(solution)/shard_map/transpose | solution.py:446
  (4 shorter events, 0.0 us)
Async XLA Ops:
  12.3 57.9 %all-to-all-start.2 = ((f32[16,3,2,1,48,128]{5,4,3,2,1,0:T(8,128)}), f32[16,3,2,1,48,128]{5,4,3,2,1,0:T(8,128)S(1)}, u32[]{:S(2)}, u32[]{:S(2)}) async-start(f32[16,3,2,1,48,128]{5,4,3,2,1,0:T(8,128)} %bitcast.11), calls=%async_computation.2 | async-start | bytes 4718592 | tf_op jit(solution)/shard_map/all_to_all | solution.py:383
  70.2 1.4 copy-start
  70.2 8.0 %copy-start.3 = (s32[4,16,2]{1,2,0:T(2,128)S(1)}, s32[4,16,2]{1,2,0:T(2,128)}, u32[]{:S(2)}) copy-start(s32[4,16,2]{1,2,0:T(2,128)} %param.14) | copy-start | bytes 1540
  71.6 107.3 %all-to-all-start = ((f32[16,3,2,2,48,128]{5,4,3,2,1,0:T(8,128)}), f32[16,3,2,2,48,128]{5,4,3,2,1,0:T(8,128)}, u32[]{:S(2)}, u32[]{:S(2)}) async-start(f32[16,3,2,2,48,128]{5,4,3,2,1,0:T(8,128)} %bitcast.10), calls=%async_computation | async-start | bytes 9437184 | tf_op jit(solution)/shard_map/all_to_all | solution.py:383
  178.9 23.6 %all-to-all-start.3 = ((f32[16,3,24,128]{3,2,1,0:T(8,128)}), f32[16,3,24,128]{3,2,1,0:T(8,128)S(1)}, u32[]{:S(2)}, u32[]{:S(2)}) async-start(f32[16,3,24,128]{3,2,1,0:T(8,128)} %middle_narrow.1), calls=%async_computation.3 | async-start | bytes 1179648 | tf_op jit(solution)/shard_map/all_to_all | solution.py:383
  202.5 4.8 %copy-start.2 = (f32[16,3,24,128]{3,2,1,0:T(8,128)}, f32[16,3,24,128]{3,2,1,0:T(8,128)S(1)}, u32[]{:S(2)}) copy-start(f32[16,3,24,128]{3,2,1,0:T(8,128)S(1)} %all-to-all-done.3.refs_0_) | copy-start | bytes 1769476
  202.5 32.0 %all-to-all-start.1 = ((f32[16,3,48,128]{3,2,1,0:T(8,128)}), f32[16,3,48,128]{3,2,1,0:T(8,128)S(1)}, u32[]{:S(2)}, u32[]{:S(2)}) async-start(f32[16,3,48,128]{3,2,1,0:T(8,128)} %middle_wide.1), calls=%async_computation.1 | async-start | bytes 2359296 | tf_op jit(solution)/shard_map/all_to_all | solution.py:383
  234.5 1.0 copy-start.1
  243.6 6.1 %collective-permute-start = (f32[1,6,4,18432]{3,2,1,0:T(4,128)}, f32[1,6,4,18432]{3,2,1,0:T(4,128)S(1)}, u32[]{:S(2)}, u32[]{:S(2)}) collective-permute-start(f32[1,6,4,18432]{3,2,1,0:T(4,128)} %inverse_wide.1), channel_id=1, source_target_pairs={{16,0},{0,16},{17,1},{1,17},{18,2},{2,18},{19,3},{3,19},{20,4},{4,... | collective-permute-start | bytes 5308424 | tf_op jit(solution)/shard_map/ppermute | solution.py:428

commit v3 on v2

--- a/solution.py
+++ b/solution.py
@@ -14,6 +14,7 @@
 LANES = 128
 SUB = 8
 GRANT = 56 << 20
+SMALL_GRANT = 24 << 20
 
 
 def unitary(length):
@@ -127,16 +128,23 @@
     return lax.broadcasted_iota(jnp.int32, shape, len(shape) - 1)
 
 
-def forward_kernel(narrow, sites, pairs_y, field_a, field_b, depth, table, token, out, spectra):
-    x = pl.program_id(0)
+def forward_kernel(narrow, sites, pairs_y, field_a, field_b, depth, table, token, out, packed, *spectra):
+    for site in range(field_a.shape[1]):
+        spaces = spectra[2 * site], spectra[2 * site + 1]
+        forward_site(narrow, pairs_y, field_a.at[0, site], field_b.at[0, site], depth, table, packed.at[site], spaces)
+        for block in range(out.shape[0]):
+            out[block, site] = packed[site, block * SUB : (block + 1) * SUB, :]
+
+
+def forward_site(narrow, pairs_y, field_a, field_b, depth, table, packed, spectra):
     groups = 1 if narrow else 2
     width = LANES // 4 if narrow else LANES // 2
-    block = 2 * groups * sites * SUB
+    block = 2 * groups * SUB
     slots = []
     for group, field in enumerate((field_a, field_b)):
         tiles = [
             jnp.concatenate(
-                [field[0, 0, :, (3 * p + q) * LANES : (3 * p + q + 1) * LANES] for p in range(pairs_y)], axis=0
+                [field[:, (3 * p + q) * LANES : (3 * p + q + 1) * LANES] for p in range(pairs_y)], axis=0
             )
             for q in range(3)
         ]
@@ -145,11 +153,11 @@
             left = [tiles[e + k][part] for part in (0, 1, 0) for k in range(2)]
             result = dot(jnp.concatenate(left, axis=1), depth[e])
             for part in range(2):
-                spectra[group, part * 2 + e] = result[:, part * LANES : (part + 1) * LANES]
+                spectra[group][part * 2 + e] = result[:, part * LANES : (part + 1) * LANES]
 
         def rows_of(c, group=group):
             return jnp.concatenate(
-                [spectra[group, k, pl.ds(c, pairs_y, stride=SUB), :] for k in range(4)], axis=0
+                [spectra[group][k, pl.ds(c, pairs_y, stride=SUB), :] for k in range(4)], axis=0
             )
 
         if narrow:
@@ -169,8 +177,8 @@
             odd = result[(2 * part + 1) * half : (2 * part + 2) * half]
             merged = jnp.where(lane_index(even.shape) // width % 2 == 0, even, odd)
             for i, (group, slot, _) in enumerate(batch):
-                start = ((part * groups + group) * sites + x) * SUB + slot
-                out[pl.ds(start, half, stride=block), :] = merged[:, i * LANES : (i + 1) * LANES]
+                start = (part * groups + group) * SUB + slot
+                packed[pl.ds(start, half, stride=block), :] = merged[:, i * LANES : (i + 1) * LANES]
 
 
 def forward(field_a, field_b, depth, table, narrow, token):
@@ -179,20 +187,26 @@
     size = table.shape[0] // 2
     pairs_y = size // 2
     lines = size // 2
-    rows = lines * 2 * groups * sites * SUB
-    spot = pl.BlockSpec((1, 1, components, flat), lambda x: (0, x, 0, 0))
+    blocks = lines * 2 * groups
+    step = 1
+    spot = pl.BlockSpec((1, step, components, flat), lambda x: (0, x, 0, 0))
     whole = lambda value: pl.BlockSpec(value.shape, lambda x: (0,) * value.ndim)
     return pl.pallas_call(
         functools.partial(forward_kernel, narrow, sites, pairs_y),
-        grid=(sites,),
+        grid=(sites // step,),
         in_specs=[spot, spot, whole(depth), whole(table), pl.BlockSpec(memory_space=pl.ANY)],
-        out_specs=pl.BlockSpec((rows, LANES), lambda x: (0, 0)),
-        out_shape=jax.ShapeDtypeStruct((rows, LANES), jnp.float32),
-        scratch_shapes=[pltpu.VMEM((2, 4, pairs_y * SUB, LANES), jnp.float32)],
+        out_specs=pl.BlockSpec((blocks, step, SUB, LANES), lambda x: (0, x, 0, 0)),
+        out_shape=jax.ShapeDtypeStruct((blocks, sites, SUB, LANES), jnp.float32),
+        scratch_shapes=[pltpu.VMEM((step, blocks * SUB, LANES), jnp.float32)]
+        + [pltpu.VMEM((4, pairs_y * SUB, LANES), jnp.float32)] * (2 * step),
         compiler_params=pltpu.CompilerParams(vmem_limit_bytes=GRANT),
         cost_estimate=pl.CostEstimate(flops=8 * 10**9, bytes_accessed=12 * 10**6, transcendentals=0),
         name="forward_narrow" if narrow else "forward_wide",
     )(field_a, field_b, depth, table, token)
+
+
+def placed(space, *values):
+    return [pltpu.with_memory_space_constraint(value, space) for value in values]
 
 
 def each(refs):
@@ -239,7 +253,7 @@
             )
 
         zero = jnp.zeros((size, LANES), jnp.float32)
-        real, imag = lax.fori_loop(0, count, pair, (zero, zero), unroll=2)
+        real, imag = lax.fori_loop(0, count, pair, (zero, zero), unroll=4)
         mixed[c, 0:size, :] = real
         mixed[c, size:both, :] = imag
         return carry
@@ -286,24 +300,23 @@
             pltpu.VMEM((channels, 2 * size, LANES), jnp.float32),
             pltpu.VMEM((devices * rows, LANES), jnp.float32),
         ],
-        compiler_params=pltpu.CompilerParams(vmem_limit_bytes=GRANT),
+        compiler_params=pltpu.CompilerParams(vmem_limit_bytes=SMALL_GRANT),
         cost_estimate=pl.CostEstimate(flops=4 * 10**9, bytes_accessed=10 * 10**6, transcendentals=0),
         name="middle_narrow" if narrow else "middle_wide",
-    )(pairs, signs, *pieces, table_f, table_i)
+    )(pairs, signs, *placed(pltpu.VMEM if narrow else pltpu.HBM, *pieces), *placed(pltpu.HBM, table_f, table_i))
 
 
 def inverse_kernel(narrow, arrays, devices, channels, pairs_y, *refs):
     pieces, refs = each(refs[:arrays]), refs[arrays:]
     if narrow:
         table, depth, out, lines = refs
-        staged = out.at[0]
+        staged = partial = out
     else:
         partial, table, depth, out, lines, staged = refs
-    x = pl.program_id(0)
     thirds = pieces[0].shape[0]
     size = thirds * devices
 
-    @pl.when(x == 0)
+    @pl.when(pl.program_id(0) == 0)
     def _():
         for s in range(devices):
             for r in range(thirds):
@@ -311,6 +324,14 @@
                     start = v * SUB * size + r * devices + s
                     lines[pl.ds(start, SUB, stride=size), :] = pieces[s][r, v * SUB : (v + 1) * SUB, :]
 
+    step = partial.shape[0]
+    for site in range(step):
+        x = pl.program_id(0) * step + site
+        place = None if narrow else out.at[0, site]
+        inverse_site(narrow, channels, pairs_y, size, x, lines, table, depth, staged.at[site], partial.at[site], place)
+
+
+def inverse_site(narrow, channels, pairs_y, size, x, lines, table, depth, staged, partial, out):
     def tile(*spots):
         return jnp.concatenate([lines[pl.ds(pl.multiple_of(k * size, SUB), size), :] for k in spots], axis=0)
 
@@ -351,7 +372,7 @@
             rows = slice(p * channels, (p + 1) * channels)
             for q in range(3):
                 lanes = slice((3 * p + q) * LANES, (3 * p + q + 1) * LANES)
-                out[0, 0, :, lanes] = staged[q, rows, :] + partial[0, q, rows, :]
+                out[:, lanes] = staged[q, rows, :] + partial[q, rows, :]
 
 
 def inverse(pieces, partial, table, depth, sites, channels, flat):
@@ -361,18 +382,19 @@
     whole = lambda value: pl.BlockSpec(value.shape, lambda x: (0,) * value.ndim)
     tiles = (3, size * channels, LANES)
     lines = pltpu.VMEM((sites * pieces[0].shape[2] // sites * size, LANES), jnp.float32)
-    kept = pl.BlockSpec((1,) + tiles, lambda x: (x, 0, 0, 0))
+    step = 3 if sites % 3 == 0 else 1
+    kept = pl.BlockSpec((step,) + tiles, lambda x: (x, 0, 0, 0))
     return pl.pallas_call(
         functools.partial(inverse_kernel, narrow, len(pieces), devices, channels, size),
-        grid=(sites,),
+        grid=(sites // step,),
         in_specs=[whole(v) for v in pieces] + ([] if narrow else [kept]) + [whole(table), whole(depth)],
-        out_specs=kept if narrow else pl.BlockSpec((1, 1, channels, flat), lambda x: (0, x, 0, 0)),
+        out_specs=kept if narrow else pl.BlockSpec((1, step, channels, flat), lambda x: (0, x, 0, 0)),
         out_shape=jax.ShapeDtypeStruct((sites,) + tiles if narrow else (1, sites, channels, flat), jnp.float32),
-        scratch_shapes=[lines] if narrow else [lines, pltpu.VMEM(tiles, jnp.float32)],
-        compiler_params=pltpu.CompilerParams(vmem_limit_bytes=GRANT),
+        scratch_shapes=[lines] if narrow else [lines, pltpu.VMEM((step,) + tiles, jnp.float32)],
+        compiler_params=pltpu.CompilerParams(vmem_limit_bytes=SMALL_GRANT),
         cost_estimate=pl.CostEstimate(flops=4 * 10**9, bytes_accessed=6 * 10**6, transcendentals=0),
         name="inverse_narrow" if narrow else "inverse_wide",
-    )(*pieces, *([] if narrow else [partial]), table, depth)
+    )(*placed(pltpu.VMEM, *pieces), *([] if narrow else placed(pltpu.HBM, partial)), *placed(pltpu.HBM, table, depth))
 
 
 AT_ONCE = dict(sent_narrow=True, sent_wide=True, back_narrow=True, back_wide=True)
@@ -409,7 +431,7 @@
         name = "sent_narrow" if narrow else "sent_wide"
         groups = 1 if narrow else 2
         packed = forward(field_a, field_b, depth, table(0, name), narrow, token)
-        token = packed[:SUB]
+        token = packed[0, 0]
         packed = packed.reshape(devices, thirds, 2, groups, sites * SUB, LANES)
         sent[narrow] = exchange(packed, AT_ONCE[name])
     result = None

time: 254 us -> 249 us (0.980)
  Pallas kernels: 66.5 us -> 59.1 us
  waiting for transfers between devices: 149 us -> 153 us
    all_to_all x4, waiting for transfers between devices: 145 us -> 149 us  [exchange(): return [lax.all_to_all(packed, 'space', 0, 0, tiled=True)]]
    pallas_call x2, Pallas kernels: 15.5 us -> 11.7 us  [inverse(): pl.pallas_call(functools.partial(inverse_kernel, narrow, len(pieces), dev...]
  transfers between devices with their start and end apart: 5 -> 5, of which waited for: 5 -> 5; matrix products, arithmetic and copies ran while one was open for 1% -> 1% of each run, Pallas kernels for 18% -> 17%
where the time goes in v3:
time: 249 us
  waiting for transfers between devices  153 us (61%)
  Pallas kernels  59.1 us (24%)
  starting transfers between devices  29.3 us (12%)
  other arithmetic  4.02 us (2%)
  local copies, waits for them, and re-layouts  2.68 us (1%)
    all_to_all x4, waiting for transfers between devices, exchange(): return [lax.all_to_all(packed, 'space', 0, 0, tiled=True)]  149 us
    all_to_all x4, starting transfers between devices, exchange(): return [lax.all_to_all(packed, 'space', 0, 0, tiled=True)]  26.8 us
    pallas_call x2, Pallas kernels, forward(): pl.pallas_call(functools.partial(forward_kernel, narrow, sites, pairs_y),...  24.9 us
    pallas_call x2, Pallas kernels, middle(): pl.pallas_call(functools.partial(middle_kernel, narrow, len(pieces), devi...  22.5 us
    pallas_call x2, Pallas kernels, inverse(): pl.pallas_call(functools.partial(inverse_kernel, narrow, len(pieces), dev...  11.7 us
  transfers between devices with their start and end apart: 5, of which 5 were waited for; matrix products, arithmetic and copies ran while one was open for 1% of the time, Pallas kernels for 17%

profile of v3, /device:TPU:9, one launch (start us, length us, event | category | flops | bytes accessed | tf_op | source)
XLA Modules:
  0.0 248.5 jit_solution(2052447827044709057)
XLA Ops:
  0.6 10.5 %forward_narrow.1 = f32[96,6,8,128]{3,2,1,0:T(8,128)} custom-call(f32[1,6,8,18432]{3,2,1,0:T(8,128)} %bitcast.16, f32[1,6,8,18432]{3,2,1,0:T(8,128)} %bitcast.18, bf16[2,768,256]{2,1,0:T(8,128)(2,1)} %constant.22.clone.depth, bf16[192,576]{1,0:T(8,128)(2,1)} %constant.18.clone.table, s32[4,16]{1,0:T(4,128)} %signs.3), custom_call_target="tpu_custom_call" | custom-call | flops 8000000000 | bytes 12000000 | tf_op jit(solution)/shard_map/forward_narrow/pallas_call | solution.py:194
  11.1 6.7 %all-to-all-start.2 = ((f32[16,3,2,1,48,128]{5,4,3,2,1,0:T(8,128)}), f32[16,3,2,1,48,128]{5,4,3,2,1,0:T(8,128)S(1)}, u32[]{:S(2)}, u32[]{:S(2)}) async-start(f32[16,3,2,1,48,128]{5,4,3,2,1,0:T(8,128)} %bitcast.13), calls=%async_computation.2 | async-start | bytes 4718592 | tf_op jit(solution)/shard_map/all_to_all | solution.py:405
  17.8 1.3 slice_bitcast_fusion.token
  19.1 14.4 %forward_wide.1 = f32[192,6,8,128]{3,2,1,0:T(8,128)} custom-call(f32[1,6,8,18432]{3,2,1,0:T(8,128)} %bitcast.17, f32[1,6,8,18432]{3,2,1,0:T(8,128)} %bitcast.19, bf16[2,768,256]{2,1,0:T(8,128)(2,1)} %constant.23.clone.depth, bf16[192,576]{1,0:T(8,128)(2,1)} %constant.18.clone.table, f32[8,128]{1,0:T(8,128)} %slice_bitcast_fusion.token), custom_call_target="tpu_custom_call" | custom-call | flops 8000000000 | bytes 12000000 | tf_op jit(solution)/shard_map/forward_wide/pallas_call | solution.py:194
  33.5 35.5 %all-to-all-done.2.refs_0_ = f32[16,3,2,1,48,128]{5,4,3,2,1,0:T(8,128)S(1)} async-done(((f32[16,3,2,1,48,128]{5,4,3,2,1,0:T(8,128)}), f32[16,3,2,1,48,128]{5,4,3,2,1,0:T(8,128)S(1)}, u32[]{:S(2)}, u32[]{:S(2)}) %all-to-all-start.2) | async-done | bytes 2359328 | tf_op jit(solution)/shard_map/all_to_all | solution.py:405
  69.0 6.7 %all-to-all-start = ((f32[16,3,2,2,48,128]{5,4,3,2,1,0:T(8,128)}), f32[16,3,2,2,48,128]{5,4,3,2,1,0:T(8,128)}, u32[]{:S(2)}, u32[]{:S(2)}) async-start(f32[16,3,2,2,48,128]{5,4,3,2,1,0:T(8,128)} %bitcast.12), calls=%async_computation | async-start | bytes 9437184 | tf_op jit(solution)/shard_map/all_to_all | solution.py:405
  75.8 0.0 copy-done.2
  75.8 0.1 copy.15
  75.9 0.1 copy.16.pairs
  76.0 0.0 copy-done
  76.0 10.1 %middle_narrow.1 = f32[16,3,24,128]{3,2,1,0:T(8,128)} custom-call(s32[4,32]{1,0:T(4,128)S(1)} %copy.16.pairs, s32[4,16]{1,0:T(4,128)S(1)} %copy-done, f32[16,3,2,1,48,128]{5,4,3,2,1,0:T(8,128)S(1)} %all-to-all-done.2.refs_0_, bf16[192,576]{1,0:T(8,128)(2,1)} %constant.20.clone.refs_1_, bf16[192,576]{1,0:T(8,128)(2,1)} %constant.21.clone.refs_2_), custom_call_target="tpu_custom_call" | custom-call | flops 4000000000 | bytes 10000000 | tf_op jit(solution)/shard_map/middle_narrow/pallas_call | solution.py:291
  86.1 90.4 %all-to-all-done.refs_0_ = f32[16,3,2,2,48,128]{5,4,3,2,1,0:T(8,128)} async-done(((f32[16,3,2,2,48,128]{5,4,3,2,1,0:T(8,128)}), f32[16,3,2,2,48,128]{5,4,3,2,1,0:T(8,128)}, u32[]{:S(2)}, u32[]{:S(2)}) %all-to-all-start) | async-done | bytes 4718624 | tf_op jit(solution)/shard_map/all_to_all | solution.py:405
  176.4 8.7 %all-to-all-start.3 = ((f32[16,3,24,128]{3,2,1,0:T(8,128)}), f32[16,3,24,128]{3,2,1,0:T(8,128)S(1)}, u32[]{:S(2)}, u32[]{:S(2)}) async-start(f32[16,3,24,128]{3,2,1,0:T(8,128)} %middle_narrow.1), calls=%async_computation.3 | async-start | bytes 1179648 | tf_op jit(solution)/shard_map/all_to_all | solution.py:405
  185.2 12.4 %middle_wide.1 = f32[16,3,48,128]{3,2,1,0:T(8,128)} custom-call(s32[4,32]{1,0:T(4,128)S(1)} %copy.16.pairs, s32[4,16]{1,0:T(4,128)S(1)} %copy-done, f32[16,3,2,2,48,128]{5,4,3,2,1,0:T(8,128)} %all-to-all-done.refs_0_, bf16[192,576]{1,0:T(8,128)(2,1)} %constant.20.clone.refs_1_, bf16[192,576]{1,0:T(8,128)(2,1)} %constant.21.clone.refs_2_), custom_call_target="tpu_custom_call" | custom-call | flops 4000000000 | bytes 10000000 | tf_op jit(solution)/shard_map/middle_wide/pallas_call | solution.py:291
  197.6 2.5 all-to-all-done.3.refs_0_
  200.1 4.7 %all-to-all-start.1 = ((f32[16,3,48,128]{3,2,1,0:T(8,128)}), f32[16,3,48,128]{3,2,1,0:T(8,128)S(1)}, u32[]{:S(2)}, u32[]{:S(2)}) async-start(f32[16,3,48,128]{3,2,1,0:T(8,128)} %middle_wide.1), calls=%async_computation.1 | async-start | bytes 2359296 | tf_op jit(solution)/shard_map/all_to_all | solution.py:405
  204.7 5.1 %inverse_narrow.1.refs_1_ = f32[6,3,192,128]{3,2,1,0:T(8,128)S(1)} custom-call(f32[16,3,24,128]{3,2,1,0:T(8,128)S(1)} %all-to-all-done.3.refs_0_, bf16[384,288]{1,0:T(8,128)(2,1)} %constant.19.clone.refs_1_.refs_2_, bf16[2,2,768,256]{3,2,1,0:T(8,128)(2,1)} %constant.24.clone.refs_2_), custom_call_target="tpu_custom_call" | custom-call | flops 4000000000 | bytes 6000000 | tf_op jit(solution)/shard_map/inverse_narrow/pallas_call | solution.py:387
  209.9 0.0 copy-start.1
  209.9 1.2 copy-done.1
  211.1 20.8 %all-to-all-done.1.refs_0_ = f32[16,3,48,128]{3,2,1,0:T(8,128)S(1)} async-done(((f32[16,3,48,128]{3,2,1,0:T(8,128)}), f32[16,3,48,128]{3,2,1,0:T(8,128)S(1)}, u32[]{:S(2)}, u32[]{:S(2)}) %all-to-all-start.1) | async-done | bytes 1179680 | tf_op jit(solution)/shard_map/all_to_all | solution.py:405
  231.9 6.5 %inverse_wide.1 = f32[1,6,4,18432]{3,2,1,0:T(4,128)} custom-call(f32[16,3,48,128]{3,2,1,0:T(8,128)S(1)} %all-to-all-done.1.refs_0_, f32[6,3,192,128]{3,2,1,0:T(8,128)} %copy-done.1, bf16[384,288]{1,0:T(8,128)(2,1)} %constant.19.clone.refs_1_.refs_2_, bf16[1,2,768,256]{3,2,1,0:T(8,128)(2,1)} %constant.25.clone.refs_3_), custom_call_target="tpu_custom_call" | custom-call | flops 4000000000 | bytes 6000000 | tf_op jit(solution)/shard_map/inverse_wide/pallas_call | solution.py:387
  238.4 2.5 %collective-permute-start = (f32[1,6,4,18432]{3,2,1,0:T(4,128)}, f32[1,6,4,18432]{3,2,1,0:T(4,128)S(1)}, u32[]{:S(2)}, u32[]{:S(2)}) collective-permute-start(f32[1,6,4,18432]{3,2,1,0:T(4,128)} %inverse_wide.1), channel_id=1, source_target_pairs={{16,0},{0,16},{17,1},{1,17},{18,2},{2,18},{19,3},{3,19},{20,4},{4,... | collective-permute-start | bytes 5308424 | tf_op jit(solution)/shard_map/ppermute | solution.py:450
  241.0 3.5 %collective-permute-done = f32[1,6,4,18432]{3,2,1,0:T(4,128)S(1)} collective-permute-done((f32[1,6,4,18432]{3,2,1,0:T(4,128)}, f32[1,6,4,18432]{3,2,1,0:T(4,128)S(1)}, u32[]{:S(2)}, u32[]{:S(2)}) %collective-permute-start) | collective-permute-done | bytes 1769504 | tf_op jit(solution)/shard_map/ppermute | solution.py:450
  244.5 4.0 %fusion = (f32[1,4,6,18432]{3,1,2,0:T(4,128)}, f32[1,4,6,18432]{3,1,2,0:T(4,128)}) fusion(f32[1,6,4,18432]{3,2,1,0:T(4,128)S(1)} %collective-permute-done, f32[1,6,4,18432]{3,2,1,0:T(4,128)} %inverse_wide.1), kind=kLoop, calls=%fused_computation.1 | loop fusion | flops 1769472 | bytes 7077888 | tf_op jit(solution)/shard_map/transpose | solution.py:468
  (2 shorter events, 0.0 us)
Async XLA Ops:
  11.1 57.9 %all-to-all-start.2 = ((f32[16,3,2,1,48,128]{5,4,3,2,1,0:T(8,128)}), f32[16,3,2,1,48,128]{5,4,3,2,1,0:T(8,128)S(1)}, u32[]{:S(2)}, u32[]{:S(2)}) async-start(f32[16,3,2,1,48,128]{5,4,3,2,1,0:T(8,128)} %bitcast.13), calls=%async_computation.2 | async-start | bytes 4718592 | tf_op jit(solution)/shard_map/all_to_all | solution.py:405
  69.0 6.7 %copy-start.2 = (s32[4,16,2]{1,2,0:T(2,128)S(1)}, s32[4,16,2]{1,2,0:T(2,128)}, u32[]{:S(2)}) copy-start(s32[4,16,2]{1,2,0:T(2,128)} %param.14) | copy-start | bytes 1540
  69.0 6.9 %copy-start = (s32[4,16]{1,0:T(4,128)S(1)}, s32[4,16]{1,0:T(4,128)}, u32[]{:S(2)}) copy-start(s32[4,16]{1,0:T(4,128)} %signs.3) | copy-start | bytes 772
  69.0 107.4 %all-to-all-start = ((f32[16,3,2,2,48,128]{5,4,3,2,1,0:T(8,128)}), f32[16,3,2,2,48,128]{5,4,3,2,1,0:T(8,128)}, u32[]{:S(2)}, u32[]{:S(2)}) async-start(f32[16,3,2,2,48,128]{5,4,3,2,1,0:T(8,128)} %bitcast.12), calls=%async_computation | async-start | bytes 9437184 | tf_op jit(solution)/shard_map/all_to_all | solution.py:405
  176.4 23.6 %all-to-all-start.3 = ((f32[16,3,24,128]{3,2,1,0:T(8,128)}), f32[16,3,24,128]{3,2,1,0:T(8,128)S(1)}, u32[]{:S(2)}, u32[]{:S(2)}) async-start(f32[16,3,24,128]{3,2,1,0:T(8,128)} %middle_narrow.1), calls=%async_computation.3 | async-start | bytes 1179648 | tf_op jit(solution)/shard_map/all_to_all | solution.py:405
  200.1 31.8 %all-to-all-start.1 = ((f32[16,3,48,128]{3,2,1,0:T(8,128)}), f32[16,3,48,128]{3,2,1,0:T(8,128)S(1)}, u32[]{:S(2)}, u32[]{:S(2)}) async-start(f32[16,3,48,128]{3,2,1,0:T(8,128)} %middle_wide.1), calls=%async_computation.1 | async-start | bytes 2359296 | tf_op jit(solution)/shard_map/all_to_all | solution.py:405
  209.9 1.2 copy-start.1
  238.4 6.1 %collective-permute-start = (f32[1,6,4,18432]{3,2,1,0:T(4,128)}, f32[1,6,4,18432]{3,2,1,0:T(4,128)S(1)}, u32[]{:S(2)}, u32[]{:S(2)}) collective-permute-start(f32[1,6,4,18432]{3,2,1,0:T(4,128)} %inverse_wide.1), channel_id=1, source_target_pairs={{16,0},{0,16},{17,1},{1,17},{18,2},{2,18},{19,3},{3,19},{20,4},{4,... | collective-permute-start | bytes 5308424 | tf_op jit(solution)/shard_map/ppermute | solution.py:450

commit v4 on v3

--- a/solution.py
+++ b/solution.py
@@ -375,19 +375,22 @@
                 out[:, lanes] = staged[q, rows, :] + partial[q, rows, :]
 
 
-def inverse(pieces, partial, table, depth, sites, channels, flat):
+def inverse(pieces, partial, table, depth, sites, channels, flat, share=0, shares=1):
     narrow = partial is None
     size = table.shape[1] // 6
     devices = size // pieces[0].shape[1]
     whole = lambda value: pl.BlockSpec(value.shape, lambda x: (0,) * value.ndim)
     tiles = (3, size * channels, LANES)
-    lines = pltpu.VMEM((sites * pieces[0].shape[2] // sites * size, LANES), jnp.float32)
+    rows = pieces[0].shape[2] // shares
+    sites = sites // shares
+    lines = pltpu.VMEM((rows * size, LANES), jnp.float32)
+    part = lambda value: pl.BlockSpec(value.shape[:2] + (rows, LANES), lambda x: (0, 0, share, 0))
     step = 3 if sites % 3 == 0 else 1
-    kept = pl.BlockSpec((step,) + tiles, lambda x: (x, 0, 0, 0))
+    kept = pl.BlockSpec((step,) + tiles, lambda x: (x + share * sites // step, 0, 0, 0))
     return pl.pallas_call(
         functools.partial(inverse_kernel, narrow, len(pieces), devices, channels, size),
         grid=(sites // step,),
-        in_specs=[whole(v) for v in pieces] + ([] if narrow else [kept]) + [whole(table), whole(depth)],
+        in_specs=[part(v) for v in pieces] + ([] if narrow else [kept]) + [whole(table), whole(depth)],
         out_specs=kept if narrow else pl.BlockSpec((1, step, channels, flat), lambda x: (0, x, 0, 0)),
         out_shape=jax.ShapeDtypeStruct((sites,) + tiles if narrow else (1, sites, channels, flat), jnp.float32),
         scratch_shapes=[lines] if narrow else [lines, pltpu.VMEM((step,) + tiles, jnp.float32)],
@@ -434,13 +437,16 @@
         token = packed[0, 0]
         packed = packed.reshape(devices, thirds, 2, groups, sites * SUB, LANES)
         sent[narrow] = exchange(packed, AT_ONCE[name])
-    result = None
+    partial = None
+    shares = 2 if sites % 2 == 0 and sites // 2 * 2 * channels % SUB == 0 else 1
     for narrow, depth in ((True, depth_in), (False, depth_iw)):
         come, go = ("sent_narrow", "back_narrow") if narrow else ("sent_wide", "back_wide")
         mixed = middle(sent[narrow], flat_pairs, signs, table(2, come), table(3, go), sites, channels, narrow)
         back = exchange(mixed, AT_ONCE[go])
-        result = inverse(back, result, table(1, go), depth, sites, channels, flat)
-    return result
+        shared = functools.partial(inverse, back, partial, table(1, go), depth, sites, channels, flat)
+        if narrow:
+            partial = shared()
+    return [shared(share, shares) for share in range(shares)]
 
 
 def neighbours(value):
@@ -459,13 +465,57 @@
     return correlator, later - correlator, later - 2.0 * correlator + earlier
 
 
+def differences_kernel(count, own, *refs):
+    later, earlier = refs[0], refs[count - 1]
+    outs = refs[-3:]
+    outs[0][...] = own[...]
+    outs[1][...] = later[...] - own[...]
+    outs[2][...] = later[...] - 2.0 * own[...] + earlier[...]
+
+
+def write_differences(own, others, share, shares, written):
+    _, sites, channels, flat = own.shape
+    block = (1, 1, channels, flat)
+    mine = pl.BlockSpec(block, lambda x: (0, x, 0, 0))
+    shape = jax.ShapeDtypeStruct((1, sites * shares, channels, flat), jnp.float32)
+    count = len(others)
+    return pl.pallas_call(
+        functools.partial(differences_kernel, count),
+        grid=(sites,),
+        in_specs=[mine] * (1 + count) + [pl.BlockSpec(memory_space=pl.ANY)] * len(written),
+        out_specs=[pl.BlockSpec(block, lambda x: (0, x + share * sites, 0, 0))] * 3,
+        out_shape=[shape] * 3,
+        input_output_aliases={1 + count + k: k for k in range(len(written))},
+        compiler_params=pltpu.CompilerParams(vmem_limit_bytes=SMALL_GRANT),
+        cost_estimate=pl.CostEstimate(flops=10**6, bytes_accessed=5 * own.size * 4, transcendentals=0),
+        name="differences",
+    )(own, *others, *written)
+
+
+def one_time(tables, field_a, field_b, pairs, signs):
+    devices = lax.axis_size("tm")
+    up = [(i, (i + 1) % devices) for i in range(devices)]
+    shares = fast_slice(field_a, field_b, pairs, signs, tables)
+    written = []
+    for share, own in enumerate(shares):
+        others = [lax.ppermute(own, "tm", [(j, i) for i, j in up])]
+        if devices != 2:
+            others.append(lax.ppermute(own, "tm", up))
+        written = write_differences(own, others, share, len(shares), written)
+    return written
+
+
 def fast_device(tables, field_a, field_b, pairs, signs):
     field_a, field_b = field_a.swapaxes(1, 2), field_b.swapaxes(1, 2)
-    parts = [
-        fast_slice(field_a[t : t + 1], field_b[t : t + 1], pairs, signs, tables)
-        for t in range(field_a.shape[0])
-    ]
-    return tuple(out.swapaxes(1, 2) for out in differences(jnp.concatenate(parts, axis=0)))
+    if field_a.shape[0] == 1:
+        outs = one_time(tables, field_a, field_b, pairs, signs)
+    else:
+        parts = [
+            jnp.concatenate(fast_slice(field_a[t : t + 1], field_b[t : t + 1], pairs, signs, tables), axis=1)
+            for t in range(field_a.shape[0])
+        ]
+        outs = differences(jnp.concatenate(parts, axis=0))
+    return tuple(out.swapaxes(1, 2) for out in outs)
 
 
 def dft_tables(length):

time: 249 us -> 247 us (level)
  Pallas kernels: 59.1 us -> 63.4 us
  other arithmetic: 4.02 us -> 0 us
  waiting for transfers between devices: 153 us -> 150 us
    transpose x1 -> x0, other arithmetic: 4.02 us -> none  [fast_device(): out.swapaxes(1, 2)]
    pallas_call x0 -> x2, Pallas kernels: none -> 3.86 us  [write_differences(): pl.pallas_call(functools.partial(differences_kernel, count), grid=(sites,...]
    ppermute x1 -> x2, waiting for transfers between devices: 3.53 us -> 0.46 us  [one_time(): others = [lax.ppermute(own, 'tm', [(j, i) for i, j in up])]]
    pallas_call x2 -> x3, Pallas kernels: 11.7 us -> 12.2 us  [inverse(): pl.pallas_call(functools.partial(inverse_kernel, narrow, len(pieces), dev...]
  transfers between devices with their start and end apart: 5 -> 6, of which waited for: 5 -> 5; matrix products, arithmetic and copies ran while one was open for 1% -> 1% of each run, Pallas kernels for 17% -> 19%
where the time goes in v4:
time: 247 us; the launch traced here: 246 us
  waiting for transfers between devices  150 us (61%)
  Pallas kernels  63.4 us (26%)
  starting transfers between devices  29.5 us (12%)
  local copies, waits for them, and re-layouts  2.68 us (1%)
    all_to_all x4, waiting for transfers between devices, exchange(): return [lax.all_to_all(packed, 'space', 0, 0, tiled=True)]  149 us
    all_to_all x4, starting transfers between devices, exchange(): return [lax.all_to_all(packed, 'space', 0, 0, tiled=True)]  26.8 us
    pallas_call x2, Pallas kernels, forward(): pl.pallas_call(functools.partial(forward_kernel, narrow, sites, pairs_y),...  24.9 us
    pallas_call x2, Pallas kernels, middle(): pl.pallas_call(functools.partial(middle_kernel, narrow, len(pieces), devi...  22.5 us
    pallas_call x3, Pallas kernels, inverse(): pl.pallas_call(functools.partial(inverse_kernel, narrow, len(pieces), dev...  12.2 us
  transfers between devices with their start and end apart: 6, of which 5 were waited for; matrix products, arithmetic and copies ran while one was open for 1% of the time, Pallas kernels for 19%

profile of v4, /device:TPU:9, one launch (start us, length us, event | category | flops | bytes accessed | tf_op | source)
XLA Modules:
  0.0 245.9 jit_solution(3727694069251473039)
XLA Ops:
  0.6 10.5 %forward_narrow.1 = f32[96,6,8,128]{3,2,1,0:T(8,128)} custom-call(f32[1,6,8,18432]{3,2,1,0:T(8,128)} %bitcast.16, f32[1,6,8,18432]{3,2,1,0:T(8,128)} %bitcast.18, bf16[2,768,256]{2,1,0:T(8,128)(2,1)} %constant.20.clone.depth, bf16[192,576]{1,0:T(8,128)(2,1)} %constant.16.clone.table, s32[4,16]{1,0:T(4,128)} %signs.3), custom_call_target="tpu_custom_call" | custom-call | flops 8000000000 | bytes 12000000 | tf_op jit(solution)/shard_map/forward_narrow/pallas_call | solution.py:194
  11.1 6.7 %all-to-all-start.2 = ((f32[16,3,2,1,48,128]{5,4,3,2,1,0:T(8,128)}), f32[16,3,2,1,48,128]{5,4,3,2,1,0:T(8,128)S(1)}, u32[]{:S(2)}, u32[]{:S(2)}) async-start(f32[16,3,2,1,48,128]{5,4,3,2,1,0:T(8,128)} %bitcast.11), calls=%async_computation.2 | async-start | bytes 4718592 | tf_op jit(solution)/shard_map/all_to_all | solution.py:408
  17.8 1.3 slice_bitcast_fusion.token
  19.1 14.4 %forward_wide.1 = f32[192,6,8,128]{3,2,1,0:T(8,128)} custom-call(f32[1,6,8,18432]{3,2,1,0:T(8,128)} %bitcast.17, f32[1,6,8,18432]{3,2,1,0:T(8,128)} %bitcast.19, bf16[2,768,256]{2,1,0:T(8,128)(2,1)} %constant.21.clone.depth, bf16[192,576]{1,0:T(8,128)(2,1)} %constant.16.clone.table, f32[8,128]{1,0:T(8,128)} %slice_bitcast_fusion.token), custom_call_target="tpu_custom_call" | custom-call | flops 8000000000 | bytes 12000000 | tf_op jit(solution)/shard_map/forward_wide/pallas_call | solution.py:194
  33.5 35.5 %all-to-all-done.2.refs_0_ = f32[16,3,2,1,48,128]{5,4,3,2,1,0:T(8,128)S(1)} async-done(((f32[16,3,2,1,48,128]{5,4,3,2,1,0:T(8,128)}), f32[16,3,2,1,48,128]{5,4,3,2,1,0:T(8,128)S(1)}, u32[]{:S(2)}, u32[]{:S(2)}) %all-to-all-start.2) | async-done | bytes 2359328 | tf_op jit(solution)/shard_map/all_to_all | solution.py:408
  69.0 6.7 %all-to-all-start = ((f32[16,3,2,2,48,128]{5,4,3,2,1,0:T(8,128)}), f32[16,3,2,2,48,128]{5,4,3,2,1,0:T(8,128)}, u32[]{:S(2)}, u32[]{:S(2)}) async-start(f32[16,3,2,2,48,128]{5,4,3,2,1,0:T(8,128)} %bitcast.10), calls=%async_computation | async-start | bytes 9437184 | tf_op jit(solution)/shard_map/all_to_all | solution.py:408
  75.8 0.1 copy.18
  75.8 0.1 copy.19.pairs
  75.9 10.1 %middle_narrow.1 = f32[16,3,24,128]{3,2,1,0:T(8,128)} custom-call(s32[4,32]{1,0:T(4,128)S(1)} %copy.19.pairs, s32[4,16]{1,0:T(4,128)S(1)} %copy-done, f32[16,3,2,1,48,128]{5,4,3,2,1,0:T(8,128)S(1)} %all-to-all-done.2.refs_0_, bf16[192,576]{1,0:T(8,128)(2,1)} %constant.18.clone.refs_1_, bf16[192,576]{1,0:T(8,128)(2,1)} %constant.19.clone.refs_2_), custom_call_target="tpu_custom_call" | custom-call | flops 4000000000 | bytes 10000000 | tf_op jit(solution)/shard_map/middle_narrow/pallas_call | solution.py:291
  86.0 90.4 %all-to-all-done.refs_0_ = f32[16,3,2,2,48,128]{5,4,3,2,1,0:T(8,128)} async-done(((f32[16,3,2,2,48,128]{5,4,3,2,1,0:T(8,128)}), f32[16,3,2,2,48,128]{5,4,3,2,1,0:T(8,128)}, u32[]{:S(2)}, u32[]{:S(2)}) %all-to-all-start) | async-done | bytes 4718624 | tf_op jit(solution)/shard_map/all_to_all | solution.py:408
  176.4 8.7 %all-to-all-start.3 = ((f32[16,3,24,128]{3,2,1,0:T(8,128)}), f32[16,3,24,128]{3,2,1,0:T(8,128)S(1)}, u32[]{:S(2)}, u32[]{:S(2)}) async-start(f32[16,3,24,128]{3,2,1,0:T(8,128)} %middle_narrow.1), calls=%async_computation.3 | async-start | bytes 1179648 | tf_op jit(solution)/shard_map/all_to_all | solution.py:408
  185.1 12.4 %middle_wide.1 = f32[16,3,48,128]{3,2,1,0:T(8,128)} custom-call(s32[4,32]{1,0:T(4,128)S(1)} %copy.19.pairs, s32[4,16]{1,0:T(4,128)S(1)} %copy-done, f32[16,3,2,2,48,128]{5,4,3,2,1,0:T(8,128)} %all-to-all-done.refs_0_, bf16[192,576]{1,0:T(8,128)(2,1)} %constant.18.clone.refs_1_, bf16[192,576]{1,0:T(8,128)(2,1)} %constant.19.clone.refs_2_), custom_call_target="tpu_custom_call" | custom-call | flops 4000000000 | bytes 10000000 | tf_op jit(solution)/shard_map/middle_wide/pallas_call | solution.py:291
  197.6 2.5 %all-to-all-done.3.refs_0_ = f32[16,3,24,128]{3,2,1,0:T(8,128)S(1)} async-done(((f32[16,3,24,128]{3,2,1,0:T(8,128)}), f32[16,3,24,128]{3,2,1,0:T(8,128)S(1)}, u32[]{:S(2)}, u32[]{:S(2)}) %all-to-all-start.3) | async-done | bytes 589856 | tf_op jit(solution)/shard_map/all_to_all | solution.py:408
  200.0 4.7 %all-to-all-start.1 = ((f32[16,3,48,128]{3,2,1,0:T(8,128)}), f32[16,3,48,128]{3,2,1,0:T(8,128)S(1)}, u32[]{:S(2)}, u32[]{:S(2)}) async-start(f32[16,3,48,128]{3,2,1,0:T(8,128)} %middle_wide.1), calls=%async_computation.1 | async-start | bytes 2359296 | tf_op jit(solution)/shard_map/all_to_all | solution.py:408
  204.7 5.1 %inverse_narrow.1.refs_1_ = f32[6,3,192,128]{3,2,1,0:T(8,128)S(1)} custom-call(f32[16,3,24,128]{3,2,1,0:T(8,128)S(1)} %all-to-all-done.3.refs_0_, bf16[384,288]{1,0:T(8,128)(2,1)} %constant.17.clone.refs_1_.refs_2_, bf16[2,2,768,256]{3,2,1,0:T(8,128)(2,1)} %constant.22.clone.refs_2_), custom_call_target="tpu_custom_call" | custom-call | flops 4000000000 | bytes 6000000 | tf_op jit(solution)/shard_map/inverse_narrow/pallas_call | solution.py:390
  209.9 1.2 copy-done.1
  211.1 20.8 %all-to-all-done.1.refs_0_ = f32[16,3,48,128]{3,2,1,0:T(8,128)S(1)} async-done(((f32[16,3,48,128]{3,2,1,0:T(8,128)}), f32[16,3,48,128]{3,2,1,0:T(8,128)S(1)}, u32[]{:S(2)}, u32[]{:S(2)}) %all-to-all-start.1) | async-done | bytes 1179680 | tf_op jit(solution)/shard_map/all_to_all | solution.py:408
  231.9 3.5 %inverse_wide.3.own = f32[1,3,4,18432]{3,2,1,0:T(4,128)S(1)} custom-call(f32[16,3,48,128]{3,2,1,0:T(8,128)S(1)} %all-to-all-done.1.refs_0_, f32[6,3,192,128]{3,2,1,0:T(8,128)} %copy-done.1, bf16[384,288]{1,0:T(8,128)(2,1)} %constant.17.clone.refs_1_.refs_2_, bf16[1,2,768,256]{3,2,1,0:T(8,128)(2,1)} %constant.23.clone.refs_3_), custom_call_target="tpu_custom_call" | custom-call | flops 4000000000 | bytes 6000000 | tf_op jit(solution)/shard_map/inverse_wide/pallas_call | solution.py:390
  235.4 2.6 %collective-permute-start.1 = (f32[1,3,4,18432]{3,2,1,0:T(4,128)S(1)}, f32[1,3,4,18432]{3,2,1,0:T(4,128)S(1)}, u32[]{:S(2)}, u32[]{:S(2)}) collective-permute-start(f32[1,3,4,18432]{3,2,1,0:T(4,128)S(1)} %inverse_wide.3.own), channel_id=1, source_target_pairs={{16,0},{0,16},{17,1},{1,17},{18,2},{2,18},{19,3},{3,19},{20,4},{4,... | collective-permute-start | bytes 2654216 | tf_op jit(solution)/shard_map/ppermute | solution.py:501
  238.0 3.5 %inverse_wide.2.own = f32[1,3,4,18432]{3,2,1,0:T(4,128)S(1)} custom-call(f32[16,3,48,128]{3,2,1,0:T(8,128)S(1)} %all-to-all-done.1.refs_0_, f32[6,3,192,128]{3,2,1,0:T(8,128)} %copy-done.1, bf16[384,288]{1,0:T(8,128)(2,1)} %constant.17.clone.refs_1_.refs_2_, bf16[1,2,768,256]{3,2,1,0:T(8,128)(2,1)} %constant.23.clone.refs_3_), custom_call_target="tpu_custom_call" | custom-call | flops 4000000000 | bytes 6000000 | tf_op jit(solution)/shard_map/inverse_wide/pallas_call | solution.py:390
  241.5 0.1 collective-permute-start
  241.6 1.9 differences.2
  243.6 0.5 collective-permute-done.refs_0_
  244.0 1.9 differences.3
  (6 shorter events, 0.0 us)
Async XLA Ops:
  11.1 57.9 %all-to-all-start.2 = ((f32[16,3,2,1,48,128]{5,4,3,2,1,0:T(8,128)}), f32[16,3,2,1,48,128]{5,4,3,2,1,0:T(8,128)S(1)}, u32[]{:S(2)}, u32[]{:S(2)}) async-start(f32[16,3,2,1,48,128]{5,4,3,2,1,0:T(8,128)} %bitcast.11), calls=%async_computation.2 | async-start | bytes 4718592 | tf_op jit(solution)/shard_map/all_to_all | solution.py:408
  69.0 6.7 %copy-start.2 = (s32[4,16,2]{1,2,0:T(2,128)S(1)}, s32[4,16,2]{1,2,0:T(2,128)}, u32[]{:S(2)}) copy-start(s32[4,16,2]{1,2,0:T(2,128)} %param.14) | copy-start | bytes 1540
  69.0 6.9 %copy-start = (s32[4,16]{1,0:T(4,128)S(1)}, s32[4,16]{1,0:T(4,128)}, u32[]{:S(2)}) copy-start(s32[4,16]{1,0:T(4,128)} %signs.3) | copy-start | bytes 772
  69.0 107.4 %all-to-all-start = ((f32[16,3,2,2,48,128]{5,4,3,2,1,0:T(8,128)}), f32[16,3,2,2,48,128]{5,4,3,2,1,0:T(8,128)}, u32[]{:S(2)}, u32[]{:S(2)}) async-start(f32[16,3,2,2,48,128]{5,4,3,2,1,0:T(8,128)} %bitcast.10), calls=%async_computation | async-start | bytes 9437184 | tf_op jit(solution)/shard_map/all_to_all | solution.py:408
  176.4 23.6 %all-to-all-start.3 = ((f32[16,3,24,128]{3,2,1,0:T(8,128)}), f32[16,3,24,128]{3,2,1,0:T(8,128)S(1)}, u32[]{:S(2)}, u32[]{:S(2)}) async-start(f32[16,3,24,128]{3,2,1,0:T(8,128)} %middle_narrow.1), calls=%async_computation.3 | async-start | bytes 1179648 | tf_op jit(solution)/shard_map/all_to_all | solution.py:408
  200.0 31.8 %all-to-all-start.1 = ((f32[16,3,48,128]{3,2,1,0:T(8,128)}), f32[16,3,48,128]{3,2,1,0:T(8,128)S(1)}, u32[]{:S(2)}, u32[]{:S(2)}) async-start(f32[16,3,48,128]{3,2,1,0:T(8,128)} %middle_wide.1), calls=%async_computation.1 | async-start | bytes 2359296 | tf_op jit(solution)/shard_map/all_to_all | solution.py:408
  209.8 1.2 copy-start.1
  235.4 6.2 %collective-permute-start.1 = (f32[1,3,4,18432]{3,2,1,0:T(4,128)S(1)}, f32[1,3,4,18432]{3,2,1,0:T(4,128)S(1)}, u32[]{:S(2)}, u32[]{:S(2)}) collective-permute-start(f32[1,3,4,18432]{3,2,1,0:T(4,128)S(1)} %inverse_wide.3.own), channel_id=1, source_target_pairs={{16,0},{0,16},{17,1},{1,17},{18,2},{2,18},{19,3},{3,19},{20,4},{4,... | collective-permute-start | bytes 2654216 | tf_op jit(solution)/shard_map/ppermute | solution.py:501
  241.5 2.5 %collective-permute-start = (f32[1,3,4,18432]{3,2,1,0:T(4,128)S(1)}, f32[1,3,4,18432]{3,2,1,0:T(4,128)S(1)}, u32[]{:S(2)}, u32[]{:S(2)}) collective-permute-start(f32[1,3,4,18432]{3,2,1,0:T(4,128)S(1)} %inverse_wide.2.own), channel_id=1, source_target_pairs={{16,0},{0,16},{17,1},{1,17},{18,2},{2,18},{19,3},{3,19},{20,4},{4,... | collective-permute-start | bytes 2654216 | tf_op jit(solution)/shard_map/ppermute | solution.py:501

commit v5 on v4

--- a/solution.py
+++ b/solution.py
@@ -153,7 +153,7 @@
             left = [tiles[e + k][part] for part in (0, 1, 0) for k in range(2)]
             result = dot(jnp.concatenate(left, axis=1), depth[e])
             for part in range(2):
-                spectra[group][part * 2 + e] = result[:, part * LANES : (part + 1) * LANES]
+                spectra[group][part * 2 + e, : result.shape[0]] = result[:, part * LANES : (part + 1) * LANES]
 
         def rows_of(c, group=group):
             return jnp.concatenate(
@@ -197,8 +197,8 @@
         in_specs=[spot, spot, whole(depth), whole(table), pl.BlockSpec(memory_space=pl.ANY)],
         out_specs=pl.BlockSpec((blocks, step, SUB, LANES), lambda x: (0, x, 0, 0)),
         out_shape=jax.ShapeDtypeStruct((blocks, sites, SUB, LANES), jnp.float32),
-        scratch_shapes=[pltpu.VMEM((step, blocks * SUB, LANES), jnp.float32)]
-        + [pltpu.VMEM((4, pairs_y * SUB, LANES), jnp.float32)] * (2 * step),
+        scratch_shapes=[pltpu.VMEM((step, (blocks + 2 * groups) * SUB, LANES), jnp.float32)]
+        + [pltpu.VMEM((4, (pairs_y + 1) * SUB, LANES), jnp.float32)] * (2 * step),
         compiler_params=pltpu.CompilerParams(vmem_limit_bytes=GRANT),
         cost_estimate=pl.CostEstimate(flops=8 * 10**9, bytes_accessed=12 * 10**6, transcendentals=0),
         name="forward_narrow" if narrow else "forward_wide",
@@ -295,10 +295,10 @@
         out_specs=pl.BlockSpec((devices, 1, rows, LANES), lambda r: (0, r, 0, 0)),
         out_shape=jax.ShapeDtypeStruct((devices, steps, rows, LANES), jnp.float32),
         scratch_shapes=[
-            pltpu.VMEM((groups, SUB * 2 * size, LANES), jnp.float32),
+            pltpu.VMEM((groups, (SUB + 1) * 2 * size, LANES), jnp.float32),
             pltpu.VMEM((3 * SUB, 2 * size, LANES), jnp.float32),
             pltpu.VMEM((channels, 2 * size, LANES), jnp.float32),
-            pltpu.VMEM((devices * rows, LANES), jnp.float32),
+            pltpu.VMEM((devices * rows + SUB, LANES), jnp.float32),
         ],
         compiler_params=pltpu.CompilerParams(vmem_limit_bytes=SMALL_GRANT),
         cost_estimate=pl.CostEstimate(flops=4 * 10**9, bytes_accessed=10 * 10**6, transcendentals=0),
@@ -309,8 +309,8 @@
 def inverse_kernel(narrow, arrays, devices, channels, pairs_y, *refs):
     pieces, refs = each(refs[:arrays]), refs[arrays:]
     if narrow:
-        table, depth, out, lines = refs
-        staged = partial = out
+        table, depth, out, lines, staged = refs
+        partial = out
     else:
         partial, table, depth, out, lines, staged = refs
     thirds = pieces[0].shape[0]
@@ -367,7 +367,9 @@
             zero, one = products[0][rows], products[1][rows]
             for q, value in enumerate((zero[:, :LANES], zero[:, LANES:] + one[:, :LANES], one[:, LANES:])):
                 staged[q, pl.ds(c, pairs_y, stride=channels), :] = value
-    if not narrow:
+    if narrow:
+        partial[...] = staged[:, : partial.shape[1], :]
+    else:
         for p in range(pairs_y):
             rows = slice(p * channels, (p + 1) * channels)
             for q in range(3):
@@ -383,7 +385,7 @@
     tiles = (3, size * channels, LANES)
     rows = pieces[0].shape[2] // shares
     sites = sites // shares
-    lines = pltpu.VMEM((rows * size, LANES), jnp.float32)
+    lines = pltpu.VMEM(((rows + 1) * size, LANES), jnp.float32)
     part = lambda value: pl.BlockSpec(value.shape[:2] + (rows, LANES), lambda x: (0, 0, share, 0))
     step = 3 if sites % 3 == 0 else 1
     kept = pl.BlockSpec((step,) + tiles, lambda x: (x + share * sites // step, 0, 0, 0))
@@ -393,7 +395,7 @@
         in_specs=[part(v) for v in pieces] + ([] if narrow else [kept]) + [whole(table), whole(depth)],
         out_specs=kept if narrow else pl.BlockSpec((1, step, channels, flat), lambda x: (0, x, 0, 0)),
         out_shape=jax.ShapeDtypeStruct((sites,) + tiles if narrow else (1, sites, channels, flat), jnp.float32),
-        scratch_shapes=[lines] if narrow else [lines, pltpu.VMEM((step,) + tiles, jnp.float32)],
+        scratch_shapes=[lines, pltpu.VMEM((step, 3, size * channels + SUB, LANES), jnp.float32)],
         compiler_params=pltpu.CompilerParams(vmem_limit_bytes=SMALL_GRANT),
         cost_estimate=pl.CostEstimate(flops=4 * 10**9, bytes_accessed=6 * 10**6, transcendentals=0),
         name="inverse_narrow" if narrow else "inverse_wide",

time: 247 us -> 247 us (level)
  no operation moved by 1% of the time
where the time goes in v5:
time: 247 us; the launch traced here: 246 us
  waiting for transfers between devices  150 us (61%)
  Pallas kernels  63.6 us (26%)
  starting transfers between devices  29.5 us (12%)
  local copies, waits for them, and re-layouts  2.68 us (1%)
    all_to_all x4, waiting for transfers between devices, exchange(): return [lax.all_to_all(packed, 'space', 0, 0, tiled=True)]  149 us
    all_to_all x4, starting transfers between devices, exchange(): return [lax.all_to_all(packed, 'space', 0, 0, tiled=True)]  26.8 us
    pallas_call x2, Pallas kernels, forward(): pl.pallas_call(functools.partial(forward_kernel, narrow, sites, pairs_y),...  24.9 us
    pallas_call x2, Pallas kernels, middle(): pl.pallas_call(functools.partial(middle_kernel, narrow, len(pieces), devi...  22.5 us
    pallas_call x3, Pallas kernels, inverse(): pl.pallas_call(functools.partial(inverse_kernel, narrow, len(pieces), dev...  12.3 us
  transfers between devices with their start and end apart: 6, of which 5 were waited for; matrix products, arithmetic and copies ran while one was open for 1% of the time, Pallas kernels for 19%

profile of v5, /device:TPU:9, one launch (start us, length us, event | category | flops | bytes accessed | tf_op | source)
XLA Modules:
  0.0 245.9 jit_solution(1477034710164479279)
XLA Ops:
  0.6 10.5 %forward_narrow.1 = f32[96,6,8,128]{3,2,1,0:T(8,128)} custom-call(f32[1,6,8,18432]{3,2,1,0:T(8,128)} %bitcast.16, f32[1,6,8,18432]{3,2,1,0:T(8,128)} %bitcast.18, bf16[2,768,256]{2,1,0:T(8,128)(2,1)} %constant.20.clone.depth, bf16[192,576]{1,0:T(8,128)(2,1)} %constant.16.clone.table, s32[4,16]{1,0:T(4,128)} %signs.3), custom_call_target="tpu_custom_call" | custom-call | flops 8000000000 | bytes 12000000 | tf_op jit(solution)/shard_map/forward_narrow/pallas_call | solution.py:194
  11.1 6.7 %all-to-all-start.2 = ((f32[16,3,2,1,48,128]{5,4,3,2,1,0:T(8,128)}), f32[16,3,2,1,48,128]{5,4,3,2,1,0:T(8,128)S(1)}, u32[]{:S(2)}, u32[]{:S(2)}) async-start(f32[16,3,2,1,48,128]{5,4,3,2,1,0:T(8,128)} %bitcast.11), calls=%async_computation.2 | async-start | bytes 4718592 | tf_op jit(solution)/shard_map/all_to_all | solution.py:410
  17.8 1.3 slice_bitcast_fusion.token
  19.1 14.4 %forward_wide.1 = f32[192,6,8,128]{3,2,1,0:T(8,128)} custom-call(f32[1,6,8,18432]{3,2,1,0:T(8,128)} %bitcast.17, f32[1,6,8,18432]{3,2,1,0:T(8,128)} %bitcast.19, bf16[2,768,256]{2,1,0:T(8,128)(2,1)} %constant.21.clone.depth, bf16[192,576]{1,0:T(8,128)(2,1)} %constant.16.clone.table, f32[8,128]{1,0:T(8,128)} %slice_bitcast_fusion.token), custom_call_target="tpu_custom_call" | custom-call | flops 8000000000 | bytes 12000000 | tf_op jit(solution)/shard_map/forward_wide/pallas_call | solution.py:194
  33.5 35.5 %all-to-all-done.2.refs_0_ = f32[16,3,2,1,48,128]{5,4,3,2,1,0:T(8,128)S(1)} async-done(((f32[16,3,2,1,48,128]{5,4,3,2,1,0:T(8,128)}), f32[16,3,2,1,48,128]{5,4,3,2,1,0:T(8,128)S(1)}, u32[]{:S(2)}, u32[]{:S(2)}) %all-to-all-start.2) | async-done | bytes 2359328 | tf_op jit(solution)/shard_map/all_to_all | solution.py:410
  69.0 6.7 %all-to-all-start = ((f32[16,3,2,2,48,128]{5,4,3,2,1,0:T(8,128)}), f32[16,3,2,2,48,128]{5,4,3,2,1,0:T(8,128)}, u32[]{:S(2)}, u32[]{:S(2)}) async-start(f32[16,3,2,2,48,128]{5,4,3,2,1,0:T(8,128)} %bitcast.10), calls=%async_computation | async-start | bytes 9437184 | tf_op jit(solution)/shard_map/all_to_all | solution.py:410
  75.8 0.1 copy.18
  75.8 0.1 copy.19.pairs
  75.9 10.1 %middle_narrow.1 = f32[16,3,24,128]{3,2,1,0:T(8,128)} custom-call(s32[4,32]{1,0:T(4,128)S(1)} %copy.19.pairs, s32[4,16]{1,0:T(4,128)S(1)} %copy-done, f32[16,3,2,1,48,128]{5,4,3,2,1,0:T(8,128)S(1)} %all-to-all-done.2.refs_0_, bf16[192,576]{1,0:T(8,128)(2,1)} %constant.18.clone.refs_1_, bf16[192,576]{1,0:T(8,128)(2,1)} %constant.19.clone.refs_2_), custom_call_target="tpu_custom_call" | custom-call | flops 4000000000 | bytes 10000000 | tf_op jit(solution)/shard_map/middle_narrow/pallas_call | solution.py:291
  86.0 90.4 %all-to-all-done.refs_0_ = f32[16,3,2,2,48,128]{5,4,3,2,1,0:T(8,128)} async-done(((f32[16,3,2,2,48,128]{5,4,3,2,1,0:T(8,128)}), f32[16,3,2,2,48,128]{5,4,3,2,1,0:T(8,128)}, u32[]{:S(2)}, u32[]{:S(2)}) %all-to-all-start) | async-done | bytes 4718624 | tf_op jit(solution)/shard_map/all_to_all | solution.py:410
  176.4 8.7 %all-to-all-start.3 = ((f32[16,3,24,128]{3,2,1,0:T(8,128)}), f32[16,3,24,128]{3,2,1,0:T(8,128)S(1)}, u32[]{:S(2)}, u32[]{:S(2)}) async-start(f32[16,3,24,128]{3,2,1,0:T(8,128)} %middle_narrow.1), calls=%async_computation.3 | async-start | bytes 1179648 | tf_op jit(solution)/shard_map/all_to_all | solution.py:410
  185.1 12.4 %middle_wide.1 = f32[16,3,48,128]{3,2,1,0:T(8,128)} custom-call(s32[4,32]{1,0:T(4,128)S(1)} %copy.19.pairs, s32[4,16]{1,0:T(4,128)S(1)} %copy-done, f32[16,3,2,2,48,128]{5,4,3,2,1,0:T(8,128)} %all-to-all-done.refs_0_, bf16[192,576]{1,0:T(8,128)(2,1)} %constant.18.clone.refs_1_, bf16[192,576]{1,0:T(8,128)(2,1)} %constant.19.clone.refs_2_), custom_call_target="tpu_custom_call" | custom-call | flops 4000000000 | bytes 10000000 | tf_op jit(solution)/shard_map/middle_wide/pallas_call | solution.py:291
  197.6 2.5 %all-to-all-done.3.refs_0_ = f32[16,3,24,128]{3,2,1,0:T(8,128)S(1)} async-done(((f32[16,3,24,128]{3,2,1,0:T(8,128)}), f32[16,3,24,128]{3,2,1,0:T(8,128)S(1)}, u32[]{:S(2)}, u32[]{:S(2)}) %all-to-all-start.3) | async-done | bytes 589856 | tf_op jit(solution)/shard_map/all_to_all | solution.py:410
  200.0 4.7 %all-to-all-start.1 = ((f32[16,3,48,128]{3,2,1,0:T(8,128)}), f32[16,3,48,128]{3,2,1,0:T(8,128)S(1)}, u32[]{:S(2)}, u32[]{:S(2)}) async-start(f32[16,3,48,128]{3,2,1,0:T(8,128)} %middle_wide.1), calls=%async_computation.1 | async-start | bytes 2359296 | tf_op jit(solution)/shard_map/all_to_all | solution.py:410
  204.7 5.3 %inverse_narrow.1.refs_1_ = f32[6,3,192,128]{3,2,1,0:T(8,128)S(1)} custom-call(f32[16,3,24,128]{3,2,1,0:T(8,128)S(1)} %all-to-all-done.3.refs_0_, bf16[384,288]{1,0:T(8,128)(2,1)} %constant.17.clone.refs_1_.refs_2_, bf16[2,2,768,256]{3,2,1,0:T(8,128)(2,1)} %constant.22.clone.refs_2_), custom_call_target="tpu_custom_call" | custom-call | flops 4000000000 | bytes 6000000 | tf_op jit(solution)/shard_map/inverse_narrow/pallas_call | solution.py:392
  210.0 1.2 copy-done.1
  211.2 20.6 %all-to-all-done.1.refs_0_ = f32[16,3,48,128]{3,2,1,0:T(8,128)S(1)} async-done(((f32[16,3,48,128]{3,2,1,0:T(8,128)}), f32[16,3,48,128]{3,2,1,0:T(8,128)S(1)}, u32[]{:S(2)}, u32[]{:S(2)}) %all-to-all-start.1) | async-done | bytes 1179680 | tf_op jit(solution)/shard_map/all_to_all | solution.py:410
  231.9 3.5 %inverse_wide.3.own = f32[1,3,4,18432]{3,2,1,0:T(4,128)S(1)} custom-call(f32[16,3,48,128]{3,2,1,0:T(8,128)S(1)} %all-to-all-done.1.refs_0_, f32[6,3,192,128]{3,2,1,0:T(8,128)} %copy-done.1, bf16[384,288]{1,0:T(8,128)(2,1)} %constant.17.clone.refs_1_.refs_2_, bf16[1,2,768,256]{3,2,1,0:T(8,128)(2,1)} %constant.23.clone.refs_3_), custom_call_target="tpu_custom_call" | custom-call | flops 4000000000 | bytes 6000000 | tf_op jit(solution)/shard_map/inverse_wide/pallas_call | solution.py:392
  235.4 2.6 %collective-permute-start.1 = (f32[1,3,4,18432]{3,2,1,0:T(4,128)S(1)}, f32[1,3,4,18432]{3,2,1,0:T(4,128)S(1)}, u32[]{:S(2)}, u32[]{:S(2)}) collective-permute-start(f32[1,3,4,18432]{3,2,1,0:T(4,128)S(1)} %inverse_wide.3.own), channel_id=1, source_target_pairs={{16,0},{0,16},{17,1},{1,17},{18,2},{2,18},{19,3},{3,19},{20,4},{4,... | collective-permute-start | bytes 2654216 | tf_op jit(solution)/shard_map/ppermute | solution.py:503
  238.0 3.5 %inverse_wide.2.own = f32[1,3,4,18432]{3,2,1,0:T(4,128)S(1)} custom-call(f32[16,3,48,128]{3,2,1,0:T(8,128)S(1)} %all-to-all-done.1.refs_0_, f32[6,3,192,128]{3,2,1,0:T(8,128)} %copy-done.1, bf16[384,288]{1,0:T(8,128)(2,1)} %constant.17.clone.refs_1_.refs_2_, bf16[1,2,768,256]{3,2,1,0:T(8,128)(2,1)} %constant.23.clone.refs_3_), custom_call_target="tpu_custom_call" | custom-call | flops 4000000000 | bytes 6000000 | tf_op jit(solution)/shard_map/inverse_wide/pallas_call | solution.py:392
  241.5 0.1 collective-permute-start
  241.6 1.9 differences.2
  243.6 0.5 collective-permute-done.refs_0_
  244.0 1.9 differences.3
  (6 shorter events, 0.0 us)
Async XLA Ops:
  11.1 57.9 %all-to-all-start.2 = ((f32[16,3,2,1,48,128]{5,4,3,2,1,0:T(8,128)}), f32[16,3,2,1,48,128]{5,4,3,2,1,0:T(8,128)S(1)}, u32[]{:S(2)}, u32[]{:S(2)}) async-start(f32[16,3,2,1,48,128]{5,4,3,2,1,0:T(8,128)} %bitcast.11), calls=%async_computation.2 | async-start | bytes 4718592 | tf_op jit(solution)/shard_map/all_to_all | solution.py:410
  69.0 6.7 %copy-start.2 = (s32[4,16,2]{1,2,0:T(2,128)S(1)}, s32[4,16,2]{1,2,0:T(2,128)}, u32[]{:S(2)}) copy-start(s32[4,16,2]{1,2,0:T(2,128)} %param.14) | copy-start | bytes 1540
  69.0 6.9 %copy-start = (s32[4,16]{1,0:T(4,128)S(1)}, s32[4,16]{1,0:T(4,128)}, u32[]{:S(2)}) copy-start(s32[4,16]{1,0:T(4,128)} %signs.3) | copy-start | bytes 772
  69.0 107.4 %all-to-all-start = ((f32[16,3,2,2,48,128]{5,4,3,2,1,0:T(8,128)}), f32[16,3,2,2,48,128]{5,4,3,2,1,0:T(8,128)}, u32[]{:S(2)}, u32[]{:S(2)}) async-start(f32[16,3,2,2,48,128]{5,4,3,2,1,0:T(8,128)} %bitcast.10), calls=%async_computation | async-start | bytes 9437184 | tf_op jit(solution)/shard_map/all_to_all | solution.py:410
  176.4 23.6 %all-to-all-start.3 = ((f32[16,3,24,128]{3,2,1,0:T(8,128)}), f32[16,3,24,128]{3,2,1,0:T(8,128)S(1)}, u32[]{:S(2)}, u32[]{:S(2)}) async-start(f32[16,3,24,128]{3,2,1,0:T(8,128)} %middle_narrow.1), calls=%async_computation.3 | async-start | bytes 1179648 | tf_op jit(solution)/shard_map/all_to_all | solution.py:410
  200.0 31.8 %all-to-all-start.1 = ((f32[16,3,48,128]{3,2,1,0:T(8,128)}), f32[16,3,48,128]{3,2,1,0:T(8,128)S(1)}, u32[]{:S(2)}, u32[]{:S(2)}) async-start(f32[16,3,48,128]{3,2,1,0:T(8,128)} %middle_wide.1), calls=%async_computation.1 | async-start | bytes 2359296 | tf_op jit(solution)/shard_map/all_to_all | solution.py:410
  210.0 1.2 copy-start.1
  235.4 6.2 %collective-permute-start.1 = (f32[1,3,4,18432]{3,2,1,0:T(4,128)S(1)}, f32[1,3,4,18432]{3,2,1,0:T(4,128)S(1)}, u32[]{:S(2)}, u32[]{:S(2)}) collective-permute-start(f32[1,3,4,18432]{3,2,1,0:T(4,128)S(1)} %inverse_wide.3.own), channel_id=1, source_target_pairs={{16,0},{0,16},{17,1},{1,17},{18,2},{2,18},{19,3},{3,19},{20,4},{4,... | collective-permute-start | bytes 2654216 | tf_op jit(solution)/shard_map/ppermute | solution.py:503
  241.5 2.5 %collective-permute-start = (f32[1,3,4,18432]{3,2,1,0:T(4,128)S(1)}, f32[1,3,4,18432]{3,2,1,0:T(4,128)S(1)}, u32[]{:S(2)}, u32[]{:S(2)}) collective-permute-start(f32[1,3,4,18432]{3,2,1,0:T(4,128)S(1)} %inverse_wide.2.own), channel_id=1, source_target_pairs={{16,0},{0,16},{17,1},{1,17},{18,2},{2,18},{19,3},{3,19},{20,4},{4,... | collective-permute-start | bytes 2654216 | tf_op jit(solution)/shard_map/ppermute | solution.py:503

commit v6 on v5

--- a/solution.py
+++ b/solution.py
@@ -399,7 +399,7 @@
         compiler_params=pltpu.CompilerParams(vmem_limit_bytes=SMALL_GRANT),
         cost_estimate=pl.CostEstimate(flops=4 * 10**9, bytes_accessed=6 * 10**6, transcendentals=0),
         name="inverse_narrow" if narrow else "inverse_wide",
-    )(*placed(pltpu.VMEM, *pieces), *([] if narrow else placed(pltpu.HBM, partial)), *placed(pltpu.HBM, table, depth))
+    )(*placed(pltpu.VMEM, *pieces), *([] if narrow else placed(pltpu.VMEM, partial)), *placed(pltpu.HBM if narrow else pltpu.VMEM, table, depth))
 
 
 AT_ONCE = dict(sent_narrow=True, sent_wide=True, back_narrow=True, back_wide=True)

time: 247 us -> 245 us (level)
  Pallas kernels: 63.6 us -> 60.4 us
    pallas_call x3, Pallas kernels: 12.3 us -> 9.2 us  [inverse(): pl.pallas_call(functools.partial(inverse_kernel, narrow, len(pieces), dev...]
  transfers between devices with their start and end apart: 6 -> 6, of which waited for: 5 -> 6; matrix products, arithmetic and copies ran while one was open for 1% -> 1% of each run, Pallas kernels for 19% -> 19%
where the time goes in v6:
time: 245 us; the launch traced here: 244 us
  waiting for transfers between devices  149 us (61%)
  Pallas kernels  60.4 us (25%)
  starting transfers between devices  29.5 us (12%)
  local copies, waits for them, and re-layouts  4.18 us (2%)
    all_to_all x4, waiting for transfers between devices, exchange(): return [lax.all_to_all(packed, 'space', 0, 0, tiled=True)]  149 us
    all_to_all x4, starting transfers between devices, exchange(): return [lax.all_to_all(packed, 'space', 0, 0, tiled=True)]  26.8 us
    pallas_call x2, Pallas kernels, forward(): pl.pallas_call(functools.partial(forward_kernel, narrow, sites, pairs_y),...  24.9 us
    pallas_call x2, Pallas kernels, middle(): pl.pallas_call(functools.partial(middle_kernel, narrow, len(pieces), devi...  22.5 us
    pallas_call x3, Pallas kernels, inverse(): pl.pallas_call(functools.partial(inverse_kernel, narrow, len(pieces), dev...  9.2 us
  transfers between devices with their start and end apart: 6, of which 6 were waited for; matrix products, arithmetic and copies ran while one was open for 1% of the time, Pallas kernels for 19%

profile of v6, /device:TPU:9, one launch (start us, length us, event | category | flops | bytes accessed | tf_op | source)
XLA Modules:
  0.0 244.2 jit_solution(5324012780204993508)
XLA Ops:
  0.6 10.5 %forward_narrow.1 = f32[96,6,8,128]{3,2,1,0:T(8,128)} custom-call(f32[1,6,8,18432]{3,2,1,0:T(8,128)} %bitcast.16, f32[1,6,8,18432]{3,2,1,0:T(8,128)} %bitcast.18, bf16[2,768,256]{2,1,0:T(8,128)(2,1)} %constant.20.clone.depth, bf16[192,576]{1,0:T(8,128)(2,1)} %constant.16.clone.table, s32[4,16]{1,0:T(4,128)} %signs.3), custom_call_target="tpu_custom_call" | custom-call | flops 8000000000 | bytes 12000000 | tf_op jit(solution)/shard_map/forward_narrow/pallas_call | solution.py:194
  11.1 6.7 %all-to-all-start.2 = ((f32[16,3,2,1,48,128]{5,4,3,2,1,0:T(8,128)}), f32[16,3,2,1,48,128]{5,4,3,2,1,0:T(8,128)S(1)}, u32[]{:S(2)}, u32[]{:S(2)}) async-start(f32[16,3,2,1,48,128]{5,4,3,2,1,0:T(8,128)} %bitcast.11), calls=%async_computation.2 | async-start | bytes 4718592 | tf_op jit(solution)/shard_map/all_to_all | solution.py:410
  17.8 1.3 slice_bitcast_fusion.token
  19.1 14.4 %forward_wide.1 = f32[192,6,8,128]{3,2,1,0:T(8,128)} custom-call(f32[1,6,8,18432]{3,2,1,0:T(8,128)} %bitcast.17, f32[1,6,8,18432]{3,2,1,0:T(8,128)} %bitcast.19, bf16[2,768,256]{2,1,0:T(8,128)(2,1)} %constant.21.clone.depth, bf16[192,576]{1,0:T(8,128)(2,1)} %constant.16.clone.table, f32[8,128]{1,0:T(8,128)} %slice_bitcast_fusion.token), custom_call_target="tpu_custom_call" | custom-call | flops 8000000000 | bytes 12000000 | tf_op jit(solution)/shard_map/forward_wide/pallas_call | solution.py:194
  33.5 35.5 %all-to-all-done.2.refs_0_ = f32[16,3,2,1,48,128]{5,4,3,2,1,0:T(8,128)S(1)} async-done(((f32[16,3,2,1,48,128]{5,4,3,2,1,0:T(8,128)}), f32[16,3,2,1,48,128]{5,4,3,2,1,0:T(8,128)S(1)}, u32[]{:S(2)}, u32[]{:S(2)}) %all-to-all-start.2) | async-done | bytes 2359328 | tf_op jit(solution)/shard_map/all_to_all | solution.py:410
  69.0 6.7 %all-to-all-start = ((f32[16,3,2,2,48,128]{5,4,3,2,1,0:T(8,128)}), f32[16,3,2,2,48,128]{5,4,3,2,1,0:T(8,128)}, u32[]{:S(2)}, u32[]{:S(2)}) async-start(f32[16,3,2,2,48,128]{5,4,3,2,1,0:T(8,128)} %bitcast.10), calls=%async_computation | async-start | bytes 9437184 | tf_op jit(solution)/shard_map/all_to_all | solution.py:410
  75.8 0.1 copy.18
  75.8 0.1 copy.19.pairs
  75.9 10.1 %middle_narrow.1 = f32[16,3,24,128]{3,2,1,0:T(8,128)} custom-call(s32[4,32]{1,0:T(4,128)S(1)} %copy.19.pairs, s32[4,16]{1,0:T(4,128)S(1)} %copy-done, f32[16,3,2,1,48,128]{5,4,3,2,1,0:T(8,128)S(1)} %all-to-all-done.2.refs_0_, bf16[192,576]{1,0:T(8,128)(2,1)} %constant.18.clone.refs_1_, bf16[192,576]{1,0:T(8,128)(2,1)} %constant.19.clone.refs_2_), custom_call_target="tpu_custom_call" | custom-call | flops 4000000000 | bytes 10000000 | tf_op jit(solution)/shard_map/middle_narrow/pallas_call | solution.py:291
  86.0 90.4 %all-to-all-done.refs_0_ = f32[16,3,2,2,48,128]{5,4,3,2,1,0:T(8,128)} async-done(((f32[16,3,2,2,48,128]{5,4,3,2,1,0:T(8,128)}), f32[16,3,2,2,48,128]{5,4,3,2,1,0:T(8,128)}, u32[]{:S(2)}, u32[]{:S(2)}) %all-to-all-start) | async-done | bytes 4718624 | tf_op jit(solution)/shard_map/all_to_all | solution.py:410
  176.4 8.7 %all-to-all-start.3 = ((f32[16,3,24,128]{3,2,1,0:T(8,128)}), f32[16,3,24,128]{3,2,1,0:T(8,128)S(1)}, u32[]{:S(2)}, u32[]{:S(2)}) async-start(f32[16,3,24,128]{3,2,1,0:T(8,128)} %middle_narrow.1), calls=%async_computation.3 | async-start | bytes 1179648 | tf_op jit(solution)/shard_map/all_to_all | solution.py:410
  185.1 12.4 %middle_wide.1 = f32[16,3,48,128]{3,2,1,0:T(8,128)} custom-call(s32[4,32]{1,0:T(4,128)S(1)} %copy.19.pairs, s32[4,16]{1,0:T(4,128)S(1)} %copy-done, f32[16,3,2,2,48,128]{5,4,3,2,1,0:T(8,128)} %all-to-all-done.refs_0_, bf16[192,576]{1,0:T(8,128)(2,1)} %constant.18.clone.refs_1_, bf16[192,576]{1,0:T(8,128)(2,1)} %constant.19.clone.refs_2_), custom_call_target="tpu_custom_call" | custom-call | flops 4000000000 | bytes 10000000 | tf_op jit(solution)/shard_map/middle_wide/pallas_call | solution.py:291
  197.6 2.5 %all-to-all-done.3.refs_0_ = f32[16,3,24,128]{3,2,1,0:T(8,128)S(1)} async-done(((f32[16,3,24,128]{3,2,1,0:T(8,128)}), f32[16,3,24,128]{3,2,1,0:T(8,128)S(1)}, u32[]{:S(2)}, u32[]{:S(2)}) %all-to-all-start.3) | async-done | bytes 589856 | tf_op jit(solution)/shard_map/all_to_all | solution.py:410
  200.0 4.7 %all-to-all-start.1 = ((f32[16,3,48,128]{3,2,1,0:T(8,128)}), f32[16,3,48,128]{3,2,1,0:T(8,128)S(1)}, u32[]{:S(2)}, u32[]{:S(2)}) async-start(f32[16,3,48,128]{3,2,1,0:T(8,128)} %middle_wide.1), calls=%async_computation.1 | async-start | bytes 2359296 | tf_op jit(solution)/shard_map/all_to_all | solution.py:410
  204.7 5.4 %inverse_narrow.1.refs_1_ = f32[6,3,192,128]{3,2,1,0:T(8,128)S(1)} custom-call(f32[16,3,24,128]{3,2,1,0:T(8,128)S(1)} %all-to-all-done.3.refs_0_, bf16[384,288]{1,0:T(8,128)(2,1)} %constant.17.clone.refs_1_.refs_2_, bf16[2,2,768,256]{3,2,1,0:T(8,128)(2,1)} %constant.22.clone.refs_2_), custom_call_target="tpu_custom_call" | custom-call | flops 4000000000 | bytes 6000000 | tf_op jit(solution)/shard_map/inverse_narrow/pallas_call | solution.py:392
  210.1 1.2 copy-done.3
  211.3 20.6 %all-to-all-done.1.refs_0_ = f32[16,3,48,128]{3,2,1,0:T(8,128)S(1)} async-done(((f32[16,3,48,128]{3,2,1,0:T(8,128)}), f32[16,3,48,128]{3,2,1,0:T(8,128)S(1)}, u32[]{:S(2)}, u32[]{:S(2)}) %all-to-all-start.1) | async-done | bytes 1179680 | tf_op jit(solution)/shard_map/all_to_all | solution.py:410
  231.9 1.5 copy-done.4
  233.3 1.9 inverse_wide.3.own
  235.2 2.6 %collective-permute-start.1 = (f32[1,3,4,18432]{3,2,1,0:T(4,128)S(1)}, f32[1,3,4,18432]{3,2,1,0:T(4,128)S(1)}, u32[]{:S(2)}, u32[]{:S(2)}) collective-permute-start(f32[1,3,4,18432]{3,2,1,0:T(4,128)S(1)} %inverse_wide.3.own), channel_id=1, source_target_pairs={{16,0},{0,16},{17,1},{1,17},{18,2},{2,18},{19,3},{3,19},{20,4},{4,... | collective-permute-start | bytes 2654216 | tf_op jit(solution)/shard_map/ppermute | solution.py:503
  237.9 1.9 inverse_wide.2.own
  239.9 1.9 differences.2
  241.8 0.4 collective-permute-done.refs_0_
  242.3 1.9 differences.3
  (12 shorter events, 0.1 us)
Async XLA Ops:
  11.1 57.9 %all-to-all-start.2 = ((f32[16,3,2,1,48,128]{5,4,3,2,1,0:T(8,128)}), f32[16,3,2,1,48,128]{5,4,3,2,1,0:T(8,128)S(1)}, u32[]{:S(2)}, u32[]{:S(2)}) async-start(f32[16,3,2,1,48,128]{5,4,3,2,1,0:T(8,128)} %bitcast.11), calls=%async_computation.2 | async-start | bytes 4718592 | tf_op jit(solution)/shard_map/all_to_all | solution.py:410
  69.0 6.7 %copy-start.5 = (s32[4,16,2]{1,2,0:T(2,128)S(1)}, s32[4,16,2]{1,2,0:T(2,128)}, u32[]{:S(2)}) copy-start(s32[4,16,2]{1,2,0:T(2,128)} %param.14) | copy-start | bytes 1540
  69.0 6.9 %copy-start = (s32[4,16]{1,0:T(4,128)S(1)}, s32[4,16]{1,0:T(4,128)}, u32[]{:S(2)}) copy-start(s32[4,16]{1,0:T(4,128)} %signs.3) | copy-start | bytes 772
  69.0 107.4 %all-to-all-start = ((f32[16,3,2,2,48,128]{5,4,3,2,1,0:T(8,128)}), f32[16,3,2,2,48,128]{5,4,3,2,1,0:T(8,128)}, u32[]{:S(2)}, u32[]{:S(2)}) async-start(f32[16,3,2,2,48,128]{5,4,3,2,1,0:T(8,128)} %bitcast.10), calls=%async_computation | async-start | bytes 9437184 | tf_op jit(solution)/shard_map/all_to_all | solution.py:410
  176.4 23.6 %all-to-all-start.3 = ((f32[16,3,24,128]{3,2,1,0:T(8,128)}), f32[16,3,24,128]{3,2,1,0:T(8,128)S(1)}, u32[]{:S(2)}, u32[]{:S(2)}) async-start(f32[16,3,24,128]{3,2,1,0:T(8,128)} %middle_narrow.1), calls=%async_computation.3 | async-start | bytes 1179648 | tf_op jit(solution)/shard_map/all_to_all | solution.py:410
  200.0 31.8 %all-to-all-start.1 = ((f32[16,3,48,128]{3,2,1,0:T(8,128)}), f32[16,3,48,128]{3,2,1,0:T(8,128)S(1)}, u32[]{:S(2)}, u32[]{:S(2)}) async-start(f32[16,3,48,128]{3,2,1,0:T(8,128)} %middle_wide.1), calls=%async_computation.1 | async-start | bytes 2359296 | tf_op jit(solution)/shard_map/all_to_all | solution.py:410
  204.7 27.2 %copy-start.1 = (bf16[1,2,768,256]{3,2,1,0:T(8,128)(2,1)S(1)}, bf16[1,2,768,256]{3,2,1,0:T(8,128)(2,1)}, u32[]{:S(2)}) copy-start(bf16[1,2,768,256]{3,2,1,0:T(8,128)(2,1)} %constant.23.clone.refs_3_) | copy-start | bytes 2359300
  204.7 27.2 %copy-start.2 = (bf16[384,288]{1,0:T(8,128)(2,1)S(1)}, bf16[384,288]{1,0:T(8,128)(2,1)}, u32[]{:S(2)}) copy-start(bf16[384,288]{1,0:T(8,128)(2,1)} %constant.17.clone.refs_1_.refs_2_) | copy-start | bytes 663556
  210.1 1.2 copy-start.3
  231.9 1.5 copy-start.4
  235.2 4.7 %collective-permute-start.1 = (f32[1,3,4,18432]{3,2,1,0:T(4,128)S(1)}, f32[1,3,4,18432]{3,2,1,0:T(4,128)S(1)}, u32[]{:S(2)}, u32[]{:S(2)}) collective-permute-start(f32[1,3,4,18432]{3,2,1,0:T(4,128)S(1)} %inverse_wide.3.own), channel_id=1, source_target_pairs={{16,0},{0,16},{17,1},{1,17},{18,2},{2,18},{19,3},{3,19},{20,4},{4,... | collective-permute-start | bytes 2654216 | tf_op jit(solution)/shard_map/ppermute | solution.py:503
  239.8 2.5 %collective-permute-start = (f32[1,3,4,18432]{3,2,1,0:T(4,128)S(1)}, f32[1,3,4,18432]{3,2,1,0:T(4,128)S(1)}, u32[]{:S(2)}, u32[]{:S(2)}) collective-permute-start(f32[1,3,4,18432]{3,2,1,0:T(4,128)S(1)} %inverse_wide.2.own), channel_id=1, source_target_pairs={{16,0},{0,16},{17,1},{1,17},{18,2},{2,18},{19,3},{3,19},{20,4},{4,... | collective-permute-start | bytes 2654216 | tf_op jit(solution)/shard_map/ppermute | solution.py:503

commit v7 on v6

--- a/solution.py
+++ b/solution.py
@@ -106,7 +106,7 @@
         matrix = np.block([[cos[k] * keep, sin[k] * keep], [-sin[k] * keep, cos[k] * keep]])
         gap = np.zeros((matrix.shape[0], 2 * LANES - 2 * length))
         both = (np.concatenate([matrix, gap], axis=1), np.concatenate([gap, matrix], axis=1))
-        out.append(np.stack([right_table(b) for b in both]))
+        out.append(np.stack([np.concatenate(halves(b)) for b in both]))
     return np.stack(out)
 
 
@@ -361,7 +361,9 @@
         products = []
         for e in range(2):
             left = [jnp.concatenate([rows_of(value, e, c) for c in members], axis=0) for value in (high, low)]
-            products.append(dot(jnp.concatenate([left[0], left[1], left[0]], axis=1), depth[k, e]))
+            high_rows, low_rows = depth[k, e, : 2 * LANES], depth[k, e, 2 * LANES :]
+            right = jnp.concatenate([high_rows, high_rows, low_rows], axis=0)
+            products.append(dot(jnp.concatenate([left[0], left[1], left[0]], axis=1), right))
         for i, c in enumerate(members):
             rows = slice(i * pairs_y, (i + 1) * pairs_y)
             zero, one = products[0][rows], products[1][rows]

time: 245 us -> 245 us (level)
  transfers between devices with their start and end apart: 6 -> 6, of which waited for: 6 -> 5; matrix products, arithmetic and copies ran while one was open for 1% -> 1% of each run, Pallas kernels for 19% -> 19%
where the time goes in v7:
time: 245 us; the launch traced here: 244 us
  waiting for transfers between devices  150 us (61%)
  Pallas kernels  60.3 us (25%)
  starting transfers between devices  29.5 us (12%)
  local copies, waits for them, and re-layouts  4.18 us (2%)
    all_to_all x4, waiting for transfers between devices, exchange(): return [lax.all_to_all(packed, 'space', 0, 0, tiled=True)]  149 us
    all_to_all x4, starting transfers between devices, exchange(): return [lax.all_to_all(packed, 'space', 0, 0, tiled=True)]  26.8 us
    pallas_call x2, Pallas kernels, forward(): pl.pallas_call(functools.partial(forward_kernel, narrow, sites, pairs_y),...  24.9 us
    pallas_call x2, Pallas kernels, middle(): pl.pallas_call(functools.partial(middle_kernel, narrow, len(pieces), devi...  22.5 us
    pallas_call x3, Pallas kernels, inverse(): pl.pallas_call(functools.partial(inverse_kernel, narrow, len(pieces), dev...  9.04 us
  transfers between devices with their start and end apart: 6, of which 5 were waited for; matrix products, arithmetic and copies ran while one was open for 1% of the time, Pallas kernels for 19%

profile of v7, /device:TPU:9, one launch (start us, length us, event | category | flops | bytes accessed | tf_op | source)
XLA Modules:
  0.0 244.2 jit_solution(3864749161571860836)
XLA Ops:
  0.6 10.5 %forward_narrow.1 = f32[96,6,8,128]{3,2,1,0:T(8,128)} custom-call(f32[1,6,8,18432]{3,2,1,0:T(8,128)} %bitcast.16, f32[1,6,8,18432]{3,2,1,0:T(8,128)} %bitcast.18, bf16[2,768,256]{2,1,0:T(8,128)(2,1)} %constant.20.clone.depth, bf16[192,576]{1,0:T(8,128)(2,1)} %constant.16.clone.table, s32[4,16]{1,0:T(4,128)} %signs.3), custom_call_target="tpu_custom_call" | custom-call | flops 8000000000 | bytes 12000000 | tf_op jit(solution)/shard_map/forward_narrow/pallas_call | solution.py:194
  11.1 6.7 %all-to-all-start.2 = ((f32[16,3,2,1,48,128]{5,4,3,2,1,0:T(8,128)}), f32[16,3,2,1,48,128]{5,4,3,2,1,0:T(8,128)S(1)}, u32[]{:S(2)}, u32[]{:S(2)}) async-start(f32[16,3,2,1,48,128]{5,4,3,2,1,0:T(8,128)} %bitcast.11), calls=%async_computation.2 | async-start | bytes 4718592 | tf_op jit(solution)/shard_map/all_to_all | solution.py:412
  17.8 1.3 slice_bitcast_fusion.token
  19.1 14.4 %forward_wide.1 = f32[192,6,8,128]{3,2,1,0:T(8,128)} custom-call(f32[1,6,8,18432]{3,2,1,0:T(8,128)} %bitcast.17, f32[1,6,8,18432]{3,2,1,0:T(8,128)} %bitcast.19, bf16[2,768,256]{2,1,0:T(8,128)(2,1)} %constant.21.clone.depth, bf16[192,576]{1,0:T(8,128)(2,1)} %constant.16.clone.table, f32[8,128]{1,0:T(8,128)} %slice_bitcast_fusion.token), custom_call_target="tpu_custom_call" | custom-call | flops 8000000000 | bytes 12000000 | tf_op jit(solution)/shard_map/forward_wide/pallas_call | solution.py:194
  33.5 35.5 %all-to-all-done.2.refs_0_ = f32[16,3,2,1,48,128]{5,4,3,2,1,0:T(8,128)S(1)} async-done(((f32[16,3,2,1,48,128]{5,4,3,2,1,0:T(8,128)}), f32[16,3,2,1,48,128]{5,4,3,2,1,0:T(8,128)S(1)}, u32[]{:S(2)}, u32[]{:S(2)}) %all-to-all-start.2) | async-done | bytes 2359328 | tf_op jit(solution)/shard_map/all_to_all | solution.py:412
  69.0 6.7 %all-to-all-start = ((f32[16,3,2,2,48,128]{5,4,3,2,1,0:T(8,128)}), f32[16,3,2,2,48,128]{5,4,3,2,1,0:T(8,128)}, u32[]{:S(2)}, u32[]{:S(2)}) async-start(f32[16,3,2,2,48,128]{5,4,3,2,1,0:T(8,128)} %bitcast.10), calls=%async_computation | async-start | bytes 9437184 | tf_op jit(solution)/shard_map/all_to_all | solution.py:412
  75.8 0.1 copy.18
  75.9 10.1 %middle_narrow.1 = f32[16,3,24,128]{3,2,1,0:T(8,128)} custom-call(s32[4,32]{1,0:T(4,128)S(1)} %copy.19.pairs, s32[4,16]{1,0:T(4,128)S(1)} %copy-done, f32[16,3,2,1,48,128]{5,4,3,2,1,0:T(8,128)S(1)} %all-to-all-done.2.refs_0_, bf16[192,576]{1,0:T(8,128)(2,1)} %constant.18.clone.refs_1_, bf16[192,576]{1,0:T(8,128)(2,1)} %constant.19.clone.refs_2_), custom_call_target="tpu_custom_call" | custom-call | flops 4000000000 | bytes 10000000 | tf_op jit(solution)/shard_map/middle_narrow/pallas_call | solution.py:291
  86.0 90.4 %all-to-all-done.refs_0_ = f32[16,3,2,2,48,128]{5,4,3,2,1,0:T(8,128)} async-done(((f32[16,3,2,2,48,128]{5,4,3,2,1,0:T(8,128)}), f32[16,3,2,2,48,128]{5,4,3,2,1,0:T(8,128)}, u32[]{:S(2)}, u32[]{:S(2)}) %all-to-all-start) | async-done | bytes 4718624 | tf_op jit(solution)/shard_map/all_to_all | solution.py:412
  176.4 8.7 %all-to-all-start.3 = ((f32[16,3,24,128]{3,2,1,0:T(8,128)}), f32[16,3,24,128]{3,2,1,0:T(8,128)S(1)}, u32[]{:S(2)}, u32[]{:S(2)}) async-start(f32[16,3,24,128]{3,2,1,0:T(8,128)} %middle_narrow.1), calls=%async_computation.3 | async-start | bytes 1179648 | tf_op jit(solution)/shard_map/all_to_all | solution.py:412
  185.1 12.4 %middle_wide.1 = f32[16,3,48,128]{3,2,1,0:T(8,128)} custom-call(s32[4,32]{1,0:T(4,128)S(1)} %copy.19.pairs, s32[4,16]{1,0:T(4,128)S(1)} %copy-done, f32[16,3,2,2,48,128]{5,4,3,2,1,0:T(8,128)} %all-to-all-done.refs_0_, bf16[192,576]{1,0:T(8,128)(2,1)} %constant.18.clone.refs_1_, bf16[192,576]{1,0:T(8,128)(2,1)} %constant.19.clone.refs_2_), custom_call_target="tpu_custom_call" | custom-call | flops 4000000000 | bytes 10000000 | tf_op jit(solution)/shard_map/middle_wide/pallas_call | solution.py:291
  197.6 2.5 %all-to-all-done.3.refs_0_ = f32[16,3,24,128]{3,2,1,0:T(8,128)S(1)} async-done(((f32[16,3,24,128]{3,2,1,0:T(8,128)}), f32[16,3,24,128]{3,2,1,0:T(8,128)S(1)}, u32[]{:S(2)}, u32[]{:S(2)}) %all-to-all-start.3) | async-done | bytes 589856 | tf_op jit(solution)/shard_map/all_to_all | solution.py:412
  200.0 4.7 %all-to-all-start.1 = ((f32[16,3,48,128]{3,2,1,0:T(8,128)}), f32[16,3,48,128]{3,2,1,0:T(8,128)S(1)}, u32[]{:S(2)}, u32[]{:S(2)}) async-start(f32[16,3,48,128]{3,2,1,0:T(8,128)} %middle_wide.1), calls=%async_computation.1 | async-start | bytes 2359296 | tf_op jit(solution)/shard_map/all_to_all | solution.py:412
  204.7 5.2 %inverse_narrow.1.refs_1_ = f32[6,3,192,128]{3,2,1,0:T(8,128)S(1)} custom-call(f32[16,3,24,128]{3,2,1,0:T(8,128)S(1)} %all-to-all-done.3.refs_0_, bf16[384,288]{1,0:T(8,128)(2,1)} %constant.17.clone.refs_1_.refs_2_, bf16[2,2,512,256]{3,2,1,0:T(8,128)(2,1)} %constant.22.clone.refs_2_), custom_call_target="tpu_custom_call" | custom-call | flops 4000000000 | bytes 6000000 | tf_op jit(solution)/shard_map/inverse_narrow/pallas_call | solution.py:394
  209.9 1.2 copy-done.3
  211.1 20.7 %all-to-all-done.1.refs_0_ = f32[16,3,48,128]{3,2,1,0:T(8,128)S(1)} async-done(((f32[16,3,48,128]{3,2,1,0:T(8,128)}), f32[16,3,48,128]{3,2,1,0:T(8,128)S(1)}, u32[]{:S(2)}, u32[]{:S(2)}) %all-to-all-start.1) | async-done | bytes 1179680 | tf_op jit(solution)/shard_map/all_to_all | solution.py:412
  231.9 1.5 copy-done.4
  233.3 1.9 inverse_wide.3.own
  235.3 2.6 %collective-permute-start.1 = (f32[1,3,4,18432]{3,2,1,0:T(4,128)S(1)}, f32[1,3,4,18432]{3,2,1,0:T(4,128)S(1)}, u32[]{:S(2)}, u32[]{:S(2)}) collective-permute-start(f32[1,3,4,18432]{3,2,1,0:T(4,128)S(1)} %inverse_wide.3.own), channel_id=1, source_target_pairs={{16,0},{0,16},{17,1},{1,17},{18,2},{2,18},{19,3},{3,19},{20,4},{4,... | collective-permute-start | bytes 2654216 | tf_op jit(solution)/shard_map/ppermute | solution.py:505
  237.9 1.9 inverse_wide.2.own
  239.8 0.1 collective-permute-start
  239.9 1.9 differences.2
  241.8 0.5 collective-permute-done.refs_0_
  242.3 1.9 differences.3
  (12 shorter events, 0.1 us)
Async XLA Ops:
  11.1 57.9 %all-to-all-start.2 = ((f32[16,3,2,1,48,128]{5,4,3,2,1,0:T(8,128)}), f32[16,3,2,1,48,128]{5,4,3,2,1,0:T(8,128)S(1)}, u32[]{:S(2)}, u32[]{:S(2)}) async-start(f32[16,3,2,1,48,128]{5,4,3,2,1,0:T(8,128)} %bitcast.11), calls=%async_computation.2 | async-start | bytes 4718592 | tf_op jit(solution)/shard_map/all_to_all | solution.py:412
  69.0 6.7 %copy-start.5 = (s32[4,16,2]{1,2,0:T(2,128)S(1)}, s32[4,16,2]{1,2,0:T(2,128)}, u32[]{:S(2)}) copy-start(s32[4,16,2]{1,2,0:T(2,128)} %param.14) | copy-start | bytes 1540
  69.0 6.9 %copy-start = (s32[4,16]{1,0:T(4,128)S(1)}, s32[4,16]{1,0:T(4,128)}, u32[]{:S(2)}) copy-start(s32[4,16]{1,0:T(4,128)} %signs.3) | copy-start | bytes 772
  69.0 107.4 %all-to-all-start = ((f32[16,3,2,2,48,128]{5,4,3,2,1,0:T(8,128)}), f32[16,3,2,2,48,128]{5,4,3,2,1,0:T(8,128)}, u32[]{:S(2)}, u32[]{:S(2)}) async-start(f32[16,3,2,2,48,128]{5,4,3,2,1,0:T(8,128)} %bitcast.10), calls=%async_computation | async-start | bytes 9437184 | tf_op jit(solution)/shard_map/all_to_all | solution.py:412
  176.4 23.6 %all-to-all-start.3 = ((f32[16,3,24,128]{3,2,1,0:T(8,128)}), f32[16,3,24,128]{3,2,1,0:T(8,128)S(1)}, u32[]{:S(2)}, u32[]{:S(2)}) async-start(f32[16,3,24,128]{3,2,1,0:T(8,128)} %middle_narrow.1), calls=%async_computation.3 | async-start | bytes 1179648 | tf_op jit(solution)/shard_map/all_to_all | solution.py:412
  200.0 31.8 %all-to-all-start.1 = ((f32[16,3,48,128]{3,2,1,0:T(8,128)}), f32[16,3,48,128]{3,2,1,0:T(8,128)S(1)}, u32[]{:S(2)}, u32[]{:S(2)}) async-start(f32[16,3,48,128]{3,2,1,0:T(8,128)} %middle_wide.1), calls=%async_computation.1 | async-start | bytes 2359296 | tf_op jit(solution)/shard_map/all_to_all | solution.py:412
  204.7 27.2 %copy-start.1 = (bf16[1,2,512,256]{3,2,1,0:T(8,128)(2,1)S(1)}, bf16[1,2,512,256]{3,2,1,0:T(8,128)(2,1)}, u32[]{:S(2)}) copy-start(bf16[1,2,512,256]{3,2,1,0:T(8,128)(2,1)} %constant.23.clone.refs_3_) | copy-start | bytes 1572868
  204.7 27.2 %copy-start.2 = (bf16[384,288]{1,0:T(8,128)(2,1)S(1)}, bf16[384,288]{1,0:T(8,128)(2,1)}, u32[]{:S(2)}) copy-start(bf16[384,288]{1,0:T(8,128)(2,1)} %constant.17.clone.refs_1_.refs_2_) | copy-start | bytes 663556
  209.9 1.2 copy-start.3
  231.9 1.5 copy-start.4
  235.3 4.7 %collective-permute-start.1 = (f32[1,3,4,18432]{3,2,1,0:T(4,128)S(1)}, f32[1,3,4,18432]{3,2,1,0:T(4,128)S(1)}, u32[]{:S(2)}, u32[]{:S(2)}) collective-permute-start(f32[1,3,4,18432]{3,2,1,0:T(4,128)S(1)} %inverse_wide.3.own), channel_id=1, source_target_pairs={{16,0},{0,16},{17,1},{1,17},{18,2},{2,18},{19,3},{3,19},{20,4},{4,... | collective-permute-start | bytes 2654216 | tf_op jit(solution)/shard_map/ppermute | solution.py:505
  239.8 2.5 %collective-permute-start = (f32[1,3,4,18432]{3,2,1,0:T(4,128)S(1)}, f32[1,3,4,18432]{3,2,1,0:T(4,128)S(1)}, u32[]{:S(2)}, u32[]{:S(2)}) collective-permute-start(f32[1,3,4,18432]{3,2,1,0:T(4,128)S(1)} %inverse_wide.2.own), channel_id=1, source_target_pairs={{16,0},{0,16},{17,1},{1,17},{18,2},{2,18},{19,3},{3,19},{20,4},{4,... | collective-permute-start | bytes 2654216 | tf_op jit(solution)/shard_map/ppermute | solution.py:505

commit v8 on v7

--- a/solution.py
+++ b/solution.py
@@ -94,7 +94,7 @@
     matrix = np.block([[cos[:, k], -sin[:, k]], [sin[:, k], cos[:, k]]])
     gap = np.zeros((2 * LANES - 2 * length, 2 * LANES))
     both = np.stack([np.concatenate([matrix, gap]), np.concatenate([gap, matrix])])
-    return np.stack([right_table(b) for b in both])
+    return np.stack([np.concatenate(halves(b)) for b in both])
 
 
 def depth_inverse(length, first, count, halves_of):
@@ -151,7 +151,8 @@
         tiles = [split(tile) for tile in tiles]
         for e in range(2):
             left = [tiles[e + k][part] for part in (0, 1, 0) for k in range(2)]
-            result = dot(jnp.concatenate(left, axis=1), depth[e])
+            high_rows, low_rows = depth[e, : 2 * LANES], depth[e, 2 * LANES :]
+            result = dot(jnp.concatenate(left, axis=1), jnp.concatenate([high_rows, high_rows, low_rows], axis=0))
             for part in range(2):
                 spectra[group][part * 2 + e, : result.shape[0]] = result[:, part * LANES : (part + 1) * LANES]
 

time: 245 us -> 245 us (level)
  no operation moved by 1% of the time
where the time goes in v8:
time: 245 us; the launch traced here: 244 us
  waiting for transfers between devices  150 us (61%)
  Pallas kernels  60.2 us (25%)
  starting transfers between devices  29.5 us (12%)
  local copies, waits for them, and re-layouts  4.18 us (2%)
    all_to_all x4, waiting for transfers between devices, exchange(): return [lax.all_to_all(packed, 'space', 0, 0, tiled=True)]  149 us
    all_to_all x4, starting transfers between devices, exchange(): return [lax.all_to_all(packed, 'space', 0, 0, tiled=True)]  26.8 us
    pallas_call x2, Pallas kernels, forward(): pl.pallas_call(functools.partial(forward_kernel, narrow, sites, pairs_y),...  24.8 us
    pallas_call x2, Pallas kernels, middle(): pl.pallas_call(functools.partial(middle_kernel, narrow, len(pieces), devi...  22.5 us
    pallas_call x3, Pallas kernels, inverse(): pl.pallas_call(functools.partial(inverse_kernel, narrow, len(pieces), dev...  9.04 us
  transfers between devices with their start and end apart: 6, of which 5 were waited for; matrix products, arithmetic and copies ran while one was open for 1% of the time, Pallas kernels for 19%

profile of v8, /device:TPU:9, one launch (start us, length us, event | category | flops | bytes accessed | tf_op | source)
XLA Modules:
  0.0 244.1 jit_solution(18346934283349193963)
XLA Ops:
  0.6 10.4 %forward_narrow.1 = f32[96,6,8,128]{3,2,1,0:T(8,128)} custom-call(f32[1,6,8,18432]{3,2,1,0:T(8,128)} %bitcast.16, f32[1,6,8,18432]{3,2,1,0:T(8,128)} %bitcast.18, bf16[2,512,256]{2,1,0:T(8,128)(2,1)} %constant.20.clone.depth, bf16[192,576]{1,0:T(8,128)(2,1)} %constant.16.clone.table, s32[4,16]{1,0:T(4,128)} %signs.3), custom_call_target="tpu_custom_call" | custom-call | flops 8000000000 | bytes 12000000 | tf_op jit(solution)/shard_map/forward_narrow/pallas_call | solution.py:195
  11.0 6.7 %all-to-all-start.2 = ((f32[16,3,2,1,48,128]{5,4,3,2,1,0:T(8,128)}), f32[16,3,2,1,48,128]{5,4,3,2,1,0:T(8,128)S(1)}, u32[]{:S(2)}, u32[]{:S(2)}) async-start(f32[16,3,2,1,48,128]{5,4,3,2,1,0:T(8,128)} %bitcast.11), calls=%async_computation.2 | async-start | bytes 4718592 | tf_op jit(solution)/shard_map/all_to_all | solution.py:413
  17.7 1.3 slice_bitcast_fusion.token
  19.0 14.4 %forward_wide.1 = f32[192,6,8,128]{3,2,1,0:T(8,128)} custom-call(f32[1,6,8,18432]{3,2,1,0:T(8,128)} %bitcast.17, f32[1,6,8,18432]{3,2,1,0:T(8,128)} %bitcast.19, bf16[2,512,256]{2,1,0:T(8,128)(2,1)} %constant.21.clone.depth, bf16[192,576]{1,0:T(8,128)(2,1)} %constant.16.clone.table, f32[8,128]{1,0:T(8,128)} %slice_bitcast_fusion.token), custom_call_target="tpu_custom_call" | custom-call | flops 8000000000 | bytes 12000000 | tf_op jit(solution)/shard_map/forward_wide/pallas_call | solution.py:195
  33.4 35.5 %all-to-all-done.2.refs_0_ = f32[16,3,2,1,48,128]{5,4,3,2,1,0:T(8,128)S(1)} async-done(((f32[16,3,2,1,48,128]{5,4,3,2,1,0:T(8,128)}), f32[16,3,2,1,48,128]{5,4,3,2,1,0:T(8,128)S(1)}, u32[]{:S(2)}, u32[]{:S(2)}) %all-to-all-start.2) | async-done | bytes 2359328 | tf_op jit(solution)/shard_map/all_to_all | solution.py:413
  68.9 6.7 %all-to-all-start = ((f32[16,3,2,2,48,128]{5,4,3,2,1,0:T(8,128)}), f32[16,3,2,2,48,128]{5,4,3,2,1,0:T(8,128)}, u32[]{:S(2)}, u32[]{:S(2)}) async-start(f32[16,3,2,2,48,128]{5,4,3,2,1,0:T(8,128)} %bitcast.10), calls=%async_computation | async-start | bytes 9437184 | tf_op jit(solution)/shard_map/all_to_all | solution.py:413
  75.7 0.1 copy.18
  75.8 0.1 copy.19.pairs
  75.9 10.1 %middle_narrow.1 = f32[16,3,24,128]{3,2,1,0:T(8,128)} custom-call(s32[4,32]{1,0:T(4,128)S(1)} %copy.19.pairs, s32[4,16]{1,0:T(4,128)S(1)} %copy-done, f32[16,3,2,1,48,128]{5,4,3,2,1,0:T(8,128)S(1)} %all-to-all-done.2.refs_0_, bf16[192,576]{1,0:T(8,128)(2,1)} %constant.18.clone.refs_1_, bf16[192,576]{1,0:T(8,128)(2,1)} %constant.19.clone.refs_2_), custom_call_target="tpu_custom_call" | custom-call | flops 4000000000 | bytes 10000000 | tf_op jit(solution)/shard_map/middle_narrow/pallas_call | solution.py:292
  85.9 90.4 %all-to-all-done.refs_0_ = f32[16,3,2,2,48,128]{5,4,3,2,1,0:T(8,128)} async-done(((f32[16,3,2,2,48,128]{5,4,3,2,1,0:T(8,128)}), f32[16,3,2,2,48,128]{5,4,3,2,1,0:T(8,128)}, u32[]{:S(2)}, u32[]{:S(2)}) %all-to-all-start) | async-done | bytes 4718624 | tf_op jit(solution)/shard_map/all_to_all | solution.py:413
  176.3 8.7 %all-to-all-start.3 = ((f32[16,3,24,128]{3,2,1,0:T(8,128)}), f32[16,3,24,128]{3,2,1,0:T(8,128)S(1)}, u32[]{:S(2)}, u32[]{:S(2)}) async-start(f32[16,3,24,128]{3,2,1,0:T(8,128)} %middle_narrow.1), calls=%async_computation.3 | async-start | bytes 1179648 | tf_op jit(solution)/shard_map/all_to_all | solution.py:413
  185.1 12.4 %middle_wide.1 = f32[16,3,48,128]{3,2,1,0:T(8,128)} custom-call(s32[4,32]{1,0:T(4,128)S(1)} %copy.19.pairs, s32[4,16]{1,0:T(4,128)S(1)} %copy-done, f32[16,3,2,2,48,128]{5,4,3,2,1,0:T(8,128)} %all-to-all-done.refs_0_, bf16[192,576]{1,0:T(8,128)(2,1)} %constant.18.clone.refs_1_, bf16[192,576]{1,0:T(8,128)(2,1)} %constant.19.clone.refs_2_), custom_call_target="tpu_custom_call" | custom-call | flops 4000000000 | bytes 10000000 | tf_op jit(solution)/shard_map/middle_wide/pallas_call | solution.py:292
  197.5 2.5 %all-to-all-done.3.refs_0_ = f32[16,3,24,128]{3,2,1,0:T(8,128)S(1)} async-done(((f32[16,3,24,128]{3,2,1,0:T(8,128)}), f32[16,3,24,128]{3,2,1,0:T(8,128)S(1)}, u32[]{:S(2)}, u32[]{:S(2)}) %all-to-all-start.3) | async-done | bytes 589856 | tf_op jit(solution)/shard_map/all_to_all | solution.py:413
  200.0 4.7 %all-to-all-start.1 = ((f32[16,3,48,128]{3,2,1,0:T(8,128)}), f32[16,3,48,128]{3,2,1,0:T(8,128)S(1)}, u32[]{:S(2)}, u32[]{:S(2)}) async-start(f32[16,3,48,128]{3,2,1,0:T(8,128)} %middle_wide.1), calls=%async_computation.1 | async-start | bytes 2359296 | tf_op jit(solution)/shard_map/all_to_all | solution.py:413
  204.6 5.2 %inverse_narrow.1.refs_1_ = f32[6,3,192,128]{3,2,1,0:T(8,128)S(1)} custom-call(f32[16,3,24,128]{3,2,1,0:T(8,128)S(1)} %all-to-all-done.3.refs_0_, bf16[384,288]{1,0:T(8,128)(2,1)} %constant.17.clone.refs_1_.refs_2_, bf16[2,2,512,256]{3,2,1,0:T(8,128)(2,1)} %constant.22.clone.refs_2_), custom_call_target="tpu_custom_call" | custom-call | flops 4000000000 | bytes 6000000 | tf_op jit(solution)/shard_map/inverse_narrow/pallas_call | solution.py:395
  209.9 1.2 copy-done.3
  211.1 20.7 %all-to-all-done.1.refs_0_ = f32[16,3,48,128]{3,2,1,0:T(8,128)S(1)} async-done(((f32[16,3,48,128]{3,2,1,0:T(8,128)}), f32[16,3,48,128]{3,2,1,0:T(8,128)S(1)}, u32[]{:S(2)}, u32[]{:S(2)}) %all-to-all-start.1) | async-done | bytes 1179680 | tf_op jit(solution)/shard_map/all_to_all | solution.py:413
  231.8 1.5 copy-done.4
  233.3 1.9 inverse_wide.3.own
  235.2 2.6 %collective-permute-start.1 = (f32[1,3,4,18432]{3,2,1,0:T(4,128)S(1)}, f32[1,3,4,18432]{3,2,1,0:T(4,128)S(1)}, u32[]{:S(2)}, u32[]{:S(2)}) collective-permute-start(f32[1,3,4,18432]{3,2,1,0:T(4,128)S(1)} %inverse_wide.3.own), channel_id=1, source_target_pairs={{16,0},{0,16},{17,1},{1,17},{18,2},{2,18},{19,3},{3,19},{20,4},{4,... | collective-permute-start | bytes 2654216 | tf_op jit(solution)/shard_map/ppermute | solution.py:506
  237.8 1.9 inverse_wide.2.own
  239.9 1.9 differences.2
  241.8 0.5 collective-permute-done.refs_0_
  242.2 1.9 differences.3
  (12 shorter events, 0.1 us)
Async XLA Ops:
  11.0 57.9 %all-to-all-start.2 = ((f32[16,3,2,1,48,128]{5,4,3,2,1,0:T(8,128)}), f32[16,3,2,1,48,128]{5,4,3,2,1,0:T(8,128)S(1)}, u32[]{:S(2)}, u32[]{:S(2)}) async-start(f32[16,3,2,1,48,128]{5,4,3,2,1,0:T(8,128)} %bitcast.11), calls=%async_computation.2 | async-start | bytes 4718592 | tf_op jit(solution)/shard_map/all_to_all | solution.py:413
  68.9 6.8 %copy-start.5 = (s32[4,16,2]{1,2,0:T(2,128)S(1)}, s32[4,16,2]{1,2,0:T(2,128)}, u32[]{:S(2)}) copy-start(s32[4,16,2]{1,2,0:T(2,128)} %param.14) | copy-start | bytes 1540
  68.9 6.9 %copy-start = (s32[4,16]{1,0:T(4,128)S(1)}, s32[4,16]{1,0:T(4,128)}, u32[]{:S(2)}) copy-start(s32[4,16]{1,0:T(4,128)} %signs.3) | copy-start | bytes 772
  68.9 107.4 %all-to-all-start = ((f32[16,3,2,2,48,128]{5,4,3,2,1,0:T(8,128)}), f32[16,3,2,2,48,128]{5,4,3,2,1,0:T(8,128)}, u32[]{:S(2)}, u32[]{:S(2)}) async-start(f32[16,3,2,2,48,128]{5,4,3,2,1,0:T(8,128)} %bitcast.10), calls=%async_computation | async-start | bytes 9437184 | tf_op jit(solution)/shard_map/all_to_all | solution.py:413
  176.3 23.6 %all-to-all-start.3 = ((f32[16,3,24,128]{3,2,1,0:T(8,128)}), f32[16,3,24,128]{3,2,1,0:T(8,128)S(1)}, u32[]{:S(2)}, u32[]{:S(2)}) async-start(f32[16,3,24,128]{3,2,1,0:T(8,128)} %middle_narrow.1), calls=%async_computation.3 | async-start | bytes 1179648 | tf_op jit(solution)/shard_map/all_to_all | solution.py:413
  200.0 31.8 %all-to-all-start.1 = ((f32[16,3,48,128]{3,2,1,0:T(8,128)}), f32[16,3,48,128]{3,2,1,0:T(8,128)S(1)}, u32[]{:S(2)}, u32[]{:S(2)}) async-start(f32[16,3,48,128]{3,2,1,0:T(8,128)} %middle_wide.1), calls=%async_computation.1 | async-start | bytes 2359296 | tf_op jit(solution)/shard_map/all_to_all | solution.py:413
  204.6 27.2 %copy-start.1 = (bf16[1,2,512,256]{3,2,1,0:T(8,128)(2,1)S(1)}, bf16[1,2,512,256]{3,2,1,0:T(8,128)(2,1)}, u32[]{:S(2)}) copy-start(bf16[1,2,512,256]{3,2,1,0:T(8,128)(2,1)} %constant.23.clone.refs_3_) | copy-start | bytes 1572868
  204.6 27.2 %copy-start.2 = (bf16[384,288]{1,0:T(8,128)(2,1)S(1)}, bf16[384,288]{1,0:T(8,128)(2,1)}, u32[]{:S(2)}) copy-start(bf16[384,288]{1,0:T(8,128)(2,1)} %constant.17.clone.refs_1_.refs_2_) | copy-start | bytes 663556
  209.9 1.2 copy-start.3
  231.8 1.5 copy-start.4
  235.2 4.7 %collective-permute-start.1 = (f32[1,3,4,18432]{3,2,1,0:T(4,128)S(1)}, f32[1,3,4,18432]{3,2,1,0:T(4,128)S(1)}, u32[]{:S(2)}, u32[]{:S(2)}) collective-permute-start(f32[1,3,4,18432]{3,2,1,0:T(4,128)S(1)} %inverse_wide.3.own), channel_id=1, source_target_pairs={{16,0},{0,16},{17,1},{1,17},{18,2},{2,18},{19,3},{3,19},{20,4},{4,... | collective-permute-start | bytes 2654216 | tf_op jit(solution)/shard_map/ppermute | solution.py:506
  239.7 2.5 %collective-permute-start = (f32[1,3,4,18432]{3,2,1,0:T(4,128)S(1)}, f32[1,3,4,18432]{3,2,1,0:T(4,128)S(1)}, u32[]{:S(2)}, u32[]{:S(2)}) collective-permute-start(f32[1,3,4,18432]{3,2,1,0:T(4,128)S(1)} %inverse_wide.2.own), channel_id=1, source_target_pairs={{16,0},{0,16},{17,1},{1,17},{18,2},{2,18},{19,3},{3,19},{20,4},{4,... | collective-permute-start | bytes 2654216 | tf_op jit(solution)/shard_map/ppermute | solution.py:506
